TPU v7x, 128 devices: a whole 4x4x4 slice. The times are simulated.
128 devices in a mesh: dom: 16 (over y, z), inner: 8 (over x, core).
Axes of the slice: x: 4, y: 4, z: 4, core: 2. Of those that a mesh axis runs over, the one named last changes fastest.
Arguments:
- start_field: float32 [128, 256, 8, 128], P('dom', 'inner'), may hold values from -1.5 to 1.5, as said below
- source_field: float32 [128, 256, 8, 128], P('dom', 'inner'), may hold values from -5 to 5, as said below
- coefficients: float32 [3, 16, 32, 128], P(None, 'dom', 'inner'), may hold values from 0.3 to 3
- outflow: int32 [128, 256], P('dom', 'inner'), may hold values from 0 to 1, as said below
Outputs:
- solution_field: float32 [128, 256, 8, 128], P('dom', 'inner')
- residual: float32 [128, 256, 8, 128], P('dom', 'inner')
Inputs may be any that keep to these rules, and one draw needn't show every extreme that they name: `start_field`: Continuous: all copies of a shared node hold the same value. `source_field`: Continuous: all copies of a shared node hold the same value. A node column is 1 where any element column holding it is an outflow column; all copies of a shared node column agree.
All inputs are finite; a program needn't handle non-finite values.
Results may differ from a plain program's by a relative error of at most 0.0003.
Values sent between devices are 32-bit elements; how exact they have to be, the bound alone decides.
No kernel may reach another device: no remote copies, remote signals or barrier semaphores. Data moves between devices by JAX's collectives and lax.ppermute only.
A program may use at most 64 MiB of HBM per device.

v0:
```python
import functools
import math

import jax
import jax.numpy as jnp
import ml_dtypes
import numpy as np
from jax import lax
from jax.experimental import pallas as pl
from jax.experimental.pallas import tpu as pltpu
from jax.sharding import PartitionSpec as P

INTERIOR_POINTS = (
    -0.8717401485096066,
    -0.5917001814331423,
    -0.2092992179024789,
    0.2092992179024789,
    0.5917001814331423,
    0.8717401485096066,
)
F32 = jnp.float32
BF16 = jnp.bfloat16
VMEM_BYTES = 48 * 1024 * 1024


def legendre_seven(points):
    previous = points * 0.0 + 1.0
    current = points.copy()
    for degree in range(1, 7):
        following = ((2 * degree + 1) * points * current - degree * previous) / (degree + 1)
        previous = current
        current = following
    return current


def jacobi_eigen(matrix):
    extent = matrix.shape[0]
    current = matrix.copy()
    vectors = np.eye(extent)
    for sweep_number in range(12):
        for first_index in range(extent):
            for second_index in range(first_index + 1, extent):
                angle = 0.5 * math.atan2(
                    2.0 * float(current[first_index, second_index]),
                    float(current[second_index, second_index] - current[first_index, first_index]),
                )
                cosine = math.cos(angle)
                sine = math.sin(angle)
                rotation = np.eye(extent)
                rotation[first_index, first_index] = cosine
                rotation[second_index, second_index] = cosine
                rotation[first_index, second_index] = sine
                rotation[second_index, first_index] = -sine
                current = rotation.T @ current @ rotation
                vectors = vectors @ rotation
    return (np.array([float(current[index, index]) for index in range(extent)]), vectors)


def quadrature_tables():
    grid_points = np.array((-1.0,) + INTERIOR_POINTS + (1.0,))
    end_values = legendre_seven(grid_points)
    weights = 2.0 / (56.0 * end_values**2)
    derivative = np.zeros((8, 8))
    for row_index in range(8):
        for column_index in range(8):
            if row_index != column_index:
                derivative[row_index, column_index] = end_values[row_index] / (
                    end_values[column_index] * (grid_points[row_index] - grid_points[column_index])
                )
    derivative[0, 0] = -14.0
    derivative[7, 7] = 14.0
    stiffness = derivative.T @ (weights[:, None] * derivative)
    three_stiffness = np.zeros((22, 22))
    three_mass = np.zeros(22)
    for element_index in range(3):
        element_offset = 7 * element_index
        three_stiffness[
            element_offset : element_offset + 8, element_offset : element_offset + 8
        ] += stiffness
        three_mass[element_offset : element_offset + 8] += weights
    inverse_root = 1.0 / np.sqrt(three_mass[6:16])
    symmetric = inverse_root[:, None] * three_stiffness[6:16, 6:16] * inverse_root[None, :]
    eigen_values, eigen_vectors = jacobi_eigen(symmetric)
    eigen_basis = inverse_root[:, None] * eigen_vectors
    return tuple(
        table.astype(np.float32).astype(np.float64)
        for table in (stiffness, weights, eigen_basis, eigen_values)
    )


STIFF, WEIGHT, BASIS, EIGEN = quadrature_tables()
PARITY = [1.0 if BASIS[0, p] * BASIS[9, p] > 0 else -1.0 for p in range(10)]
HALF_BASIS = np.array(
    [[0.5 * (BASIS[a, p] + PARITY[p] * BASIS[9 - a, p]) for p in range(10)] for a in range(5)]
)
EVEN = [p for p in range(10) if PARITY[p] > 0]
ODD = [p for p in range(10) if PARITY[p] < 0]


def two_parts(matrix):
    high = matrix.astype(ml_dtypes.bfloat16)
    low = (matrix - high.astype(np.float64)).astype(ml_dtypes.bfloat16)
    return high, low


def operator_tables():
    along_second = np.kron(STIFF, np.diag(WEIGHT))
    along_third = np.kron(np.diag(WEIGHT), STIFF)
    sets = []
    for places in (range(8), (0, 1, 6, 7)):
        rows = [8 * j + k for j in places for k in range(8)]
        high, low = two_parts(np.concatenate([along_second[rows], along_third[rows]]))
        sets.append(np.concatenate([high, high, low], axis=1))
    return sets


def transform_tables():
    own = BASIS[1:9]
    beside = np.zeros((8, 10))
    beside[0] = BASIS[8]
    beside[1] = BASIS[9]
    beside[6] = BASIS[0]
    beside[7] = BASIS[1]
    back = np.zeros((160, 112))
    back[:80, :100] = np.kron(BASIS, own)
    back[80:, :100] = np.kron(BASIS, beside)
    back_high, back_low = two_parts(back)
    forward_high, forward_low = two_parts(back.T)
    return (
        (forward_high, forward_low),
        (np.concatenate([back_high, back_high], axis=1), back_low),
    )


def value_tables():
    second_values = np.ones((112, 128), np.float32)
    third_values = np.ones((112, 128), np.float32)
    second_values[:100] = np.repeat(EIGEN, 10)[:, None]
    third_values[:100] = np.tile(EIGEN, 10)[:, None]
    return second_values, third_values


OPERATOR_OWN, OPERATOR_SIDE = operator_tables()
PLANE_WEIGHTS = np.broadcast_to(
    (WEIGHT[:, None] * WEIGHT[None, :])[:, :, None], (8, 8, 128)
).astype(np.float32)
FORWARD, BACKWARD = transform_tables()
VALUES = value_tables()
LANES = (slice(0, 128), slice(128, 256))


def lane_ids():
    return lax.broadcasted_iota(jnp.int32, (8, 128), 1)


def row_ids():
    return lax.broadcasted_iota(jnp.int32, (8, 128), 0)


def split(values):
    high = values.astype(BF16)
    return high, (values - high.astype(F32)).astype(BF16)


def dot(left, right):
    return jnp.dot(left, right, preferred_element_type=F32)


def ends(place, axis):
    return (
        jnp.where(place[2 * axis] > 0, 1.0, 0.0),
        jnp.where(place[2 * axis] < place[2 * axis + 1] - 1, 1.0, 0.0),
    )


def top_flags():
    return ((lane_ids() == 127) & (row_ids() == 7)).astype(F32)


def own_keep(outflow, top, i, column):
    return 1.0 - outflow[i, column].astype(F32) * top


def ghost_keep(message, i):
    return jnp.where(row_ids() == 7, message[i, 8], 1.0)


def spread_row(row):
    return jnp.broadcast_to(row, (8, 128))


def column_of(n):
    return 31 if n == 28 else 8 * (n // 7) + n % 7


def whole(memory=None):
    return pl.BlockSpec(memory_space=memory or pltpu.VMEM)


def layers(count, rows):
    return jax.ShapeDtypeStruct((count, rows, 8, 128), F32)


def call(body, outs, scalars, scratch, name, args, flops):
    bytes_accessed = sum(4 * math.prod(a.shape) for a in (*args, *outs))
    return pl.pallas_call(
        body,
        out_shape=tuple(outs),
        in_specs=[whole(pltpu.SMEM if n < scalars else None) for n in range(len(args))],
        out_specs=tuple(whole() for _ in outs),
        scratch_shapes=scratch,
        compiler_params=pltpu.CompilerParams(vmem_limit_bytes=VMEM_BYTES),
        cost_estimate=pl.CostEstimate(
            flops=flops, bytes_accessed=bytes_accessed, transcendentals=0
        ),
        name=name,
    )(*args)


def pack_body(start_low, start_high, source_low, source_high, coefficients, outflow, low, high):
    top = top_flags()
    rows = row_ids()
    for target, start, source, first, node, element in (
        (low, start_low, source_low, 1, 1, 0),
        (high, start_high, source_high, 0, 6, 3),
    ):
        gains = [spread_row(coefficients[c, 0, element : element + 1, :]) for c in range(3)]
        info = jnp.where(rows == 0, gains[0], jnp.where(rows == 1, gains[1], gains[2]))

        def step(i, carry, target=target, start=start, source=source, first=first, node=node,
                 element=element, info=info):
            target[i, 0:7] = start[i, first : first + 7]
            target[i, 7] = source[i, 0]
            keep = own_keep(outflow, top, i, 8 * element + node)
            target[i, 8] = jnp.where(rows == 7, keep, info)
            return carry

        lax.fori_loop(0, 8, step, 0)


def pack_first(start, source, coefficients, outflow):
    def block(rows, at):
        return pl.BlockSpec((8, rows, 8, 128), lambda g: (0, at, 0, 0))

    return pl.pallas_call(
        pack_body,
        grid=(1,),
        out_shape=(layers(8, 9), layers(8, 9)),
        in_specs=[
            block(8, 0),
            block(8, 3),
            block(1, 1),
            block(1, 30),
            pl.BlockSpec((3, 1, 4, 128), lambda g: (0, 0, 0, 0)),
            pl.BlockSpec(memory_space=pltpu.SMEM),
        ],
        out_specs=(block(9, 0), block(9, 0)),
        name="pack_first",
    )(start, start, source, source, coefficients, outflow)


def first_direction(values):
    sums = [values[a] + values[7 - a] for a in range(4)]
    gaps = [values[a] - values[7 - a] for a in range(4)]
    outs = [None] * 8
    for i in range(4):
        even = odd = None
        for a in range(4):
            even_term = sums[a] * float(0.5 * (STIFF[i, a] + STIFF[i, 7 - a]))
            odd_term = gaps[a] * float(0.5 * (STIFF[i, a] - STIFF[i, 7 - a]))
            even = even_term if even is None else even + even_term
            odd = odd_term if odd is None else odd + odd_term
        outs[i] = even + odd
        outs[7 - i] = even - odd
    return outs


def products(pair, table, count, planes):
    def step(i, carry):
        values = jnp.concatenate(
            [field[i, at : at + 8].reshape(64, 128) for field, at in pair], axis=1
        )
        high, low = split(values)
        planes[i, 0:count] = dot(table[...], jnp.concatenate([high, low, high], axis=0))
        return carry

    lax.fori_loop(0, 8, step, 0, unroll=2)


def combine(field, at, gain, weights, planes, lane, second_at, third_at, image, target, add):
    terms = first_direction([field[a, at] for a in range(8)])
    plane = gain[0] * weights
    for i in range(8):
        second = planes[i, pl.ds(second_at, 8), lane]
        third = planes[i, pl.ds(third_at, 8), lane]
        value = plane * terms[i] + float(WEIGHT[i]) * (gain[1] * second + gain[2] * third)
        if add:
            value = value + image[i, target]
        image[i, target] = value


def own_elements(pair, gains, table, plane_weights, planes, image, offset):
    products([(field, at) for _, field, at, _, _ in pair], table, 128, planes)
    for (e, field, at, add_first, add_last), lane in zip(pair, LANES):
        gain = gains(e)
        base = 7 * e + offset

        def row(j, add, field=field, at=at, lane=lane, gain=gain, base=base):
            start = 8 * j if isinstance(j, int) else pl.multiple_of(8 * j, 8)
            combine(
                field, at + j, gain, plane_weights[j], planes, lane, start, start + 64,
                image, base + j, add,
            )

        row(0, add_first)
        lax.fori_loop(1, 7, lambda j, c, row=row: (row(j, False), c)[1], 0)
        row(7, add_last)


def own_gains(coefficients):
    return lambda e: [spread_row(coefficients[c, 0, e : e + 1, :]) for c in range(3)]


def side_gains(flag, message):
    return [spread_row(message[0, 8, c : c + 1, :] * flag) for c in range(3)]


def side_elements(field, low_at, high_at, low_gain, high_gain, table, plane_weights, planes, image):
    products([(field, low_at), (field, high_at)], table, 64, planes)
    for q in range(2):
        combine(
            field, low_at + 6 + q, low_gain, plane_weights[6 + q], planes, LANES[0],
            16 + 8 * q, 48 + 8 * q, image, q, q == 1,
        )
        combine(
            field, high_at + q, high_gain, plane_weights[q], planes, LANES[1],
            8 * q, 32 + 8 * q, image, 29 + q, q == 0,
        )


def finish_residual(image_row, source_part, outflow, from_low, from_high, low, inner, high):
    top = top_flags()

    def place_row(i, y, value):
        if i < 2:
            low[i, y] = value
        if 0 < i < 7:
            inner[i - 1, y] = value
        if i > 5:
            high[i - 6, y] = value

    for i in range(8):

        def own_row(y, column, i=i):
            value = source_part[i, y] - image_row(i, y)
            place_row(i, y, own_keep(outflow, top, i, column) * value)

        place_row(i, 0, ghost_keep(from_low, i) * (source_part[i, 0] - image_row(i, 0)))
        place_row(i, 30, ghost_keep(from_high, i) * (source_part[i, 30] - image_row(i, 30)))
        own_row(29, 31)

        def step(e, carry, own_row=own_row):
            for j in range(7):
                own_row(1 + 7 * e + j, 8 * e + j)
            return carry

        lax.fori_loop(0, 4, step, 0)


def plane_scratch():
    return pltpu.VMEM((8, 128, 256), F32)


def own_image_body(coefficients, start, own_table, plane_weights, image, planes):
    gains = own_gains(coefficients)
    for pair in ((0, 1), (2, 3)):
        own_elements(
            [(e, start, 8 * e, e > 0, False) for e in pair],
            gains, own_table, plane_weights, planes, image, 1,
        )


def reciprocal_body(coefficients, second_values, third_values, result):
    gain = [[coefficients[c, 0, e : e + 1, :] for e in range(4)] for c in range(3)]

    def step(block, carry):
        at = pl.multiple_of(16 * block, 16)
        second = second_values[pl.ds(at, 16), :]
        third = third_values[pl.ds(at, 16), :]
        for e in range(4):
            rest = gain[1][e] * second + gain[2][e] * third
            for p in range(10):
                result[p, e // 2, pl.ds(at, 16), LANES[e % 2]] = 1.0 / (
                    rest + gain[0][e] * float(EIGEN[p])
                )
        return carry

    lax.fori_loop(0, 7, step, 0)


def first_join_body(
    place, outflow, start, source, coefficients, from_low, from_high, side_table, plane_weights,
    own_image, source_part, low, inner, high, planes, field, image,
):
    lane = lane_ids()
    row = row_ids()
    inner_face = ((row == 0) & (lane > 0)) | ((row == 7) & (lane < 127))
    third_share = jnp.where(inner_face, 0.5, 1.0)
    below, above = ends(place, 0)
    low_flag, high_flag = ends(place, 1)
    for i in range(8):
        field[i, 0:7] = from_low[i, 0:7]
        field[i, 7] = start[i, 0]
        field[i, 8] = start[i, 31]
        field[i, 9:16] = from_high[i, 0:7]
        image[i, 1] = own_image[i, 1]
        image[i, 29] = own_image[i, 29]
        share = third_share
        if i == 0:
            share = third_share * (1.0 - 0.5 * below)
        if i == 7:
            share = third_share * (1.0 - 0.5 * above)
        source_part[i, 0] = from_low[i, 7] * (share * low_flag)
        source_part[i, 30] = from_high[i, 7] * (share * high_flag)
        source_part[i, 29] = source[i, 31] * share

        def step(e, carry, i=i, share=share):
            for j in range(7):
                source_part[i, 1 + 7 * e + j] = source[i, 8 * e + j] * share
            return carry

        lax.fori_loop(0, 4, step, 0)
    side_elements(
        field, 0, 8, side_gains(low_flag, from_low), side_gains(high_flag, from_high),
        side_table, plane_weights, planes, image,
    )

    for i in range(8):
        image[i, 2:29] = own_image[i, 2:29]
    finish_residual(
        lambda i, y: image[i, y], source_part, outflow, from_low, from_high, low, inner, high
    )


def forward_layers(source, count, forward_high, forward_low, spectral):
    lane = lane_ids()
    row = row_ids()
    lower_half = row < 4
    valid = (lower_half & (lane < 127)) | ((row > 3) & (lane > 0))

    def columns(a, e):
        own = [source[a, 7 * e + b] for b in range(10)]
        beside = [
            jnp.where(
                valid,
                jnp.where(lower_half, pltpu.roll(v, 127, 1), pltpu.roll(v, 1, 1)),
                0.0,
            )
            for v in own
        ]
        return jnp.concatenate(own + beside, axis=0)

    def step(half, carry):
        for part in range(2):
            a = 2 * half + part
            for pair in range(2):
                values = jnp.concatenate([columns(a, 2 * pair), columns(a, 2 * pair + 1)], axis=1)
                top, bottom = split(values)
                spectral[a, pair] = (
                    dot(forward_high[...], top)
                    + dot(forward_high[...], bottom)
                    + dot(forward_low[...], top)
                )
        return carry

    lax.fori_loop(0, count // 2, step, 0)


def backward_layers(halves, count, backward, backward_low, target):
    lane = lane_ids()
    row = row_ids()
    lower_half = row < 4
    valid = (lower_half & (lane > 0)) | ((row > 3) & (lane < 127))

    def step(half, carry):
        for part in range(2):
            a = 2 * half + part
            tail = None
            for pair in range(2):
                result = dot(backward[...], halves[a, pair]) + dot(
                    backward_low[...], halves[a, pair, 0:112]
                )
                for side in range(2):
                    e = 2 * pair + side
                    rows = []
                    for b in range(10):
                        main = result[8 * b : 8 * b + 8, LANES[side]]
                        beside = result[80 + 8 * b : 88 + 8 * b, LANES[side]]
                        moved = jnp.where(
                            lower_half, pltpu.roll(beside, 1, 1), pltpu.roll(beside, 127, 1)
                        )
                        rows.append(main + jnp.where(valid, moved, 0.0))
                    if tail is not None:
                        for b in range(3):
                            rows[b] = rows[b] + tail[b]
                    for b in range(7):
                        target[a, 7 * e + b] = rows[b]
                    tail = rows[7:]
            for b in range(3):
                target[a, 28 + b] = tail[b]
        return carry

    lax.fori_loop(0, count // 2, step, 0)


def inner_forward_body(inner, forward_high, forward_low, spectral):
    forward_layers(inner, 6, forward_high, forward_low, spectral)


def edge_solve_body(
    place, reciprocals, forward_high, forward_low, backward, backward_low, spectral,
    low, high, from_low, from_high, out_low, out_high, inner_halves, edges, edge_spectral, halves,
):
    below, above = ends(place, 0)

    def gather(y, carry):
        edges[0, y] = below * from_low[0, y]
        edges[1, y] = low[0, y] + below * from_low[1, y]
        edges[2, y] = high[1, y] + above * from_high[0, y]
        edges[3, y] = above * from_high[1, y]
        return carry

    lax.fori_loop(0, 31, gather, 0)
    forward_layers(edges, 4, forward_high, forward_low, edge_spectral)

    def layer(a):
        if a < 2:
            return edge_spectral, halves, a
        if a < 8:
            return spectral, inner_halves, a - 2
        return edge_spectral, halves, a - 6

    def middle_step(block, carry):
        at = pl.multiple_of(16 * block, 16)
        for e in range(4):
            spot = (e // 2, pl.ds(at, 16), LANES[e % 2])
            values = [layer(a)[0][(layer(a)[2],) + spot] for a in range(10)]
            sums = [values[a] + values[9 - a] for a in range(5)]
            gaps = [values[a] - values[9 - a] for a in range(5)]
            modes = []
            for p in range(10):
                sides = sums if PARITY[p] > 0 else gaps
                total = sides[0] * float(HALF_BASIS[0, p])
                for a in range(1, 5):
                    total = total + sides[a] * float(HALF_BASIS[a, p])
                modes.append(total * reciprocals[(p,) + spot])
            for a in range(5):
                even = odd = None
                for p in EVEN:
                    term = modes[p] * float(HALF_BASIS[a, p])
                    even = term if even is None else even + term
                for p in ODD:
                    term = modes[p] * float(HALF_BASIS[a, p])
                    odd = term if odd is None else odd + term
                for spot_layer, value in ((a, even + odd), (9 - a, even - odd)):
                    top, bottom = split(value)
                    _, target, index = layer(spot_layer)
                    target[index, e // 2, pl.ds(at, 16), LANES[e % 2]] = top
                    target[index, e // 2, pl.ds(112 + at, 16), LANES[e % 2]] = bottom
        return carry

    lax.fori_loop(0, 7, middle_step, 0)

    def back(first, target):
        backward_layers(halves.at[first : first + 2], 2, backward, backward_low, target)

    back(0, out_low)
    back(2, out_high)


def inner_backward_body(inner_halves, backward, backward_low, out_inner):
    backward_layers(inner_halves, 6, backward, backward_low, out_inner)


def residual_body(place, low, inner, high, from_low, from_high, residual):
    row = row_ids()
    lane = lane_ids()
    below, above = ends(place, 0)
    for i in range(8):

        def value_at(y, i=i):
            if i == 0:
                value = low[0, y] + below * from_low[1, y]
            elif i == 7:
                value = high[1, y] + above * from_high[0, y]
            else:
                value = inner[i - 1, y]
            before = jnp.where((row == 0) & (lane > 0), pltpu.roll(pltpu.roll(value, 1, 0), 1, 1), 0.0)
            after = jnp.where(
                (row == 7) & (lane < 127), pltpu.roll(pltpu.roll(value, 7, 0), 127, 1), 0.0
            )
            return value + before + after

        def step(e, carry, i=i, value_at=value_at):
            for j in range(8):
                residual[i, 8 * e + j] = value_at(1 + 7 * e + j)
            return carry

        lax.fori_loop(0, 4, step, 0)


def fold_row(ends_flags, i, y, low, inner, high, from_low, from_high):
    below, above = ends_flags
    if i == 0:
        return low[1, y] + below * from_low[0, y]
    if i == 1:
        return inner[0, y] + below * from_low[1, y]
    if i < 6:
        return inner[i - 1, y]
    if i == 6:
        return inner[5, y] + above * from_high[0, y]
    return high[0, y] + above * from_high[1, y]


def fold_body(count, place, outflow, low, inner, high, from_low, from_high, to_low, to_high):
    top = top_flags()
    flags = ends(place, 0)
    for i in range(8):
        for y in (*range(count), *range(31 - count, 31)):
            value = fold_row(flags, i, y, low, inner, high, from_low, from_high)
            if 3 <= y < 28:
                value = own_keep(outflow, top, i, column_of(y - 1)) * value
            if y < count:
                to_low[i, y] = value
            else:
                to_high[i, y - 31 + count] = value


def update_body(
    place, outflow, start, coefficients, own_table, plane_weights, low, inner, high,
    from_low, from_high, field, image, planes,
):
    top = top_flags()
    flags = ends(place, 0)
    parts = (low, inner, high, from_low, from_high)
    for i in range(8):
        field[i, 0] = fold_row(flags, i, 0, *parts)
        field[i, 30] = fold_row(flags, i, 30, *parts)

        def row(y, column, i=i):
            value = own_keep(outflow, top, i, column) * fold_row(flags, i, y, *parts)
            field[i, y] = start[i, column] + value

        row(29, 31)

        def step(e, carry, row=row):
            for j in range(7):
                row(1 + 7 * e + j, 8 * e + j)
            return carry

        lax.fori_loop(0, 4, step, 0)
    own_elements(
        [(1, field, 8, False, False), (2, field, 15, True, False)],
        own_gains(coefficients), own_table, plane_weights, planes, image, -7,
    )


def second_join_body(
    place, outflow, coefficients, from_low, from_high, own_table, side_table, plane_weights,
    field, middle_image, source_part, low_news, high_news,
    changed, low, inner, high, planes, rows, image,
):
    top = top_flags()
    low_flag, high_flag = ends(place, 1)
    for i in range(8):
        rows[i, 0:6] = from_low[i, 0:6] + low_news[i, 0:6]
        rows[i, 6] = from_low[i, 6] + ghost_keep(from_low, i) * (
            field[i, 0] + low_flag * low_news[i, 6]
        )
        for n in range(2):
            news = own_keep(outflow, top, i, n) * (low_flag * low_news[i, 7 + n])
            value = field[i, 1 + n] + news
            rows[i, 7 + n] = value
            changed[i, n] = value
            news = own_keep(outflow, top, i, 30 + n) * (high_flag * high_news[i, n])
            value = field[i, 28 + n] + news
            rows[i, 21 + n] = value
            changed[i, 2 + n] = value
        rows[i, 9:15] = field[i, 3:9]
        rows[i, 15:21] = field[i, 22:28]
        rows[i, 23] = from_high[i, 0] + ghost_keep(from_high, i) * (
            field[i, 30] + high_flag * high_news[i, 2]
        )
        rows[i, 24:30] = from_high[i, 1:7] + high_news[i, 3:9]
        image[i, 8] = middle_image[i, 0]
        image[i, 22] = middle_image[i, 14]
    own_elements(
        [(0, rows, 7, False, True), (3, rows, 15, True, False)],
        own_gains(coefficients), own_table, plane_weights, planes, image, 1,
    )
    side_elements(
        rows, 0, 22, side_gains(low_flag, from_low), side_gains(high_flag, from_high),
        side_table, plane_weights, planes, image,
    )
    for i in range(8):
        image[i, 9:22] = middle_image[i, 1:14]
    finish_residual(
        lambda i, y: image[i, y], source_part, outflow, from_low, from_high, low, inner, high
    )


def last_update_body(
    place, outflow, field, changed, low, inner, high, from_low, from_high, result
):
    top = top_flags()
    flags = ends(place, 0)
    parts = (low, inner, high, from_low, from_high)
    for i in range(8):
        for n in range(29):
            column = column_of(n)
            keep = own_keep(outflow, top, i, column)
            if n < 2:
                value = changed[i, n]
            elif n > 26:
                value = changed[i, n - 25]
            else:
                value = field[i, n + 1]
            value = value + keep * fold_row(flags, i, n + 1, *parts)
            result[i, column] = value
            if n % 7 == 0 and 0 < n < 28:
                result[i, column - 1] = value


def last_join_body(place, outflow, before, low_news, high_news, result):
    top = top_flags()
    low_flag, high_flag = ends(place, 1)
    side = pl.program_id(0)
    flag = jnp.where(side == 0, low_flag, high_flag)
    for i in range(8):
        for n in range(2):
            news = jnp.where(side == 0, low_news[i, n], high_news[i, n])
            keep = own_keep(outflow, top, i, 30 * side + n)
            result[i, n] = before[i, n] + keep * (flag * news)


def last_join(place, outflow, before, low_news, high_news):
    block = pl.BlockSpec((8, 2, 8, 128), lambda g: (0, 15 * g, 0, 0))
    return pl.pallas_call(
        last_join_body,
        grid=(2,),
        out_shape=layers(8, 32),
        in_specs=[whole(pltpu.SMEM), whole(pltpu.SMEM), block, whole(), whole()],
        out_specs=block,
        input_output_aliases={2: 0},
        name="last_join",
    )(place, outflow, before, low_news, high_news)


def exchange(to_low, to_high, axis):
    count = lax.axis_size(axis)
    upward = [(i, (i + 1) % count) for i in range(count)]
    downward = [((i + 1) % count, i) for i in range(count)]
    return lax.ppermute(to_high, axis, upward), lax.ppermute(to_low, axis, downward)


def modes_shape(count, rows, dtype):
    return jax.ShapeDtypeStruct((count, 2, rows, 256), dtype)


def solve(place, reciprocals, parts):
    forward = [jnp.asarray(t) for t in FORWARD]
    backward = [jnp.asarray(t) for t in BACKWARD]
    low, inner, high = parts
    received = exchange(low, high, "dom")
    (spectral,) = call(
        inner_forward_body, [modes_shape(6, 112, F32)], 0, [], "inner_forward",
        (inner, *forward), 3 * 10**8,
    )
    out_low, out_high, halves = call(
        edge_solve_body,
        [layers(2, 31), layers(2, 31), modes_shape(6, 224, BF16)],
        1,
        [
            pltpu.VMEM((4, 31, 8, 128), F32),
            pltpu.VMEM((4, 2, 112, 256), F32),
            pltpu.VMEM((4, 2, 224, 256), BF16),
        ],
        "edge_solve",
        (place, reciprocals, *forward, *backward, spectral, low, high, *received),
        10**9,
    )
    returned = exchange(out_low, out_high, "dom")
    (out_inner,) = call(
        inner_backward_body, [layers(6, 31)], 0, [], "inner_backward",
        (halves, *backward), 3 * 10**8,
    )
    return received, (out_low, out_inner, out_high, *returned)


def fold(count, place, outflow, parts):
    return call(
        functools.partial(fold_body, count), [layers(8, count), layers(8, count)], 2, [],
        "fold", (place, outflow, *parts), 10**6,
    )


def shards(start, source, coefficients, outflow):
    own_table, side_table, plane_weights = [
        jnp.asarray(t) for t in (OPERATOR_OWN, OPERATOR_SIDE, PLANE_WEIGHTS)
    ]
    place = jnp.stack(
        [
            lax.axis_index("dom"),
            lax.axis_size("dom"),
            lax.axis_index("inner"),
            lax.axis_size("inner"),
        ]
    ).astype(jnp.int32)
    from_low, from_high = exchange(*pack_first(start, source, coefficients, outflow), "inner")
    (own_image,) = call(
        own_image_body, [layers(8, 31)], 0, [plane_scratch()], "own_image",
        (coefficients, start, own_table, plane_weights), 3 * 10**8,
    )
    (reciprocals,) = call(
        reciprocal_body, [modes_shape(10, 112, F32)], 0, [], "reciprocals",
        (coefficients, *[jnp.asarray(t) for t in VALUES]), 10**8,
    )
    source_part, *parts = call(
        first_join_body,
        [layers(8, 31), layers(2, 31), layers(6, 31), layers(2, 31)],
        2,
        [plane_scratch(), pltpu.VMEM((8, 16, 8, 128), F32), pltpu.VMEM((8, 31, 8, 128), F32)],
        "first_join",
        (
            place, outflow, start, source, coefficients, from_low, from_high, side_table,
            plane_weights, own_image,
        ),
        10**8,
    )
    received, solved = solve(place, reciprocals, parts)
    news = exchange(*fold(9, place, outflow, solved), "inner")
    field, middle_image = call(
        update_body, [layers(8, 31), layers(8, 15)], 2, [plane_scratch()], "update",
        (place, outflow, start, coefficients, own_table, plane_weights, *solved), 2 * 10**8,
    )
    changed, *parts = call(
        second_join_body,
        [layers(8, 4), layers(2, 31), layers(6, 31), layers(2, 31)],
        2,
        [plane_scratch(), pltpu.VMEM((8, 30, 8, 128), F32), pltpu.VMEM((8, 31, 8, 128), F32)],
        "second_join",
        (
            place, outflow, coefficients, from_low, from_high, own_table, side_table,
            plane_weights, field, middle_image, source_part, *news,
        ),
        2 * 10**8,
    )
    received, solved = solve(place, reciprocals, parts)
    (residual,) = call(
        residual_body, [layers(8, 32)], 1, [], "residual", (place, *parts, *received), 10**7,
    )
    news = exchange(*fold(2, place, outflow, solved), "inner")
    (iterate,) = call(
        last_update_body, [layers(8, 32)], 2, [], "last_update",
        (place, outflow, field, changed, *solved), 10**7,
    )
    return last_join(place, outflow, iterate, *news), residual


def solution(mesh):
    placed = (
        P("dom", "inner", None, None),
        P("dom", "inner", None, None),
        P(None, "dom", "inner", None),
        P("dom", "inner"),
    )
    return jax.shard_map(
        shards,
        mesh=mesh,
        in_specs=placed,
        out_specs=(P("dom", "inner", None, None), P("dom", "inner", None, None)),
        check_vma=False,
    )
```

profile of v0, /device:TPU:0, one launch (start us, length us, event | category | flops | bytes accessed | tf_op | source)
XLA Modules:
  0.0 94.5 jit_solution(16573637850216232026)
XLA Ops:
  0.7 2.1 %pack_first.1 = (f32[8,9,8,128]{3,2,1,0:T(8,128)}, f32[8,9,8,128]{3,2,1,0:T(8,128)}) custom-call(f32[8,32,8,128]{3,2,1,0:T(8,128)} %start.5, f32[8,32,8,128]{3,2,1,0:T(8,128)} %start.5, f32[8,32,8,128]{3,2,1,0:T(8,128)} %source.1, f32[8,32,8,128]{3,2,1,0:T(8,128)} %source.1, f32[3,1,4,128]{3,2,1,0:T(4,128)} %coefficients.11, s32[8,32]{1,0:T(8,128)} %outflow.15), custom_call_target="tpu_custom_call" | custom-call | tf_op jit(solution)/shard_map/pack_first/pallas_call | solution.py:245
  2.8 2.9 %collective-permute-start.1 = (f32[8,9,8,128]{3,2,1,0:T(8,128)}, f32[8,9,8,128]{3,2,1,0:T(8,128)S(1)}, u32[]{:S(2)}, u32[]{:S(2)}) collective-permute-start(f32[8,9,8,128]{3,2,1,0:T(8,128)} %get-tuple-element.25), channel_id=1, source_target_pairs={{1,0},{2,1},{3,2},{4,3},{5,4},{6,5},{7,6},{0,7},{9,8},{10,9},{11,1... | collective-permute-start | bytes 884744 | tf_op jit(solution)/shard_map/ppermute | solution.py:763
  5.8 2.2 %own_image.1 = f32[8,31,8,128]{3,2,1,0:T(8,128)S(1)} custom-call(f32[3,1,4,128]{3,2,1,0:T(4,128)S(1)} %copy-done.10, f32[8,32,8,128]{3,2,1,0:T(8,128)S(1)} %copy-done, bf16[128,192]{1,0:T(8,128)(2,1)S(1)} %copy-done.7, f32[8,8,128]{2,1,0:T(8,128)S(1)} %copy-done.8), custom_call_target="tpu_custom_call" | custom-call | flops 300000000 | bytes 2201600 | tf_op jit(solution)/shard_map/own_image/pallas_call | solution.py:206
  8.0 2.3 %collective-permute-done.from_low = f32[8,9,8,128]{3,2,1,0:T(8,128)S(1)} collective-permute-done((f32[8,9,8,128]{3,2,1,0:T(8,128)}, f32[8,9,8,128]{3,2,1,0:T(8,128)S(1)}, u32[]{:S(2)}, u32[]{:S(2)}) %collective-permute-start) | collective-permute-done | bytes 294944 | tf_op jit(solution)/shard_map/ppermute | solution.py:763
  10.4 2.4 %first_join.1 = (f32[8,31,8,128]{3,2,1,0:T(8,128)S(1)}, f32[2,31,8,128]{3,2,1,0:T(8,128)S(1)}, f32[6,31,8,128]{3,2,1,0:T(8,128)S(1)}, f32[2,31,8,128]{3,2,1,0:T(8,128)S(1)}) custom-call(s32[4]{0:T(128)S(1)} %pad_add_fusion.place, s32[8,32]{1,0:T(8,128)S(1)} %copy-done.9, f32[8,32,8,128]{3,2,1,0:T(8,128)S(1)} %copy-done, f32[8,32,8,128]{3,2,1,0:T(8,128)S(1)} %copy-done.2, ...), custom_call_target="tpu_custom_call" | custom-call | flops 100000000 | bytes 6077456 | tf_op jit(solution)/shard_map/first_join/pallas_call | solution.py:206
  12.8 2.1 %collective-permute-start.2 = (f32[2,31,8,128]{3,2,1,0:T(8,128)S(1)}, f32[2,31,8,128]{3,2,1,0:T(8,128)S(1)}, u32[]{:S(2)}, u32[]{:S(2)}) collective-permute-start(f32[2,31,8,128]{3,2,1,0:T(8,128)S(1)} %get-tuple-element.28.high), channel_id=1, source_target_pairs={{0,8},{8,16},{16,24},{24,32},{32,40},{40,48},{48,56},{56,64},{64,7... | collective-permute-start | bytes 761864 | tf_op jit(solution)/shard_map/ppermute | solution.py:763
  14.9 4.7 %collective-permute-start.3 = (f32[2,31,8,128]{3,2,1,0:T(8,128)S(1)}, f32[2,31,8,128]{3,2,1,0:T(8,128)S(1)}, u32[]{:S(2)}, u32[]{:S(2)}) collective-permute-start(f32[2,31,8,128]{3,2,1,0:T(8,128)S(1)} %get-tuple-element.27.low), channel_id=1, source_target_pairs={{8,0},{16,8},{24,16},{32,24},{40,32},{48,40},{56,48},{64,56},{72,6... | collective-permute-start | bytes 761864 | tf_op jit(solution)/shard_map/ppermute | solution.py:763
  22.8 3.3 %collective-permute-done.2.from_low = f32[2,31,8,128]{3,2,1,0:T(8,128)S(1)} collective-permute-done((f32[2,31,8,128]{3,2,1,0:T(8,128)S(1)}, f32[2,31,8,128]{3,2,1,0:T(8,128)S(1)}, u32[]{:S(2)}, u32[]{:S(2)}) %collective-permute-start.2) | collective-permute-done | bytes 253984 | tf_op jit(solution)/shard_map/ppermute | solution.py:763
  26.1 5.5 %edge_solve.2 = (f32[2,31,8,128]{3,2,1,0:T(8,128)S(1)}, f32[2,31,8,128]{3,2,1,0:T(8,128)S(1)}, bf16[6,2,224,256]{3,2,1,0:T(8,128)(2,1)S(1)}) custom-call(s32[4]{0:T(128)S(1)} %pad_add_fusion.place, f32[10,2,112,256]{3,2,1,0:T(8,128)} %copy-done.1, bf16[112,160]{1,0:T(8,128)(2,1)S(1)} %copy-done.4, bf16[112,160]{1,0:T(8,128)(2,1)S(1)} %copy-done.5, ...), custom_call_target="tpu_custom_call" | custom-call | flops 1000000000 | bytes 8304656 | tf_op jit(solution)/shard_map/edge_solve/pallas_call | solution.py:206
  31.7 5.3 %collective-permute-start.5 = (f32[2,31,8,128]{3,2,1,0:T(8,128)S(1)}, f32[2,31,8,128]{3,2,1,0:T(8,128)S(1)}, u32[]{:S(2)}, u32[]{:S(2)}) collective-permute-start(f32[2,31,8,128]{3,2,1,0:T(8,128)S(1)} %get-tuple-element.29.low), channel_id=1, source_target_pairs={{8,0},{16,8},{24,16},{32,24},{40,32},{48,40},{56,48},{64,56},{72,6... | collective-permute-start | bytes 761864 | tf_op jit(solution)/shard_map/ppermute | solution.py:763
  38.4 4.5 %collective-permute-done.4.from_low = f32[2,31,8,128]{3,2,1,0:T(8,128)S(1)} collective-permute-done((f32[2,31,8,128]{3,2,1,0:T(8,128)S(1)}, f32[2,31,8,128]{3,2,1,0:T(8,128)S(1)}, u32[]{:S(2)}, u32[]{:S(2)}) %collective-permute-start.4) | collective-permute-done | bytes 253984 | tf_op jit(solution)/shard_map/ppermute | solution.py:763
  43.6 2.9 %collective-permute-start.7 = (f32[8,9,8,128]{3,2,1,0:T(8,128)S(1)}, f32[8,9,8,128]{3,2,1,0:T(8,128)S(1)}, u32[]{:S(2)}, u32[]{:S(2)}) collective-permute-start(f32[8,9,8,128]{3,2,1,0:T(8,128)S(1)} %get-tuple-element.36), channel_id=1, source_target_pairs={{1,0},{2,1},{3,2},{4,3},{5,4},{6,5},{7,6},{0,7},{9,8},{10,9},{11,1... | collective-permute-start | bytes 884744 | tf_op jit(solution)/shard_map/ppermute | solution.py:763
  46.5 2.4 %update.1 = (f32[8,31,8,128]{3,2,1,0:T(8,128)S(1)}, f32[8,15,8,128]{3,2,1,0:T(8,128)S(1)}) custom-call(s32[4]{0:T(128)S(1)} %pad_add_fusion.place, s32[8,32]{1,0:T(8,128)S(1)} %copy-done.9, f32[8,32,8,128]{3,2,1,0:T(8,128)S(1)} %copy-done, f32[3,1,4,128]{3,2,1,0:T(4,128)S(1)} %copy-done.10, bf16[128,192]{1,0:T(8,128)(2,1)S(1)} %copy-done.7, ...), custom_call_target="tpu_custom_call" | custom-call | flops 200000000 | bytes 4471824 | tf_op jit(solution)/shard_map/update/pallas_call | solution.py:206
  48.9 2.0 %collective-permute-done.6.low_news = f32[8,9,8,128]{3,2,1,0:T(8,128)S(1)} collective-permute-done((f32[8,9,8,128]{3,2,1,0:T(8,128)S(1)}, f32[8,9,8,128]{3,2,1,0:T(8,128)S(1)}, u32[]{:S(2)}, u32[]{:S(2)}) %collective-permute-start.6) | collective-permute-done | bytes 294944 | tf_op jit(solution)/shard_map/ppermute | solution.py:763
  50.9 3.3 %second_join.1 = (f32[8,4,8,128]{3,2,1,0:T(8,128)S(1)}, f32[2,31,8,128]{3,2,1,0:T(8,128)S(1)}, f32[6,31,8,128]{3,2,1,0:T(8,128)S(1)}, f32[2,31,8,128]{3,2,1,0:T(8,128)S(1)}) custom-call(s32[4]{0:T(128)S(1)} %pad_add_fusion.place, s32[8,32]{1,0:T(8,128)S(1)} %copy-done.9, f32[3,1,4,128]{3,2,1,0:T(4,128)S(1)} %copy-done.10, ...), custom_call_target="tpu_custom_call" | custom-call | flops 200000000 | bytes 5291024 | tf_op jit(solution)/shard_map/second_join/pallas_call | solution.py:206
  54.2 5.3 %collective-permute-start.9 = (f32[2,31,8,128]{3,2,1,0:T(8,128)S(1)}, f32[2,31,8,128]{3,2,1,0:T(8,128)S(1)}, u32[]{:S(2)}, u32[]{:S(2)}) collective-permute-start(f32[2,31,8,128]{3,2,1,0:T(8,128)S(1)} %get-tuple-element.39.low), channel_id=1, source_target_pairs={{8,0},{16,8},{24,16},{32,24},{40,32},{48,40},{56,48},{64,56},{72,6... | collective-permute-start | bytes 761864 | tf_op jit(solution)/shard_map/ppermute | solution.py:763
  61.0 4.7 %collective-permute-done.8.from_low = f32[2,31,8,128]{3,2,1,0:T(8,128)S(1)} collective-permute-done((f32[2,31,8,128]{3,2,1,0:T(8,128)S(1)}, f32[2,31,8,128]{3,2,1,0:T(8,128)S(1)}, u32[]{:S(2)}, u32[]{:S(2)}) %collective-permute-start.8) | collective-permute-done | bytes 253984 | tf_op jit(solution)/shard_map/ppermute | solution.py:763
  65.7 5.4 %edge_solve.3 = (f32[2,31,8,128]{3,2,1,0:T(8,128)S(1)}, f32[2,31,8,128]{3,2,1,0:T(8,128)S(1)}, bf16[6,2,224,256]{3,2,1,0:T(8,128)(2,1)S(1)}) custom-call(s32[4]{0:T(128)S(1)} %pad_add_fusion.place, f32[10,2,112,256]{3,2,1,0:T(8,128)} %copy-done.1, bf16[112,160]{1,0:T(8,128)(2,1)S(1)} %copy-done.4, bf16[112,160]{1,0:T(8,128)(2,1)S(1)} %copy-done.5, ...), custom_call_target="tpu_custom_call" | custom-call | flops 1000000000 | bytes 8304656 | tf_op jit(solution)/shard_map/edge_solve/pallas_call | solution.py:206
  71.2 5.3 %collective-permute-start.11 = (f32[2,31,8,128]{3,2,1,0:T(8,128)S(1)}, f32[2,31,8,128]{3,2,1,0:T(8,128)S(1)}, u32[]{:S(2)}, u32[]{:S(2)}) collective-permute-start(f32[2,31,8,128]{3,2,1,0:T(8,128)S(1)} %get-tuple-element.41.low), channel_id=1, source_target_pairs={{8,0},{16,8},{24,16},{32,24},{40,32},{48,40},{56,48},{64,56},{72,6... | collective-permute-start | bytes 761864 | tf_op jit(solution)/shard_map/ppermute | solution.py:763
  77.9 3.9 %collective-permute-done.10.from_low = f32[2,31,8,128]{3,2,1,0:T(8,128)S(1)} collective-permute-done((f32[2,31,8,128]{3,2,1,0:T(8,128)S(1)}, f32[2,31,8,128]{3,2,1,0:T(8,128)S(1)}, u32[]{:S(2)}, u32[]{:S(2)}) %collective-permute-start.10) | collective-permute-done | bytes 253984 | tf_op jit(solution)/shard_map/ppermute | solution.py:763
  82.5 2.9 %collective-permute-start.13 = (f32[8,2,8,128]{3,2,1,0:T(8,128)S(1)}, f32[8,2,8,128]{3,2,1,0:T(8,128)S(1)}, u32[]{:S(2)}, u32[]{:S(2)}) collective-permute-start(f32[8,2,8,128]{3,2,1,0:T(8,128)S(1)} %get-tuple-element.45), channel_id=1, source_target_pairs={{1,0},{2,1},{3,2},{4,3},{5,4},{6,5},{7,6},{0,7},{9,8},{10,9},{11,1... | collective-permute-start | bytes 196616 | tf_op jit(solution)/shard_map/ppermute | solution.py:763
  85.5 4.3 %residual.1 = f32[8,32,8,128]{3,2,1,0:T(8,128)} custom-call(s32[4]{0:T(128)S(1)} %pad_add_fusion.place, f32[2,31,8,128]{3,2,1,0:T(8,128)S(1)} %get-tuple-element.39.low, f32[6,31,8,128]{3,2,1,0:T(8,128)S(1)} %get-tuple-element.38.inner, f32[2,31,8,128]{3,2,1,0:T(8,128)S(1)} %get-tuple-element.40.high, f32[2,31,8,128]{3,2,1,0:T(8,128)S(1)} %collective-permute-done.8.from_low, ...), custom_call_target="tpu_custom_call" | custom-call | flops 10000000 | bytes 2826256 | tf_op jit(solution)/shard_map/residual/pallas_call | solution.py:206
  89.8 1.8 %last_update.1.before = f32[8,32,8,128]{3,2,1,0:T(8,128)} custom-call(s32[4]{0:T(128)S(1)} %pad_add_fusion.place, s32[8,32]{1,0:T(8,128)S(1)} %copy-done.9, f32[8,31,8,128]{3,2,1,0:T(8,128)S(1)} %get-tuple-element.32.field, f32[8,4,8,128]{3,2,1,0:T(8,128)S(1)} %get-tuple-element.37.changed, f32[2,31,8,128]{3,2,1,0:T(8,128)S(1)} %get-tuple-element.41.low, ...), custom_call_target="tpu_custom_call" | custom-call | flops 10000000 | bytes 3974160 | tf_op jit(solution)/shard_map/last_update/pallas_call | solution.py:206
  92.8 1.7 %last_join.1 = f32[8,32,8,128]{3,2,1,0:T(8,128)} custom-call(s32[4]{0:T(128)} %copy-done.12, s32[8,32]{1,0:T(8,128)} %outflow.15, f32[8,32,8,128]{3,2,1,0:T(8,128)} %last_update.1.before, f32[8,2,8,128]{3,2,1,0:T(8,128)} %copy-done.15, f32[8,2,8,128]{3,2,1,0:T(8,128)} %copy-done.16), custom_call_target="tpu_custom_call", output_to_operand_aliasing={{}: (2, {})} | custom-call | tf_op jit(solution)/shard_map/last_join/pallas_call | solution.py:748
  (56 shorter events, 10.4 us)
Async XLA Ops:
  0.6 5.1 %copy-start.7 = (bf16[128,192]{1,0:T(8,128)(2,1)S(1)}, bf16[128,192]{1,0:T(8,128)(2,1)}, u32[]{:S(2)}) copy-start(bf16[128,192]{1,0:T(8,128)(2,1)} %constant.31.clone.own_table) | copy-start | bytes 147460
  0.6 5.1 %copy-start.8 = (f32[8,8,128]{2,1,0:T(8,128)S(1)}, f32[8,8,128]{2,1,0:T(8,128)}, u32[]{:S(2)}) copy-start(f32[8,8,128]{2,1,0:T(8,128)} %constant.33.clone.plane_weights) | copy-start | bytes 98308
  2.8 7.6 %copy-start.2 = (f32[8,32,8,128]{3,2,1,0:T(8,128)S(1)}, f32[8,32,8,128]{3,2,1,0:T(8,128)}, u32[]{:S(2)}) copy-start(f32[8,32,8,128]{3,2,1,0:T(8,128)} %source.1) | copy-start | bytes 3145732
  2.8 7.6 %copy-start.9 = (s32[8,32]{1,0:T(8,128)S(1)}, s32[8,32]{1,0:T(8,128)}, u32[]{:S(2)}) copy-start(s32[8,32]{1,0:T(8,128)} %outflow.15) | copy-start | bytes 3076
  2.8 7.6 %copy-start.11 = (bf16[64,192]{1,0:T(8,128)(2,1)S(1)}, bf16[64,192]{1,0:T(8,128)(2,1)}, u32[]{:S(2)}) copy-start(bf16[64,192]{1,0:T(8,128)(2,1)} %constant.32.clone.side_table) | copy-start | bytes 73732
  2.8 7.6 %collective-permute-start = (f32[8,9,8,128]{3,2,1,0:T(8,128)}, f32[8,9,8,128]{3,2,1,0:T(8,128)S(1)}, u32[]{:S(2)}, u32[]{:S(2)}) collective-permute-start(f32[8,9,8,128]{3,2,1,0:T(8,128)} %get-tuple-element.24), channel_id=1, source_target_pairs={{0,1},{1,2},{2,3},{3,4},{4,5},{5,6},{6,7},{7,0},{8,9},{9,10},{10,1... | collective-permute-start | bytes 884744 | tf_op jit(solution)/shard_map/ppermute | solution.py:763
  2.8 7.6 %collective-permute-start.1 = (f32[8,9,8,128]{3,2,1,0:T(8,128)}, f32[8,9,8,128]{3,2,1,0:T(8,128)S(1)}, u32[]{:S(2)}, u32[]{:S(2)}) collective-permute-start(f32[8,9,8,128]{3,2,1,0:T(8,128)} %get-tuple-element.25), channel_id=1, source_target_pairs={{1,0},{2,1},{3,2},{4,3},{5,4},{6,5},{7,6},{0,7},{9,8},{10,9},{11,1... | collective-permute-start | bytes 884744 | tf_op jit(solution)/shard_map/ppermute | solution.py:763
  8.0 81.7 %copy-start.12 = (s32[4]{0:T(128)}, s32[4]{0:T(128)S(1)}, u32[]{:S(2)}) copy-start(s32[4]{0:T(128)S(1)} %pad_add_fusion.place) | copy-start | bytes 52
  8.0 11.5 %copy-start.13 = (f32[112,128]{1,0:T(8,128)S(1)}, f32[112,128]{1,0:T(8,128)}, u32[]{:S(2)}) copy-start(f32[112,128]{1,0:T(8,128)} %constant.34.clone.second_values) | copy-start | bytes 172036
  8.0 11.5 %copy-start.14 = (f32[112,128]{1,0:T(8,128)S(1)}, f32[112,128]{1,0:T(8,128)}, u32[]{:S(2)}) copy-start(f32[112,128]{1,0:T(8,128)} %constant.35.clone.third_values) | copy-start | bytes 172036
  12.8 8.6 %copy-start.4 = (bf16[112,160]{1,0:T(8,128)(2,1)S(1)}, bf16[112,160]{1,0:T(8,128)(2,1)}, u32[]{:S(2)}) copy-start(bf16[112,160]{1,0:T(8,128)(2,1)} %constant.36.clone.forward_high) | copy-start | bytes 107524
  12.8 8.6 %copy-start.5 = (bf16[112,160]{1,0:T(8,128)(2,1)S(1)}, bf16[112,160]{1,0:T(8,128)(2,1)}, u32[]{:S(2)}) copy-start(bf16[112,160]{1,0:T(8,128)(2,1)} %constant.37.clone.forward_low) | copy-start | bytes 107524
  12.8 13.3 %collective-permute-start.2 = (f32[2,31,8,128]{3,2,1,0:T(8,128)S(1)}, f32[2,31,8,128]{3,2,1,0:T(8,128)S(1)}, u32[]{:S(2)}, u32[]{:S(2)}) collective-permute-start(f32[2,31,8,128]{3,2,1,0:T(8,128)S(1)} %get-tuple-element.28.high), channel_id=1, source_target_pairs={{0,8},{8,16},{16,24},{24,32},{32,40},{40,48},{48,56},{56,64},{64,7... | collective-permute-start | bytes 761864 | tf_op jit(solution)/shard_map/ppermute | solution.py:763
  14.9 11.2 %collective-permute-start.3 = (f32[2,31,8,128]{3,2,1,0:T(8,128)S(1)}, f32[2,31,8,128]{3,2,1,0:T(8,128)S(1)}, u32[]{:S(2)}, u32[]{:S(2)}) collective-permute-start(f32[2,31,8,128]{3,2,1,0:T(8,128)S(1)} %get-tuple-element.27.low), channel_id=1, source_target_pairs={{8,0},{16,8},{24,16},{32,24},{40,32},{48,40},{56,48},{64,56},{72,6... | collective-permute-start | bytes 761864 | tf_op jit(solution)/shard_map/ppermute | solution.py:763
  31.6 11.3 %collective-permute-start.4 = (f32[2,31,8,128]{3,2,1,0:T(8,128)S(1)}, f32[2,31,8,128]{3,2,1,0:T(8,128)S(1)}, u32[]{:S(2)}, u32[]{:S(2)}) collective-permute-start(f32[2,31,8,128]{3,2,1,0:T(8,128)S(1)} %get-tuple-element.31.high), channel_id=1, source_target_pairs={{0,8},{8,16},{16,24},{24,32},{32,40},{40,48},{48,56},{56,64},{64,7... | collective-permute-start | bytes 761864 | tf_op jit(solution)/shard_map/ppermute | solution.py:763
  31.7 11.2 %collective-permute-start.5 = (f32[2,31,8,128]{3,2,1,0:T(8,128)S(1)}, f32[2,31,8,128]{3,2,1,0:T(8,128)S(1)}, u32[]{:S(2)}, u32[]{:S(2)}) collective-permute-start(f32[2,31,8,128]{3,2,1,0:T(8,128)S(1)} %get-tuple-element.29.low), channel_id=1, source_target_pairs={{8,0},{16,8},{24,16},{32,24},{40,32},{48,40},{56,48},{64,56},{72,6... | collective-permute-start | bytes 761864 | tf_op jit(solution)/shard_map/ppermute | solution.py:763
  43.5 7.4 %collective-permute-start.6 = (f32[8,9,8,128]{3,2,1,0:T(8,128)S(1)}, f32[8,9,8,128]{3,2,1,0:T(8,128)S(1)}, u32[]{:S(2)}, u32[]{:S(2)}) collective-permute-start(f32[8,9,8,128]{3,2,1,0:T(8,128)S(1)} %get-tuple-element.35), channel_id=1, source_target_pairs={{0,1},{1,2},{2,3},{3,4},{4,5},{5,6},{6,7},{7,0},{8,9},{9,10},{10,1... | collective-permute-start | bytes 884744 | tf_op jit(solution)/shard_map/ppermute | solution.py:763
  43.6 7.3 %collective-permute-start.7 = (f32[8,9,8,128]{3,2,1,0:T(8,128)S(1)}, f32[8,9,8,128]{3,2,1,0:T(8,128)S(1)}, u32[]{:S(2)}, u32[]{:S(2)}) collective-permute-start(f32[8,9,8,128]{3,2,1,0:T(8,128)S(1)} %get-tuple-element.36), channel_id=1, source_target_pairs={{1,0},{2,1},{3,2},{4,3},{5,4},{6,5},{7,6},{0,7},{9,8},{10,9},{11,1... | collective-permute-start | bytes 884744 | tf_op jit(solution)/shard_map/ppermute | solution.py:763
  54.2 11.5 %collective-permute-start.8 = (f32[2,31,8,128]{3,2,1,0:T(8,128)S(1)}, f32[2,31,8,128]{3,2,1,0:T(8,128)S(1)}, u32[]{:S(2)}, u32[]{:S(2)}) collective-permute-start(f32[2,31,8,128]{3,2,1,0:T(8,128)S(1)} %get-tuple-element.40.high), channel_id=1, source_target_pairs={{0,8},{8,16},{16,24},{24,32},{32,40},{40,48},{48,56},{56,64},{64,7... | collective-permute-start | bytes 761864 | tf_op jit(solution)/shard_map/ppermute | solution.py:763
  54.2 11.5 %collective-permute-start.9 = (f32[2,31,8,128]{3,2,1,0:T(8,128)S(1)}, f32[2,31,8,128]{3,2,1,0:T(8,128)S(1)}, u32[]{:S(2)}, u32[]{:S(2)}) collective-permute-start(f32[2,31,8,128]{3,2,1,0:T(8,128)S(1)} %get-tuple-element.39.low), channel_id=1, source_target_pairs={{8,0},{16,8},{24,16},{32,24},{40,32},{48,40},{56,48},{64,56},{72,6... | collective-permute-start | bytes 761864 | tf_op jit(solution)/shard_map/ppermute | solution.py:763
  71.2 10.7 %collective-permute-start.10 = (f32[2,31,8,128]{3,2,1,0:T(8,128)S(1)}, f32[2,31,8,128]{3,2,1,0:T(8,128)S(1)}, u32[]{:S(2)}, u32[]{:S(2)}) collective-permute-start(f32[2,31,8,128]{3,2,1,0:T(8,128)S(1)} %get-tuple-element.43.high), channel_id=1, source_target_pairs={{0,8},{8,16},{16,24},{24,32},{32,40},{40,48},{48,56},{56,64},{64,7... | collective-permute-start | bytes 761864 | tf_op jit(solution)/shard_map/ppermute | solution.py:763
  71.2 10.6 %collective-permute-start.11 = (f32[2,31,8,128]{3,2,1,0:T(8,128)S(1)}, f32[2,31,8,128]{3,2,1,0:T(8,128)S(1)}, u32[]{:S(2)}, u32[]{:S(2)}) collective-permute-start(f32[2,31,8,128]{3,2,1,0:T(8,128)S(1)} %get-tuple-element.41.low), channel_id=1, source_target_pairs={{8,0},{16,8},{24,16},{32,24},{40,32},{48,40},{56,48},{64,56},{72,6... | collective-permute-start | bytes 761864 | tf_op jit(solution)/shard_map/ppermute | solution.py:763
  82.5 9.1 %collective-permute-start.12 = (f32[8,2,8,128]{3,2,1,0:T(8,128)S(1)}, f32[8,2,8,128]{3,2,1,0:T(8,128)S(1)}, u32[]{:S(2)}, u32[]{:S(2)}) collective-permute-start(f32[8,2,8,128]{3,2,1,0:T(8,128)S(1)} %get-tuple-element.44), channel_id=1, source_target_pairs={{0,1},{1,2},{2,3},{3,4},{4,5},{5,6},{6,7},{7,0},{8,9},{9,10},{10,1... | collective-permute-start | bytes 196616 | tf_op jit(solution)/shard_map/ppermute | solution.py:763
  82.5 9.0 %collective-permute-start.13 = (f32[8,2,8,128]{3,2,1,0:T(8,128)S(1)}, f32[8,2,8,128]{3,2,1,0:T(8,128)S(1)}, u32[]{:S(2)}, u32[]{:S(2)}) collective-permute-start(f32[8,2,8,128]{3,2,1,0:T(8,128)S(1)} %get-tuple-element.45), channel_id=1, source_target_pairs={{1,0},{2,1},{3,2},{4,3},{5,4},{6,5},{7,6},{0,7},{9,8},{10,9},{11,1... | collective-permute-start | bytes 196616 | tf_op jit(solution)/shard_map/ppermute | solution.py:763
  (7 other events, 22.4 us)
where the time goes:
time: 94.7 us; the launch traced here: 94.5 us
  Pallas kernels  38.2 us (40%)
  starting transfers between devices  31.8 us (34%)
  waiting for transfers between devices  20.7 us (22%)
  local copies, waits for them, and re-layouts  2.7 us (3%)
    pallas_call x15, Pallas kernels, call(): pl.pallas_call(body, out_shape=tuple(outs), in_specs=[whole(pltpu.SMEM if...  34.5 us
    ppermute x7, starting transfers between devices, exchange(): lax.ppermute(to_low, axis, downward)  29.5 us
    ppermute x7, waiting for transfers between devices, exchange(): lax.ppermute(to_high, axis, upward)  20.7 us
    unnamed x34, local copies, waits for them, and re-layouts  2.7 us
    ppermute x7, starting transfers between devices, exchange(): lax.ppermute(to_high, axis, upward)  2.37 us
    pallas_call x1, Pallas kernels, pack_first(): pl.pallas_call(pack_body, grid=(1,), out_shape=(layers(8, 9), layers(8, 9...  2.1 us
  transfers between devices with their start and end apart: 14, of which 6 were waited for; matrix products, arithmetic and copies ran while one was open for 0% of the time, Pallas kernels for 18%

commit v1 on v0

--- a/solution.py
+++ b/solution.py
@@ -20,7 +20,8 @@
 )
 F32 = jnp.float32
 BF16 = jnp.bfloat16
-VMEM_BYTES = 48 * 1024 * 1024
+VMEM_BYTES = 20 * 1024 * 1024
+PACK_VMEM_BYTES = 60 * 1024 * 1024
 
 
 def legendre_seven(points):
@@ -111,7 +112,7 @@
         rows = [8 * j + k for j in places for k in range(8)]
         high, low = two_parts(np.concatenate([along_second[rows], along_third[rows]]))
         sets.append(np.concatenate([high, high, low], axis=1))
-    return sets
+    return np.concatenate(sets)
 
 
 def transform_tables():
@@ -140,10 +141,9 @@
     return second_values, third_values
 
 
-OPERATOR_OWN, OPERATOR_SIDE = operator_tables()
-PLANE_WEIGHTS = np.broadcast_to(
-    (WEIGHT[:, None] * WEIGHT[None, :])[:, :, None], (8, 8, 128)
-).astype(np.float32)
+OPERATOR = operator_tables()
+OWN_ROWS = (0, 128)
+SIDE_ROWS = (128, 192)
 FORWARD, BACKWARD = transform_tables()
 VALUES = value_tables()
 LANES = (slice(0, 128), slice(128, 256))
@@ -183,6 +183,24 @@
 
 def ghost_keep(message, i):
     return jnp.where(row_ids() == 7, message[i, 8], 1.0)
+
+
+def weight_at(j):
+    if isinstance(j, int):
+        return float(WEIGHT[j])
+    near = jnp.minimum(j, 7 - j)
+    weight = float(WEIGHT[3])
+    for place in (2, 1, 0):
+        weight = jnp.where(near == place, float(WEIGHT[place]), weight)
+    return weight
+
+
+def row_weights():
+    near = jnp.minimum(row_ids(), 7 - row_ids())
+    weights = jnp.full((8, 128), float(WEIGHT[3]), F32)
+    for place in (2, 1, 0):
+        weights = jnp.where(near == place, float(WEIGHT[place]), weights)
+    return weights
 
 
 def spread_row(row):
@@ -217,53 +235,61 @@
     )(*args)
 
 
-def pack_body(start_low, start_high, source_low, source_high, coefficients, outflow, low, high):
+def pack_body(
+    outflow, start, source, coefficients, low, high, gains, semaphores
+):
+    sides = ((low, 1, 1, 0), (high, 24, 30, 3))
+    copies = [pltpu.make_async_copy(coefficients, gains, semaphores.at[0])]
+    for n, (target, first, node, element) in enumerate(sides):
+        copies.append(
+            pltpu.make_async_copy(
+                start.at[:, first : first + 7], target.at[:, 0:7], semaphores.at[1 + 2 * n]
+            )
+        )
+        copies.append(
+            pltpu.make_async_copy(
+                source.at[:, node : node + 1], target.at[:, 7:8], semaphores.at[2 + 2 * n]
+            )
+        )
+    for copy in copies:
+        copy.start()
+    copies[0].wait()
     top = top_flags()
     rows = row_ids()
-    for target, start, source, first, node, element in (
-        (low, start_low, source_low, 1, 1, 0),
-        (high, start_high, source_high, 0, 6, 3),
-    ):
-        gains = [spread_row(coefficients[c, 0, element : element + 1, :]) for c in range(3)]
-        info = jnp.where(rows == 0, gains[0], jnp.where(rows == 1, gains[1], gains[2]))
-
-        def step(i, carry, target=target, start=start, source=source, first=first, node=node,
-                 element=element, info=info):
-            target[i, 0:7] = start[i, first : first + 7]
-            target[i, 7] = source[i, 0]
-            keep = own_keep(outflow, top, i, 8 * element + node)
-            target[i, 8] = jnp.where(rows == 7, keep, info)
-            return carry
-
-        lax.fori_loop(0, 8, step, 0)
+    for target, first, node, element in sides:
+        rows_of = [spread_row(gains[c, 0, element : element + 1, :]) for c in range(3)]
+        gain = jnp.where(rows == 0, rows_of[0], jnp.where(rows == 1, rows_of[1], rows_of[2]))
+        for i in range(8):
+            target[i, 8] = jnp.where(rows == 7, own_keep(outflow, top, i, node), gain)
+    for copy in copies[1:]:
+        copy.wait()
 
 
 def pack_first(start, source, coefficients, outflow):
-    def block(rows, at):
-        return pl.BlockSpec((8, rows, 8, 128), lambda g: (0, at, 0, 0))
-
+    anywhere = whole(pltpu.HBM)
     return pl.pallas_call(
         pack_body,
-        grid=(1,),
-        out_shape=(layers(8, 9), layers(8, 9)),
-        in_specs=[
-            block(8, 0),
-            block(8, 3),
-            block(1, 1),
-            block(1, 30),
-            pl.BlockSpec((3, 1, 4, 128), lambda g: (0, 0, 0, 0)),
-            pl.BlockSpec(memory_space=pltpu.SMEM),
-        ],
-        out_specs=(block(9, 0), block(9, 0)),
+        out_shape=(layers(8, 9), layers(8, 9), jax.ShapeDtypeStruct(coefficients.shape, F32)),
+        in_specs=[whole(pltpu.SMEM), anywhere, anywhere, anywhere],
+        out_specs=(whole(), whole(), whole()),
+        scratch_shapes=[pltpu.SemaphoreType.DMA((5,))],
+        compiler_params=pltpu.CompilerParams(vmem_limit_bytes=PACK_VMEM_BYTES),
         name="pack_first",
-    )(start, start, source, source, coefficients, outflow)
-
-
-def first_direction(values):
+    )(outflow, start, source, coefficients)
+
+
+EDGES = (0, 1, 6, 7)
+INNER = (2, 3, 4, 5)
+EVERY = tuple(range(8))
+
+
+def first_direction(values, wanted):
     sums = [values[a] + values[7 - a] for a in range(4)]
     gaps = [values[a] - values[7 - a] for a in range(4)]
-    outs = [None] * 8
+    outs = {}
     for i in range(4):
+        if i not in wanted:
+            continue
         even = odd = None
         for a in range(4):
             even_term = sums[a] * float(0.5 * (STIFF[i, a] + STIFF[i, 7 - a]))
@@ -275,22 +301,31 @@
     return outs
 
 
-def products(pair, table, count, planes):
-    def step(i, carry):
+def products(pair, table, rows, planes, wanted):
+    def step(n, carry):
+        if wanted is EVERY:
+            i = n
+        elif wanted is INNER:
+            i = n + 2
+        else:
+            i = n + 4 * (n // 2)
         values = jnp.concatenate(
             [field[i, at : at + 8].reshape(64, 128) for field, at in pair], axis=1
         )
         high, low = split(values)
-        planes[i, 0:count] = dot(table[...], jnp.concatenate([high, low, high], axis=0))
+        planes[i, 0 : rows[1] - rows[0]] = dot(
+            table[rows[0] : rows[1]], jnp.concatenate([high, low, high], axis=0)
+        )
         return carry
 
-    lax.fori_loop(0, 8, step, 0, unroll=2)
-
-
-def combine(field, at, gain, weights, planes, lane, second_at, third_at, image, target, add):
-    terms = first_direction([field[a, at] for a in range(8)])
-    plane = gain[0] * weights
-    for i in range(8):
+    lax.fori_loop(0, len(wanted), step, 0, unroll=2)
+
+
+def combine(
+    field, at, gain, plane, planes, lane, second_at, third_at, image, target, add, wanted
+):
+    terms = first_direction([field[a, at] for a in range(8)], wanted)
+    for i in wanted:
         second = planes[i, pl.ds(second_at, 8), lane]
         third = planes[i, pl.ds(third_at, 8), lane]
         value = plane * terms[i] + float(WEIGHT[i]) * (gain[1] * second + gain[2] * third)
@@ -299,17 +334,18 @@
         image[i, target] = value
 
 
-def own_elements(pair, gains, table, plane_weights, planes, image, offset):
-    products([(field, at) for _, field, at, _, _ in pair], table, 128, planes)
+def own_elements(pair, gains, table, planes, image, offset, wanted=EVERY):
+    products([(field, at) for _, field, at, _, _ in pair], table, OWN_ROWS, planes, wanted)
     for (e, field, at, add_first, add_last), lane in zip(pair, LANES):
         gain = gains(e)
+        plane = gain[0] * row_weights()
         base = 7 * e + offset
 
-        def row(j, add, field=field, at=at, lane=lane, gain=gain, base=base):
+        def row(j, add, field=field, at=at, lane=lane, gain=gain, plane=plane, base=base):
             start = 8 * j if isinstance(j, int) else pl.multiple_of(8 * j, 8)
             combine(
-                field, at + j, gain, plane_weights[j], planes, lane, start, start + 64,
-                image, base + j, add,
+                field, at + j, gain, plane * weight_at(j), planes, lane, start, start + 64,
+                image, base + j, add, wanted,
             )
 
         row(0, add_first)
@@ -325,38 +361,33 @@
     return [spread_row(message[0, 8, c : c + 1, :] * flag) for c in range(3)]
 
 
-def side_elements(field, low_at, high_at, low_gain, high_gain, table, plane_weights, planes, image):
-    products([(field, low_at), (field, high_at)], table, 64, planes)
+def side_elements(
+    field, low_at, high_at, low_gain, high_gain, table, planes, image, wanted
+):
+    products([(field, low_at), (field, high_at)], table, SIDE_ROWS, planes, wanted)
+    low_plane = low_gain[0] * row_weights()
+    high_plane = high_gain[0] * row_weights()
     for q in range(2):
         combine(
-            field, low_at + 6 + q, low_gain, plane_weights[6 + q], planes, LANES[0],
-            16 + 8 * q, 48 + 8 * q, image, q, q == 1,
+            field, low_at + 6 + q, low_gain, low_plane * weight_at(6 + q), planes,
+            LANES[0], 16 + 8 * q, 48 + 8 * q, image, q, q == 1, wanted,
         )
         combine(
-            field, high_at + q, high_gain, plane_weights[q], planes, LANES[1],
-            8 * q, 32 + 8 * q, image, 29 + q, q == 0,
+            field, high_at + q, high_gain, high_plane * weight_at(q), planes,
+            LANES[1], 8 * q, 32 + 8 * q, image, 29 + q, q == 0, wanted,
         )
 
 
-def finish_residual(image_row, source_part, outflow, from_low, from_high, low, inner, high):
+def finish_residual(wanted, image, source_row, outflow, from_low, from_high, put):
     top = top_flags()
-
-    def place_row(i, y, value):
-        if i < 2:
-            low[i, y] = value
-        if 0 < i < 7:
-            inner[i - 1, y] = value
-        if i > 5:
-            high[i - 6, y] = value
-
-    for i in range(8):
+    for i in wanted:
 
         def own_row(y, column, i=i):
-            value = source_part[i, y] - image_row(i, y)
-            place_row(i, y, own_keep(outflow, top, i, column) * value)
-
-        place_row(i, 0, ghost_keep(from_low, i) * (source_part[i, 0] - image_row(i, 0)))
-        place_row(i, 30, ghost_keep(from_high, i) * (source_part[i, 30] - image_row(i, 30)))
+            value = source_row(i, y) - image[i, y]
+            put(i, y, own_keep(outflow, top, i, column) * value)
+
+        put(i, 0, ghost_keep(from_low, i) * (source_row(i, 0) - image[i, 0]))
+        put(i, 30, ghost_keep(from_high, i) * (source_row(i, 30) - image[i, 30]))
         own_row(29, 31)
 
         def step(e, carry, own_row=own_row):
@@ -367,17 +398,75 @@
         lax.fori_loop(0, 4, step, 0)
 
 
+def put_edges(low, high):
+    def put(i, y, value):
+        if i < 2:
+            low[i, y] = value
+        else:
+            high[i - 6, y] = value
+
+    return put
+
+
+def put_inner(low, high, inner):
+    inner[0] = low[1]
+    inner[5] = high[0]
+
+    def put(i, y, value):
+        inner[i - 1, y] = value
+
+    return put
+
+
+def source_share(place, i):
+    lane = lane_ids()
+    row = row_ids()
+    inner_face = ((row == 0) & (lane > 0)) | ((row == 7) & (lane < 127))
+    share = jnp.where(inner_face, 0.5, 1.0)
+    below, above = ends(place, 0)
+    if i == 0:
+        share = share * (1.0 - 0.5 * below)
+    if i == 7:
+        share = share * (1.0 - 0.5 * above)
+    return share
+
+
+def source_rows(place, source_part, from_low, from_high):
+    low_flag, high_flag = ends(place, 1)
+
+    def source_row(i, y):
+        if isinstance(y, int) and y == 0:
+            return from_low[i, 7] * (source_share(place, i) * low_flag)
+        if isinstance(y, int) and y == 30:
+            return from_high[i, 7] * (source_share(place, i) * high_flag)
+        return source_part[i, y]
+
+    return source_row
+
+
 def plane_scratch():
     return pltpu.VMEM((8, 128, 256), F32)
 
 
-def own_image_body(coefficients, start, own_table, plane_weights, image, planes):
+def own_image_body(
+    place, coefficients, start, source, table, image, source_part, planes
+):
     gains = own_gains(coefficients)
     for pair in ((0, 1), (2, 3)):
         own_elements(
             [(e, start, 8 * e, e > 0, False) for e in pair],
-            gains, own_table, plane_weights, planes, image, 1,
+            gains, table, planes, image, 1,
         )
+    for i in range(8):
+        share = source_share(place, i)
+        source_part[i, 29] = source[i, 31] * share
+
+        def step(e, carry, i=i, share=share):
+            for j in range(7):
+                source_part[i, 1 + 7 * e + j] = source[i, 8 * e + j] * share
+            return carry
+
+        lax.fori_loop(0, 4, step, 0)
 
 
 def reciprocal_body(coefficients, second_values, third_values, result):
@@ -399,46 +488,26 @@
 
 
 def first_join_body(
-    place, outflow, start, source, coefficients, from_low, from_high, side_table, plane_weights,
-    own_image, source_part, low, inner, high, planes, field, image,
-):
-    lane = lane_ids()
-    row = row_ids()
-    inner_face = ((row == 0) & (lane > 0)) | ((row == 7) & (lane < 127))
-    third_share = jnp.where(inner_face, 0.5, 1.0)
-    below, above = ends(place, 0)
+    wanted, place, outflow, start, from_low, from_high, table,
+    own_image, source_part, *rest,
+):
     low_flag, high_flag = ends(place, 1)
+    *outs, planes, field, image = rest
     for i in range(8):
         field[i, 0:7] = from_low[i, 0:7]
         field[i, 7] = start[i, 0]
         field[i, 8] = start[i, 31]
         field[i, 9:16] = from_high[i, 0:7]
-        image[i, 1] = own_image[i, 1]
-        image[i, 29] = own_image[i, 29]
-        share = third_share
-        if i == 0:
-            share = third_share * (1.0 - 0.5 * below)
-        if i == 7:
-            share = third_share * (1.0 - 0.5 * above)
-        source_part[i, 0] = from_low[i, 7] * (share * low_flag)
-        source_part[i, 30] = from_high[i, 7] * (share * high_flag)
-        source_part[i, 29] = source[i, 31] * share
-
-        def step(e, carry, i=i, share=share):
-            for j in range(7):
-                source_part[i, 1 + 7 * e + j] = source[i, 8 * e + j] * share
-            return carry
-
-        lax.fori_loop(0, 4, step, 0)
+    for i in wanted:
+        image[i, 1:30] = own_image[i, 1:30]
     side_elements(
         field, 0, 8, side_gains(low_flag, from_low), side_gains(high_flag, from_high),
-        side_table, plane_weights, planes, image,
-    )
-
-    for i in range(8):
-        image[i, 2:29] = own_image[i, 2:29]
+        table, planes, image, wanted,
+    )
+    put = put_edges(*outs) if wanted is EDGES else put_inner(*outs)
     finish_residual(
-        lambda i, y: image[i, y], source_part, outflow, from_low, from_high, low, inner, high
+        wanted, image, source_rows(place, source_part, from_low, from_high), outflow,
+        from_low, from_high, put,
     )
 
 
@@ -513,13 +582,60 @@
     lax.fori_loop(0, count // 2, step, 0)
 
 
-def inner_forward_body(inner, forward_high, forward_low, spectral):
+def from_modes(modes, a):
+    even = odd = None
+    for p in EVEN:
+        term = modes[p] * float(HALF_BASIS[a, p])
+        even = term if even is None else even + term
+    for p in ODD:
+        term = modes[p] * float(HALF_BASIS[a, p])
+        odd = term if odd is None else odd + term
+    return even + odd, even - odd
+
+
+def to_modes(pairs, first, modes):
+    sums = [x + y for x, y in pairs]
+    gaps = [x - y for x, y in pairs]
+    for p in range(10):
+        sides = sums if PARITY[p] > 0 else gaps
+        total = modes[p]
+        for n, value in enumerate(sides):
+            term = value * float(HALF_BASIS[first + n, p])
+            total = term if total is None else total + term
+        modes[p] = total
+    return modes
+
+
+def over_blocks(visit):
+    def step(block, carry):
+        at = pl.multiple_of(16 * block, 16)
+        for e in range(4):
+            visit(lambda shift=0, e=e: (e // 2, pl.ds(shift + at, 16), LANES[e % 2]))
+        return carry
+
+    lax.fori_loop(0, 7, step, 0)
+
+
+def store_halves(halves, layer, spot, value):
+    top, bottom = split(value)
+    halves[(layer,) + spot()] = top
+    halves[(layer,) + spot(112)] = bottom
+
+
+def inner_forward_body(inner, forward_high, forward_low, partial, spectral):
     forward_layers(inner, 6, forward_high, forward_low, spectral)
 
+    def visit(spot):
+        pairs = [(spectral[(n,) + spot()], spectral[(5 - n,) + spot()]) for n in range(3)]
+        for p, value in enumerate(to_modes(pairs, 2, [None] * 10)):
+            partial[(p,) + spot()] = value
+
+    over_blocks(visit)
+
 
 def edge_solve_body(
-    place, reciprocals, forward_high, forward_low, backward, backward_low, spectral,
-    low, high, from_low, from_high, out_low, out_high, inner_halves, edges, edge_spectral, halves,
+    place, reciprocals, forward_high, forward_low, backward, backward_low, partial,
+    low, high, from_low, from_high, out_low, out_high, modes, edges, spectral, halves,
 ):
     below, above = ends(place, 0)
 
@@ -531,45 +647,20 @@
         return carry
 
     lax.fori_loop(0, 31, gather, 0)
-    forward_layers(edges, 4, forward_high, forward_low, edge_spectral)
-
-    def layer(a):
-        if a < 2:
-            return edge_spectral, halves, a
-        if a < 8:
-            return spectral, inner_halves, a - 2
-        return edge_spectral, halves, a - 6
-
-    def middle_step(block, carry):
-        at = pl.multiple_of(16 * block, 16)
-        for e in range(4):
-            spot = (e // 2, pl.ds(at, 16), LANES[e % 2])
-            values = [layer(a)[0][(layer(a)[2],) + spot] for a in range(10)]
-            sums = [values[a] + values[9 - a] for a in range(5)]
-            gaps = [values[a] - values[9 - a] for a in range(5)]
-            modes = []
-            for p in range(10):
-                sides = sums if PARITY[p] > 0 else gaps
-                total = sides[0] * float(HALF_BASIS[0, p])
-                for a in range(1, 5):
-                    total = total + sides[a] * float(HALF_BASIS[a, p])
-                modes.append(total * reciprocals[(p,) + spot])
-            for a in range(5):
-                even = odd = None
-                for p in EVEN:
-                    term = modes[p] * float(HALF_BASIS[a, p])
-                    even = term if even is None else even + term
-                for p in ODD:
-                    term = modes[p] * float(HALF_BASIS[a, p])
-                    odd = term if odd is None else odd + term
-                for spot_layer, value in ((a, even + odd), (9 - a, even - odd)):
-                    top, bottom = split(value)
-                    _, target, index = layer(spot_layer)
-                    target[index, e // 2, pl.ds(at, 16), LANES[e % 2]] = top
-                    target[index, e // 2, pl.ds(112 + at, 16), LANES[e % 2]] = bottom
-        return carry
-
-    lax.fori_loop(0, 7, middle_step, 0)
+    forward_layers(edges, 4, forward_high, forward_low, spectral)
+
+    def visit(spot):
+        pairs = [(spectral[(n,) + spot()], spectral[(3 - n,) + spot()]) for n in range(2)]
+        values = to_modes(pairs, 0, [partial[(p,) + spot()] for p in range(10)])
+        for p in range(10):
+            values[p] = values[p] * reciprocals[(p,) + spot()]
+            modes[(p,) + spot()] = values[p]
+        for a in range(2):
+            lower, upper = from_modes(values, a)
+            store_halves(halves, a, spot, lower)
+            store_halves(halves, 3 - a, spot, upper)
+
+    over_blocks(visit)
 
     def back(first, target):
         backward_layers(halves.at[first : first + 2], 2, backward, backward_low, target)
@@ -578,14 +669,25 @@
     back(2, out_high)
 
 
-def inner_backward_body(inner_halves, backward, backward_low, out_inner):
-    backward_layers(inner_halves, 6, backward, backward_low, out_inner)
-
-
-def residual_body(place, low, inner, high, from_low, from_high, residual):
+def inner_backward_body(modes, backward, backward_low, out_inner, halves):
+    def visit(spot):
+        values = [modes[(p,) + spot()] for p in range(10)]
+        for n in range(3):
+            lower, upper = from_modes(values, n + 2)
+            store_halves(halves, n, spot, lower)
+            store_halves(halves, 5 - n, spot, upper)
+
+    over_blocks(visit)
+    backward_layers(halves, 6, backward, backward_low, out_inner)
+
+
+def residual_body(place, low, inner, high, from_low, from_high, residual, layer, semaphores):
     row = row_ids()
     lane = lane_ids()
     below, above = ends(place, 0)
+    into_first = (row == 0) & (lane > 0)
+    into_last = (row == 7) & (lane < 127)
+    copies = []
     for i in range(8):
 
         def value_at(y, i=i):
@@ -595,18 +697,33 @@
                 value = high[1, y] + above * from_high[0, y]
             else:
                 value = inner[i - 1, y]
-            before = jnp.where((row == 0) & (lane > 0), pltpu.roll(pltpu.roll(value, 1, 0), 1, 1), 0.0)
-            after = jnp.where(
-                (row == 7) & (lane < 127), pltpu.roll(pltpu.roll(value, 7, 0), 127, 1), 0.0
-            )
-            return value + before + after
+            before = pltpu.roll(pltpu.roll(value, 1, 0), 1, 1)
+            after = pltpu.roll(pltpu.roll(value, 7, 0), 127, 1)
+            return value + jnp.where(into_first, before, jnp.where(into_last, after, 0.0))
 
         def step(e, carry, i=i, value_at=value_at):
             for j in range(8):
-                residual[i, 8 * e + j] = value_at(1 + 7 * e + j)
+                layer[i, 8 * e + j] = value_at(1 + 7 * e + j)
             return carry
 
         lax.fori_loop(0, 4, step, 0)
+        copies.append(pltpu.make_async_copy(layer.at[i], residual.at[i], semaphores.at[i]))
+        copies[-1].start()
+    for copy in copies:
+        copy.wait()
+
+
+def residual_out(place, low, inner, high, received):
+    return pl.pallas_call(
+        residual_body,
+        out_shape=layers(8, 32),
+        in_specs=[whole(pltpu.SMEM)] + [whole()] * 5,
+        out_specs=whole(pltpu.HBM),
+        scratch_shapes=[pltpu.VMEM((8, 32, 8, 128), F32), pltpu.SemaphoreType.DMA((8,))],
+        cost_estimate=pl.CostEstimate(flops=10**7, bytes_accessed=2**22, transcendentals=0),
+        compiler_params=pltpu.CompilerParams(vmem_limit_bytes=VMEM_BYTES),
+        name="residual",
+    )(place, low, inner, high, *received)
 
 
 def fold_row(ends_flags, i, y, low, inner, high, from_low, from_high):
@@ -637,7 +754,7 @@
 
 
 def update_body(
-    place, outflow, start, coefficients, own_table, plane_weights, low, inner, high,
+    place, outflow, start, coefficients, table, low, inner, high,
     from_low, from_high, field, image, planes,
 ):
     top = top_flags()
@@ -661,14 +778,12 @@
         lax.fori_loop(0, 4, step, 0)
     own_elements(
         [(1, field, 8, False, False), (2, field, 15, True, False)],
-        own_gains(coefficients), own_table, plane_weights, planes, image, -7,
-    )
-
-
-def second_join_body(
-    place, outflow, coefficients, from_low, from_high, own_table, side_table, plane_weights,
-    field, middle_image, source_part, low_news, high_news,
-    changed, low, inner, high, planes, rows, image,
+        own_gains(coefficients), table, planes, image, -7,
+    )
+
+
+def second_rows_body(
+    place, outflow, from_low, from_high, field, low_news, high_news, rows, changed
 ):
     top = top_flags()
     low_flag, high_flag = ends(place, 1)
@@ -692,20 +807,51 @@
             field[i, 30] + high_flag * high_news[i, 2]
         )
         rows[i, 24:30] = from_high[i, 1:7] + high_news[i, 3:9]
-        image[i, 8] = middle_image[i, 0]
-        image[i, 22] = middle_image[i, 14]
+
+
+def second_residual(
+    wanted, place, outflow, coefficients, from_low, from_high, table,
+    rows, middle_image, source_part, planes, image, put,
+):
+    low_flag, high_flag = ends(place, 1)
+    for i in wanted:
+        image[i, 8:23] = middle_image[i]
     own_elements(
         [(0, rows, 7, False, True), (3, rows, 15, True, False)],
-        own_gains(coefficients), own_table, plane_weights, planes, image, 1,
+        own_gains(coefficients), table, planes, image, 1, wanted,
     )
     side_elements(
         rows, 0, 22, side_gains(low_flag, from_low), side_gains(high_flag, from_high),
-        side_table, plane_weights, planes, image,
-    )
-    for i in range(8):
-        image[i, 9:22] = middle_image[i, 1:14]
+        table, planes, image, wanted,
+    )
     finish_residual(
-        lambda i, y: image[i, y], source_part, outflow, from_low, from_high, low, inner, high
+        wanted, image, source_rows(place, source_part, from_low, from_high), outflow,
+        from_low, from_high, put,
+    )
+
+
+def second_edges_body(
+    place, outflow, coefficients, from_low, from_high, table,
+    field, middle_image, source_part, low_news, high_news,
+    changed, rows, low, high, planes, image,
+):
+    second_rows_body(
+        place, outflow, from_low, from_high, field, low_news, high_news, rows, changed
+    )
+    second_residual(
+        EDGES, place, outflow, coefficients, from_low, from_high, table,
+        rows, middle_image, source_part, planes, image, put_edges(low, high),
+    )
+
+
+def second_inner_body(
+    place, outflow, coefficients, from_low, from_high, table,
+    rows, middle_image, source_part, low, high, inner, planes, image,
+):
+    second_residual(
+        INNER, place, outflow, coefficients, from_low, from_high, table,
+        rows, middle_image, source_part, planes, image,
+        put_inner(low, high, inner),
     )
 
 
@@ -731,27 +877,33 @@
                 result[i, column - 1] = value
 
 
-def last_join_body(place, outflow, before, low_news, high_news, result):
+def last_join_body(place, outflow, before, low_news, high_news, result, edges, semaphores):
+    copies = [
+        pltpu.make_async_copy(before.at[:, 2:30], result.at[:, 2:30], semaphores.at[0]),
+        pltpu.make_async_copy(edges.at[:, 0:2], result.at[:, 0:2], semaphores.at[1]),
+        pltpu.make_async_copy(edges.at[:, 2:4], result.at[:, 30:32], semaphores.at[2]),
+    ]
+    copies[0].start()
     top = top_flags()
     low_flag, high_flag = ends(place, 1)
-    side = pl.program_id(0)
-    flag = jnp.where(side == 0, low_flag, high_flag)
-    for i in range(8):
-        for n in range(2):
-            news = jnp.where(side == 0, low_news[i, n], high_news[i, n])
-            keep = own_keep(outflow, top, i, 30 * side + n)
-            result[i, n] = before[i, n] + keep * (flag * news)
+    for first, at, flag, news in ((0, 0, low_flag, low_news), (30, 2, high_flag, high_news)):
+        for i in range(8):
+            for n in range(2):
+                keep = own_keep(outflow, top, i, first + n)
+                edges[i, at + n] = before[i, first + n] + keep * (flag * news[i, n])
+        copies[1 + at // 2].start()
+    for copy in copies:
+        copy.wait()
 
 
 def last_join(place, outflow, before, low_news, high_news):
-    block = pl.BlockSpec((8, 2, 8, 128), lambda g: (0, 15 * g, 0, 0))
     return pl.pallas_call(
         last_join_body,
-        grid=(2,),
         out_shape=layers(8, 32),
-        in_specs=[whole(pltpu.SMEM), whole(pltpu.SMEM), block, whole(), whole()],
-        out_specs=block,
-        input_output_aliases={2: 0},
+        in_specs=[whole(pltpu.SMEM), whole(pltpu.SMEM), whole(), whole(), whole()],
+        out_specs=whole(pltpu.HBM),
+        scratch_shapes=[pltpu.VMEM((8, 4, 8, 128), F32), pltpu.SemaphoreType.DMA((3,))],
+        compiler_params=pltpu.CompilerParams(vmem_limit_bytes=VMEM_BYTES),
         name="last_join",
     )(place, outflow, before, low_news, high_news)
 
@@ -767,18 +919,20 @@
     return jax.ShapeDtypeStruct((count, 2, rows, 256), dtype)
 
 
-def solve(place, reciprocals, parts):
+def solve(place, reciprocals, edge_parts, make_inner, beside):
     forward = [jnp.asarray(t) for t in FORWARD]
     backward = [jnp.asarray(t) for t in BACKWARD]
-    low, inner, high = parts
+    low, high = edge_parts
     received = exchange(low, high, "dom")
-    (spectral,) = call(
-        inner_forward_body, [modes_shape(6, 112, F32)], 0, [], "inner_forward",
+    inner = make_inner()
+    (partial,) = call(
+        inner_forward_body, [modes_shape(10, 112, F32)], 0,
+        [pltpu.VMEM((6, 2, 112, 256), F32)], "inner_forward",
         (inner, *forward), 3 * 10**8,
     )
-    out_low, out_high, halves = call(
+    out_low, out_high, modes = call(
         edge_solve_body,
-        [layers(2, 31), layers(2, 31), modes_shape(6, 224, BF16)],
+        [layers(2, 31), layers(2, 31), modes_shape(10, 112, F32)],
         1,
         [
             pltpu.VMEM((4, 31, 8, 128), F32),
@@ -786,15 +940,19 @@
             pltpu.VMEM((4, 2, 224, 256), BF16),
         ],
         "edge_solve",
-        (place, reciprocals, *forward, *backward, spectral, low, high, *received),
+        (place, reciprocals, *forward, *backward, partial, low, high, *received),
         10**9,
     )
     returned = exchange(out_low, out_high, "dom")
     (out_inner,) = call(
-        inner_backward_body, [layers(6, 31)], 0, [], "inner_backward",
-        (halves, *backward), 3 * 10**8,
-    )
-    return received, (out_low, out_inner, out_high, *returned)
+        inner_backward_body, [layers(6, 31)], 0,
+        [pltpu.VMEM((6, 2, 224, 256), BF16)], "inner_backward",
+        (modes, *backward), 3 * 10**8,
+    )
+    extra = beside(inner, received)
+    if extra is not None:
+        out_inner, extra = lax.optimization_barrier((out_inner, extra))
+    return (out_low, out_inner, out_high, *returned), extra
 
 
 def fold(count, place, outflow, parts):
@@ -805,9 +963,7 @@
 
 
 def shards(start, source, coefficients, outflow):
-    own_table, side_table, plane_weights = [
-        jnp.asarray(t) for t in (OPERATOR_OWN, OPERATOR_SIDE, PLANE_WEIGHTS)
-    ]
+    table = jnp.asarray(OPERATOR)
     place = jnp.stack(
         [
             lax.axis_index("dom"),
@@ -816,48 +972,66 @@
             lax.axis_size("inner"),
         ]
     ).astype(jnp.int32)
-    from_low, from_high = exchange(*pack_first(start, source, coefficients, outflow), "inner")
-    (own_image,) = call(
-        own_image_body, [layers(8, 31)], 0, [plane_scratch()], "own_image",
-        (coefficients, start, own_table, plane_weights), 3 * 10**8,
+    to_low, to_high, coefficients = pack_first(start, source, coefficients, outflow)
+    start, source, to_low, to_high = lax.optimization_barrier((start, source, to_low, to_high))
+    from_low, from_high = exchange(to_low, to_high, "inner")
+    own_image, source_part = call(
+        own_image_body, [layers(8, 31), layers(8, 31)], 1, [plane_scratch()], "own_image",
+        (place, coefficients, start, source, table), 3 * 10**8,
     )
     (reciprocals,) = call(
         reciprocal_body, [modes_shape(10, 112, F32)], 0, [], "reciprocals",
         (coefficients, *[jnp.asarray(t) for t in VALUES]), 10**8,
     )
-    source_part, *parts = call(
-        first_join_body,
-        [layers(8, 31), layers(2, 31), layers(6, 31), layers(2, 31)],
-        2,
-        [plane_scratch(), pltpu.VMEM((8, 16, 8, 128), F32), pltpu.VMEM((8, 31, 8, 128), F32)],
-        "first_join",
-        (
-            place, outflow, start, source, coefficients, from_low, from_high, side_table,
-            plane_weights, own_image,
-        ),
-        10**8,
-    )
-    received, solved = solve(place, reciprocals, parts)
+    joined = (
+        place, outflow, start, from_low, from_high, table, own_image,
+        source_part,
+    )
+    join_scratch = [
+        plane_scratch(), pltpu.VMEM((8, 16, 8, 128), F32), pltpu.VMEM((8, 31, 8, 128), F32)
+    ]
+    low, high = call(
+        functools.partial(first_join_body, EDGES), [layers(2, 31), layers(2, 31)], 2,
+        join_scratch, "first_edges", joined, 10**8,
+    )
+
+    def first_inner_body(*refs):
+        count = len(joined)
+        parts, (inner, *scratch) = refs[: count + 2], refs[count + 2 :]
+        first_join_body(INNER, *parts, inner, *scratch)
+
+    def first_inner():
+        return call(
+            first_inner_body, [layers(6, 31)], 2, join_scratch, "first_inner",
+            (*joined, low, high), 10**8,
+        )[0]
+
+    solved, _ = solve(place, reciprocals, (low, high), first_inner, lambda *_: None)
     news = exchange(*fold(9, place, outflow, solved), "inner")
     field, middle_image = call(
         update_body, [layers(8, 31), layers(8, 15)], 2, [plane_scratch()], "update",
-        (place, outflow, start, coefficients, own_table, plane_weights, *solved), 2 * 10**8,
-    )
-    changed, *parts = call(
-        second_join_body,
-        [layers(8, 4), layers(2, 31), layers(6, 31), layers(2, 31)],
-        2,
-        [plane_scratch(), pltpu.VMEM((8, 30, 8, 128), F32), pltpu.VMEM((8, 31, 8, 128), F32)],
-        "second_join",
-        (
-            place, outflow, coefficients, from_low, from_high, own_table, side_table,
-            plane_weights, field, middle_image, source_part, *news,
-        ),
-        2 * 10**8,
-    )
-    received, solved = solve(place, reciprocals, parts)
-    (residual,) = call(
-        residual_body, [layers(8, 32)], 1, [], "residual", (place, *parts, *received), 10**7,
+        (place, outflow, start, coefficients, table, *solved), 2 * 10**8,
+    )
+    operands = (
+        place, outflow, coefficients, from_low, from_high, table
+    )
+    join_scratch = [plane_scratch(), pltpu.VMEM((8, 31, 8, 128), F32)]
+    changed, rows, low, high = call(
+        second_edges_body,
+        [layers(8, 4), layers(8, 30), layers(2, 31), layers(2, 31)],
+        2, join_scratch, "second_edges",
+        (*operands, field, middle_image, source_part, *news), 2 * 10**8,
+    )
+
+    def second_inner():
+        return call(
+            second_inner_body, [layers(6, 31)], 2, join_scratch, "second_inner",
+            (*operands, rows, middle_image, source_part, low, high), 2 * 10**8,
+        )[0]
+
+    solved, residual = solve(
+        place, reciprocals, (low, high), second_inner,
+        lambda inner, received: residual_out(place, low, inner, high, received),
     )
     news = exchange(*fold(2, place, outflow, solved), "inner")
     (iterate,) = call(

time: 94.7 us -> 84.9 us (0.90)
  the two profiles are of different devices: /device:TPU:0 before, /device:TPU:1 now
where the time goes in v1:
time: 84.9 us; the launch traced here: 84.7 us
  Pallas kernels  37.6 us (44%)
  starting transfers between devices  27.8 us (33%)
  waiting for transfers between devices  16.6 us (20%)
  local copies, waits for them, and re-layouts  1.64 us (2%)
  between operations  0.92 us (1%)
    pallas_call x16, Pallas kernels, call(): pl.pallas_call(body, out_shape=tuple(outs), in_specs=[whole(pltpu.SMEM if...  29.2 us
    ppermute x7, starting transfers between devices, exchange(): lax.ppermute(to_low, axis, downward)  19.1 us
    ppermute x7, waiting for transfers between devices, exchange(): lax.ppermute(to_high, axis, upward)  9.49 us
    ppermute x7, starting transfers between devices, exchange(): lax.ppermute(to_high, axis, upward)  8.79 us
    ppermute x7, waiting for transfers between devices, exchange(): lax.ppermute(to_low, axis, downward)  7.09 us
    pallas_call x1, Pallas kernels, residual_out(): pl.pallas_call(residual_body, out_shape=layers(8, 32), in_specs=[whole(pl...  4.05 us
    pallas_call x1, Pallas kernels, pack_first(): pl.pallas_call(pack_body, out_shape=(layers(8, 9), layers(8, 9), jax.Shap...  2.79 us
  transfers between devices with their start and end apart: 14, of which 8 were waited for; matrix products, arithmetic and copies ran while one was open for 0% of the time, Pallas kernels for 26%

profile of v1, /device:TPU:1, one launch (start us, length us, event | category | flops | bytes accessed | tf_op | source)
XLA Modules:
  0.0 84.7 jit_solution(8370893949302151934)
XLA Ops:
  0.7 2.8 %pack_first.1 = (f32[8,9,8,128]{3,2,1,0:T(8,128)}, f32[8,9,8,128]{3,2,1,0:T(8,128)}, f32[3,1,4,128]{3,2,1,0:T(4,128)}) custom-call(s32[8,32]{1,0:T(8,128)} %outflow.17, f32[8,32,8,128]{3,2,1,0:T(8,128)} %start.4, f32[8,32,8,128]{3,2,1,0:T(8,128)} %source.2, f32[3,1,4,128]{3,2,1,0:T(4,128)} %coefficients.1), custom_call_target="tpu_custom_call" | custom-call | tf_op jit(solution)/shard_map/pack_first/pallas_call | solution.py:270
  3.5 2.6 %collective-permute-start = (f32[8,9,8,128]{3,2,1,0:T(8,128)}, f32[8,9,8,128]{3,2,1,0:T(8,128)S(1)}, u32[]{:S(2)}, u32[]{:S(2)}) collective-permute-start(f32[8,9,8,128]{3,2,1,0:T(8,128)} %get-tuple-element.35), channel_id=1, source_target_pairs={{0,1},{1,2},{2,3},{3,4},{4,5},{5,6},{6,7},{7,0},{8,9},{9,10},{10,1... | collective-permute-start | bytes 884744 | tf_op jit(solution)/shard_map/ppermute | solution.py:915
  7.7 2.9 %own_image.1 = (f32[8,31,8,128]{3,2,1,0:T(8,128)S(1)}, f32[8,31,8,128]{3,2,1,0:T(8,128)S(1)}) custom-call(s32[4]{0:T(128)S(1)} %pad_add_fusion.place.refs_0_, f32[3,1,4,128]{3,2,1,0:T(4,128)S(1)} %copy-done.9, f32[8,32,8,128]{3,2,1,0:T(8,128)S(1)} %copy-done, f32[8,32,8,128]{3,2,1,0:T(8,128)S(1)} %copy-done.1, bf16[192,192]{1,0:T(8,128)(2,1)S(1)} %copy-done.2), custom_call_target="tpu_custom_call" | custom-call | flops 300000000 | bytes 4282384 | tf_op jit(solution)/shard_map/own_image/pallas_call | solution.py:224
  15.5 4.6 %collective-permute-start.3 = (f32[2,31,8,128]{3,2,1,0:T(8,128)S(1)}, f32[2,31,8,128]{3,2,1,0:T(8,128)S(1)}, u32[]{:S(2)}, u32[]{:S(2)}) collective-permute-start(f32[2,31,8,128]{3,2,1,0:T(8,128)S(1)} %get-tuple-element.40.refs_8_.low), channel_id=1, source_target_pairs={{8,0},{16,8},{24,16},{32,24},{40,32},{48,40},{56,48},{64,56},{72,6... | collective-permute-start | bytes 761864 | tf_op jit(solution)/shard_map/ppermute | solution.py:915
  22.1 1.9 %inner_forward.2.partial = f32[10,2,112,256]{3,2,1,0:T(8,128)S(1)} custom-call(f32[6,31,8,128]{3,2,1,0:T(8,128)S(1)} %first_inner.1.inner, bf16[112,160]{1,0:T(8,128)(2,1)S(1)} %copy-done.5, bf16[112,160]{1,0:T(8,128)(2,1)S(1)} %copy-done.6), custom_call_target="tpu_custom_call" | custom-call | flops 300000000 | bytes 3198976 | tf_op jit(solution)/shard_map/inner_forward/pallas_call | solution.py:224
  24.0 2.5 %collective-permute-done.2.from_low = f32[2,31,8,128]{3,2,1,0:T(8,128)S(1)} collective-permute-done((f32[2,31,8,128]{3,2,1,0:T(8,128)S(1)}, f32[2,31,8,128]{3,2,1,0:T(8,128)S(1)}, u32[]{:S(2)}, u32[]{:S(2)}) %collective-permute-start.2) | collective-permute-done | bytes 253984 | tf_op jit(solution)/shard_map/ppermute | solution.py:915
  26.5 3.3 %edge_solve.2 = (f32[2,31,8,128]{3,2,1,0:T(8,128)S(1)}, f32[2,31,8,128]{3,2,1,0:T(8,128)S(1)}, f32[10,2,112,256]{3,2,1,0:T(8,128)S(1)}) custom-call(s32[4]{0:T(128)S(1)} %pad_add_fusion.place.refs_0_, f32[10,2,112,256]{3,2,1,0:T(8,128)S(1)} %reciprocals.1, bf16[112,160]{1,0:T(8,128)(2,1)S(1)} %copy-done.5, bf16[112,160]{1,0:T(8,128)(2,1)S(1)} %copy-done.6, ...), custom_call_target="tpu_custom_call" | custom-call | flops 1000000000 | bytes 8763408 | tf_op jit(solution)/shard_map/edge_solve/pallas_call | solution.py:224
  29.9 4.8 %collective-permute-start.5 = (f32[2,31,8,128]{3,2,1,0:T(8,128)S(1)}, f32[2,31,8,128]{3,2,1,0:T(8,128)S(1)}, u32[]{:S(2)}, u32[]{:S(2)}) collective-permute-start(f32[2,31,8,128]{3,2,1,0:T(8,128)S(1)} %get-tuple-element.42.low), channel_id=1, source_target_pairs={{8,0},{16,8},{24,16},{32,24},{40,32},{48,40},{56,48},{64,56},{72,6... | collective-permute-start | bytes 761864 | tf_op jit(solution)/shard_map/ppermute | solution.py:915
  34.6 2.1 %inner_backward.2.inner = f32[6,31,8,128]{3,2,1,0:T(8,128)S(1)} custom-call(f32[10,2,112,256]{3,2,1,0:T(8,128)S(1)} %get-tuple-element.43.modes, bf16[160,224]{1,0:T(8,128)(2,1)S(1)} %copy-done.4, bf16[160,112]{1,0:T(8,128)(2,1)S(1)} %copy-done.7), custom_call_target="tpu_custom_call" | custom-call | flops 300000000 | bytes 3270656 | tf_op jit(solution)/shard_map/inner_backward/pallas_call | solution.py:224
  36.7 3.4 %collective-permute-done.4.from_low = f32[2,31,8,128]{3,2,1,0:T(8,128)S(1)} collective-permute-done((f32[2,31,8,128]{3,2,1,0:T(8,128)S(1)}, f32[2,31,8,128]{3,2,1,0:T(8,128)S(1)}, u32[]{:S(2)}, u32[]{:S(2)}) %collective-permute-start.4) | collective-permute-done | bytes 253984 | tf_op jit(solution)/shard_map/ppermute | solution.py:915
  40.8 2.2 %collective-permute-start.6 = (f32[8,9,8,128]{3,2,1,0:T(8,128)S(1)}, f32[8,9,8,128]{3,2,1,0:T(8,128)S(1)}, u32[]{:S(2)}, u32[]{:S(2)}) collective-permute-start(f32[8,9,8,128]{3,2,1,0:T(8,128)S(1)} %get-tuple-element.47), channel_id=1, source_target_pairs={{0,1},{1,2},{2,3},{3,4},{4,5},{5,6},{6,7},{7,0},{8,9},{9,10},{10,1... | collective-permute-start | bytes 884744 | tf_op jit(solution)/shard_map/ppermute | solution.py:915
  43.0 2.4 %update.1 = (f32[8,31,8,128]{3,2,1,0:T(8,128)S(1)}, f32[8,15,8,128]{3,2,1,0:T(8,128)S(1)}) custom-call(s32[4]{0:T(128)S(1)} %pad_add_fusion.place.refs_0_, s32[8,32]{1,0:T(8,128)S(1)} %copy-done.8, f32[8,32,8,128]{3,2,1,0:T(8,128)S(1)} %copy-done, f32[3,1,4,128]{3,2,1,0:T(4,128)S(1)} %copy-done.10, bf16[192,192]{1,0:T(8,128)(2,1)S(1)} %copy-done.3, ...), custom_call_target="tpu_custom_call" | custom-call | flops 200000000 | bytes 4488208 | tf_op jit(solution)/shard_map/update/pallas_call | solution.py:224
  46.7 2.7 %collective-permute-done.7.high_news = f32[8,9,8,128]{3,2,1,0:T(8,128)S(1)} collective-permute-done((f32[8,9,8,128]{3,2,1,0:T(8,128)S(1)}, f32[8,9,8,128]{3,2,1,0:T(8,128)S(1)}, u32[]{:S(2)}, u32[]{:S(2)}) %collective-permute-start.7) | collective-permute-done | bytes 294944 | tf_op jit(solution)/shard_map/ppermute | solution.py:915
  49.4 2.1 %second_edges.1 = (f32[8,4,8,128]{3,2,1,0:T(8,128)S(1)}, f32[8,30,8,128]{3,2,1,0:T(8,128)S(1)}, f32[2,31,8,128]{3,2,1,0:T(8,128)S(1)}, f32[2,31,8,128]{3,2,1,0:T(8,128)S(1)}) custom-call(s32[4]{0:T(128)S(1)} %pad_add_fusion.place.refs_0_, s32[8,32]{1,0:T(8,128)S(1)} %copy-done.8, f32[3,1,4,128]{3,2,1,0:T(4,128)S(1)} %copy-done.10, ...), custom_call_target="tpu_custom_call" | custom-call | flops 200000000 | bytes 5479440 | tf_op jit(solution)/shard_map/second_edges/pallas_call | solution.py:224
  51.5 4.9 %collective-permute-start.9 = (f32[2,31,8,128]{3,2,1,0:T(8,128)S(1)}, f32[2,31,8,128]{3,2,1,0:T(8,128)S(1)}, u32[]{:S(2)}, u32[]{:S(2)}) collective-permute-start(f32[2,31,8,128]{3,2,1,0:T(8,128)S(1)} %get-tuple-element.51.low), channel_id=1, source_target_pairs={{8,0},{16,8},{24,16},{32,24},{40,32},{48,40},{56,48},{64,56},{72,6... | collective-permute-start | bytes 761864 | tf_op jit(solution)/shard_map/ppermute | solution.py:915
  56.4 2.0 %second_inner.1.inner = f32[6,31,8,128]{3,2,1,0:T(8,128)S(1)} custom-call(s32[4]{0:T(128)S(1)} %pad_add_fusion.place.refs_0_, s32[8,32]{1,0:T(8,128)S(1)} %copy-done.8, f32[3,1,4,128]{3,2,1,0:T(4,128)S(1)} %copy-done.10, f32[8,9,8,128]{3,2,1,0:T(8,128)S(1)} %collective-permute-done.from_low.refs_3_, ...), custom_call_target="tpu_custom_call" | custom-call | flops 200000000 | bytes 4504592 | tf_op jit(solution)/shard_map/second_inner/pallas_call | solution.py:224
  58.4 1.9 %inner_forward.3.partial = f32[10,2,112,256]{3,2,1,0:T(8,128)S(1)} custom-call(f32[6,31,8,128]{3,2,1,0:T(8,128)S(1)} %second_inner.1.inner, bf16[112,160]{1,0:T(8,128)(2,1)S(1)} %copy-done.5, bf16[112,160]{1,0:T(8,128)(2,1)S(1)} %copy-done.6), custom_call_target="tpu_custom_call" | custom-call | flops 300000000 | bytes 3198976 | tf_op jit(solution)/shard_map/inner_forward/pallas_call | solution.py:224
  60.3 1.9 %collective-permute-done.8.from_low = f32[2,31,8,128]{3,2,1,0:T(8,128)S(1)} collective-permute-done((f32[2,31,8,128]{3,2,1,0:T(8,128)S(1)}, f32[2,31,8,128]{3,2,1,0:T(8,128)S(1)}, u32[]{:S(2)}, u32[]{:S(2)}) %collective-permute-start.8) | collective-permute-done | bytes 253984 | tf_op jit(solution)/shard_map/ppermute | solution.py:915
  62.2 3.3 %edge_solve.3 = (f32[2,31,8,128]{3,2,1,0:T(8,128)S(1)}, f32[2,31,8,128]{3,2,1,0:T(8,128)S(1)}, f32[10,2,112,256]{3,2,1,0:T(8,128)S(1)}) custom-call(s32[4]{0:T(128)S(1)} %pad_add_fusion.place.refs_0_, f32[10,2,112,256]{3,2,1,0:T(8,128)S(1)} %reciprocals.1, bf16[112,160]{1,0:T(8,128)(2,1)S(1)} %copy-done.5, bf16[112,160]{1,0:T(8,128)(2,1)S(1)} %copy-done.6, ...), custom_call_target="tpu_custom_call" | custom-call | flops 1000000000 | bytes 8763408 | tf_op jit(solution)/shard_map/edge_solve/pallas_call | solution.py:224
  65.5 4.8 %collective-permute-start.11 = (f32[2,31,8,128]{3,2,1,0:T(8,128)S(1)}, f32[2,31,8,128]{3,2,1,0:T(8,128)S(1)}, u32[]{:S(2)}, u32[]{:S(2)}) collective-permute-start(f32[2,31,8,128]{3,2,1,0:T(8,128)S(1)} %get-tuple-element.53.low), channel_id=1, source_target_pairs={{8,0},{16,8},{24,16},{32,24},{40,32},{48,40},{56,48},{64,56},{72,6... | collective-permute-start | bytes 761864 | tf_op jit(solution)/shard_map/ppermute | solution.py:915
  70.3 4.0 %residual.1 = f32[8,32,8,128]{3,2,1,0:T(8,128)} custom-call(s32[4]{0:T(128)S(1)} %pad_add_fusion.place.refs_0_, f32[2,31,8,128]{3,2,1,0:T(8,128)S(1)} %get-tuple-element.51.low, f32[6,31,8,128]{3,2,1,0:T(8,128)S(1)} %second_inner.1.inner, f32[2,31,8,128]{3,2,1,0:T(8,128)S(1)} %get-tuple-element.52.high, ...), custom_call_target="tpu_custom_call" | custom-call | flops 10000000 | bytes 4194304 | tf_op jit(solution)/shard_map/residual/pallas_call | solution.py:717
  74.3 2.1 %inner_backward.3.inner = f32[6,31,8,128]{3,2,1,0:T(8,128)S(1)} custom-call(f32[10,2,112,256]{3,2,1,0:T(8,128)S(1)} %get-tuple-element.54.modes, bf16[160,224]{1,0:T(8,128)(2,1)S(1)} %copy-done.4, bf16[160,112]{1,0:T(8,128)(2,1)S(1)} %copy-done.7), custom_call_target="tpu_custom_call" | custom-call | flops 300000000 | bytes 3270656 | tf_op jit(solution)/shard_map/inner_backward/pallas_call | solution.py:224
  77.1 2.0 %collective-permute-start.12 = (f32[8,2,8,128]{3,2,1,0:T(8,128)S(1)}, f32[8,2,8,128]{3,2,1,0:T(8,128)S(1)}, u32[]{:S(2)}, u32[]{:S(2)}) collective-permute-start(f32[8,2,8,128]{3,2,1,0:T(8,128)S(1)} %get-tuple-element.57), channel_id=1, source_target_pairs={{0,1},{1,2},{2,3},{3,4},{4,5},{5,6},{6,7},{7,0},{8,9},{9,10},{10,1... | collective-permute-start | bytes 196616 | tf_op jit(solution)/shard_map/ppermute | solution.py:915
  80.4 2.7 %collective-permute-done.13.high_news = f32[8,2,8,128]{3,2,1,0:T(8,128)S(1)} collective-permute-done((f32[8,2,8,128]{3,2,1,0:T(8,128)S(1)}, f32[8,2,8,128]{3,2,1,0:T(8,128)S(1)}, u32[]{:S(2)}, u32[]{:S(2)}) %collective-permute-start.13) | collective-permute-done | bytes 65568 | tf_op jit(solution)/shard_map/ppermute | solution.py:915
  (50 shorter events, 14.0 us)
Async XLA Ops:
  0.6 11.8 %copy-start.8 = (s32[8,32]{1,0:T(8,128)S(1)}, s32[8,32]{1,0:T(8,128)}, u32[]{:S(2)}) copy-start(s32[8,32]{1,0:T(8,128)} %outflow.17) | copy-start | bytes 3076
  0.6 5.5 %copy-start = (f32[8,32,8,128]{3,2,1,0:T(8,128)S(1)}, f32[8,32,8,128]{3,2,1,0:T(8,128)}, u32[]{:S(2)}) copy-start(f32[8,32,8,128]{3,2,1,0:T(8,128)} %start.4) | copy-start | bytes 3145732
  0.7 5.5 %copy-start.1 = (f32[8,32,8,128]{3,2,1,0:T(8,128)S(1)}, f32[8,32,8,128]{3,2,1,0:T(8,128)}, u32[]{:S(2)}) copy-start(f32[8,32,8,128]{3,2,1,0:T(8,128)} %source.2) | copy-start | bytes 3145732
  3.5 7.2 %collective-permute-start = (f32[8,9,8,128]{3,2,1,0:T(8,128)}, f32[8,9,8,128]{3,2,1,0:T(8,128)S(1)}, u32[]{:S(2)}, u32[]{:S(2)}) collective-permute-start(f32[8,9,8,128]{3,2,1,0:T(8,128)} %get-tuple-element.35), channel_id=1, source_target_pairs={{0,1},{1,2},{2,3},{3,4},{4,5},{5,6},{6,7},{7,0},{8,9},{9,10},{10,1... | collective-permute-start | bytes 884744 | tf_op jit(solution)/shard_map/ppermute | solution.py:915
  6.1 6.4 %collective-permute-start.1 = (f32[8,9,8,128]{3,2,1,0:T(8,128)}, f32[8,9,8,128]{3,2,1,0:T(8,128)S(1)}, u32[]{:S(2)}, u32[]{:S(2)}) collective-permute-start(f32[8,9,8,128]{3,2,1,0:T(8,128)} %get-tuple-element.36), channel_id=1, source_target_pairs={{1,0},{2,1},{3,2},{4,3},{5,4},{6,5},{7,6},{0,7},{9,8},{10,9},{11,1... | collective-permute-start | bytes 884744 | tf_op jit(solution)/shard_map/ppermute | solution.py:915
  10.7 9.5 %copy-start.11 = (f32[112,128]{1,0:T(8,128)S(1)}, f32[112,128]{1,0:T(8,128)}, u32[]{:S(2)}) copy-start(f32[112,128]{1,0:T(8,128)} %constant.28.clone.second_values) | copy-start | bytes 172036
  10.7 9.5 %copy-start.12 = (f32[112,128]{1,0:T(8,128)S(1)}, f32[112,128]{1,0:T(8,128)}, u32[]{:S(2)}) copy-start(f32[112,128]{1,0:T(8,128)} %constant.29.clone.third_values) | copy-start | bytes 172036
  13.8 12.6 %collective-permute-start.2 = (f32[2,31,8,128]{3,2,1,0:T(8,128)S(1)}, f32[2,31,8,128]{3,2,1,0:T(8,128)S(1)}, u32[]{:S(2)}, u32[]{:S(2)}) collective-permute-start(f32[2,31,8,128]{3,2,1,0:T(8,128)S(1)} %get-tuple-element.41.refs_9_.high), channel_id=1, source_target_pairs={{0,8},{8,16},{16,24},{24,32},{32,40},{40,48},{48,56},{56,64},{64,7... | collective-permute-start | bytes 761864 | tf_op jit(solution)/shard_map/ppermute | solution.py:915
  15.5 10.9 %collective-permute-start.3 = (f32[2,31,8,128]{3,2,1,0:T(8,128)S(1)}, f32[2,31,8,128]{3,2,1,0:T(8,128)S(1)}, u32[]{:S(2)}, u32[]{:S(2)}) collective-permute-start(f32[2,31,8,128]{3,2,1,0:T(8,128)S(1)} %get-tuple-element.40.refs_8_.low), channel_id=1, source_target_pairs={{8,0},{16,8},{24,16},{32,24},{40,32},{48,40},{56,48},{64,56},{72,6... | collective-permute-start | bytes 761864 | tf_op jit(solution)/shard_map/ppermute | solution.py:915
  20.6 1.5 %copy-start.5 = (bf16[112,160]{1,0:T(8,128)(2,1)S(1)}, bf16[112,160]{1,0:T(8,128)(2,1)}, u32[]{:S(2)}) copy-start(bf16[112,160]{1,0:T(8,128)(2,1)} %constant.30.clone.forward_high) | copy-start | bytes 107524
  22.1 4.4 %copy-start.4 = (bf16[160,224]{1,0:T(8,128)(2,1)S(1)}, bf16[160,224]{1,0:T(8,128)(2,1)}, u32[]{:S(2)}) copy-start(bf16[160,224]{1,0:T(8,128)(2,1)} %constant.32.clone.backward) | copy-start | bytes 215044
  22.1 4.4 %copy-start.7 = (bf16[160,112]{1,0:T(8,128)(2,1)S(1)}, bf16[160,112]{1,0:T(8,128)(2,1)}, u32[]{:S(2)}) copy-start(bf16[160,112]{1,0:T(8,128)(2,1)} %constant.33.clone.backward_low) | copy-start | bytes 107524
  29.8 10.3 %collective-permute-start.4 = (f32[2,31,8,128]{3,2,1,0:T(8,128)S(1)}, f32[2,31,8,128]{3,2,1,0:T(8,128)S(1)}, u32[]{:S(2)}, u32[]{:S(2)}) collective-permute-start(f32[2,31,8,128]{3,2,1,0:T(8,128)S(1)} %get-tuple-element.44.high), channel_id=1, source_target_pairs={{0,8},{8,16},{16,24},{24,32},{32,40},{40,48},{48,56},{56,64},{64,7... | collective-permute-start | bytes 761864 | tf_op jit(solution)/shard_map/ppermute | solution.py:915
  29.9 10.3 %collective-permute-start.5 = (f32[2,31,8,128]{3,2,1,0:T(8,128)S(1)}, f32[2,31,8,128]{3,2,1,0:T(8,128)S(1)}, u32[]{:S(2)}, u32[]{:S(2)}) collective-permute-start(f32[2,31,8,128]{3,2,1,0:T(8,128)S(1)} %get-tuple-element.42.low), channel_id=1, source_target_pairs={{8,0},{16,8},{24,16},{32,24},{40,32},{48,40},{56,48},{64,56},{72,6... | collective-permute-start | bytes 761864 | tf_op jit(solution)/shard_map/ppermute | solution.py:915
  34.6 8.4 %copy-start.3 = (bf16[192,192]{1,0:T(8,128)(2,1)S(1)}, bf16[192,192]{1,0:T(8,128)(2,1)}, u32[]{:S(2)}) copy-start(bf16[192,192]{1,0:T(8,128)(2,1)} %constant.27.clone.table.refs_5_) | copy-start | bytes 221188
  34.6 8.4 %copy-start.10 = (f32[3,1,4,128]{3,2,1,0:T(4,128)S(1)}, f32[3,1,4,128]{3,2,1,0:T(4,128)}, u32[]{:S(2)}) copy-start(f32[3,1,4,128]{3,2,1,0:T(4,128)} %get-tuple-element.34.coefficients) | copy-start | bytes 18436
  40.8 5.9 %collective-permute-start.6 = (f32[8,9,8,128]{3,2,1,0:T(8,128)S(1)}, f32[8,9,8,128]{3,2,1,0:T(8,128)S(1)}, u32[]{:S(2)}, u32[]{:S(2)}) collective-permute-start(f32[8,9,8,128]{3,2,1,0:T(8,128)S(1)} %get-tuple-element.47), channel_id=1, source_target_pairs={{0,1},{1,2},{2,3},{3,4},{4,5},{5,6},{6,7},{7,0},{8,9},{9,10},{10,1... | collective-permute-start | bytes 884744 | tf_op jit(solution)/shard_map/ppermute | solution.py:915
  43.0 6.4 %collective-permute-start.7 = (f32[8,9,8,128]{3,2,1,0:T(8,128)S(1)}, f32[8,9,8,128]{3,2,1,0:T(8,128)S(1)}, u32[]{:S(2)}, u32[]{:S(2)}) collective-permute-start(f32[8,9,8,128]{3,2,1,0:T(8,128)S(1)} %get-tuple-element.48), channel_id=1, source_target_pairs={{1,0},{2,1},{3,2},{4,3},{5,4},{6,5},{7,6},{0,7},{9,8},{10,9},{11,1... | collective-permute-start | bytes 884744 | tf_op jit(solution)/shard_map/ppermute | solution.py:915
  51.5 10.7 %collective-permute-start.8 = (f32[2,31,8,128]{3,2,1,0:T(8,128)S(1)}, f32[2,31,8,128]{3,2,1,0:T(8,128)S(1)}, u32[]{:S(2)}, u32[]{:S(2)}) collective-permute-start(f32[2,31,8,128]{3,2,1,0:T(8,128)S(1)} %get-tuple-element.52.high), channel_id=1, source_target_pairs={{0,8},{8,16},{16,24},{24,32},{32,40},{40,48},{48,56},{56,64},{64,7... | collective-permute-start | bytes 761864 | tf_op jit(solution)/shard_map/ppermute | solution.py:915
  51.5 10.6 %collective-permute-start.9 = (f32[2,31,8,128]{3,2,1,0:T(8,128)S(1)}, f32[2,31,8,128]{3,2,1,0:T(8,128)S(1)}, u32[]{:S(2)}, u32[]{:S(2)}) collective-permute-start(f32[2,31,8,128]{3,2,1,0:T(8,128)S(1)} %get-tuple-element.51.low), channel_id=1, source_target_pairs={{8,0},{16,8},{24,16},{32,24},{40,32},{48,40},{56,48},{64,56},{72,6... | collective-permute-start | bytes 761864 | tf_op jit(solution)/shard_map/ppermute | solution.py:915
  65.4 11.0 %collective-permute-start.10 = (f32[2,31,8,128]{3,2,1,0:T(8,128)S(1)}, f32[2,31,8,128]{3,2,1,0:T(8,128)S(1)}, u32[]{:S(2)}, u32[]{:S(2)}) collective-permute-start(f32[2,31,8,128]{3,2,1,0:T(8,128)S(1)} %get-tuple-element.56.high), channel_id=1, source_target_pairs={{0,8},{8,16},{16,24},{24,32},{32,40},{40,48},{48,56},{56,64},{64,7... | collective-permute-start | bytes 761864 | tf_op jit(solution)/shard_map/ppermute | solution.py:915
  65.5 10.9 %collective-permute-start.11 = (f32[2,31,8,128]{3,2,1,0:T(8,128)S(1)}, f32[2,31,8,128]{3,2,1,0:T(8,128)S(1)}, u32[]{:S(2)}, u32[]{:S(2)}) collective-permute-start(f32[2,31,8,128]{3,2,1,0:T(8,128)S(1)} %get-tuple-element.53.low), channel_id=1, source_target_pairs={{8,0},{16,8},{24,16},{32,24},{40,32},{48,40},{56,48},{64,56},{72,6... | collective-permute-start | bytes 761864 | tf_op jit(solution)/shard_map/ppermute | solution.py:915
  77.1 3.4 %collective-permute-start.12 = (f32[8,2,8,128]{3,2,1,0:T(8,128)S(1)}, f32[8,2,8,128]{3,2,1,0:T(8,128)S(1)}, u32[]{:S(2)}, u32[]{:S(2)}) collective-permute-start(f32[8,2,8,128]{3,2,1,0:T(8,128)S(1)} %get-tuple-element.57), channel_id=1, source_target_pairs={{0,1},{1,2},{2,3},{3,4},{4,5},{5,6},{6,7},{7,0},{8,9},{9,10},{10,1... | collective-permute-start | bytes 196616 | tf_op jit(solution)/shard_map/ppermute | solution.py:915
  79.1 4.0 %collective-permute-start.13 = (f32[8,2,8,128]{3,2,1,0:T(8,128)S(1)}, f32[8,2,8,128]{3,2,1,0:T(8,128)S(1)}, u32[]{:S(2)}, u32[]{:S(2)}) collective-permute-start(f32[8,2,8,128]{3,2,1,0:T(8,128)S(1)} %get-tuple-element.58), channel_id=1, source_target_pairs={{1,0},{2,1},{3,2},{4,3},{5,4},{6,5},{7,6},{0,7},{9,8},{10,9},{11,1... | collective-permute-start | bytes 196616 | tf_op jit(solution)/shard_map/ppermute | solution.py:915
  (3 other events, 3.1 us)

commit v2 on v1

--- a/solution.py
+++ b/solution.py
@@ -173,6 +173,38 @@
     )
 
 
+def odd_core(place):
+    return place[2] % 2
+
+
+class Arrived:
+    def __init__(self, even, odd, odd_here, flag):
+        self.even, self.odd = even, odd
+        self.odd_factor = flag * odd_here
+        self.even_factor = flag * (1.0 - odd_here)
+
+    def __getitem__(self, index):
+        return self.even[index] * self.even_factor + self.odd[index] * self.odd_factor
+
+
+def arrived(place, first, second):
+    below, above = ends(place, 0)
+    odd_here = jnp.where(odd_core(place) == 1, 1.0, 0.0)
+    return Arrived(first, second, odd_here, below), Arrived(second, first, odd_here, above)
+
+
+def hand_over(place, low, high, first, second):
+    @pl.when(odd_core(place) == 0)
+    def _():
+        first[...] = high[...]
+        second[...] = low[...]
+
+    @pl.when(odd_core(place) == 1)
+    def _():
+        first[...] = low[...]
+        second[...] = high[...]
+
+
 def top_flags():
     return ((lane_ids() == 127) & (row_ids() == 7)).astype(F32)
 
@@ -235,33 +267,39 @@
     )(*args)
 
 
-def pack_body(
-    outflow, start, source, coefficients, low, high, gains, semaphores
-):
+def pack_body(outflow, start, source, coefficients, low, high, flags, gains, stages, semaphores):
     sides = ((low, 1, 1, 0), (high, 24, 30, 3))
-    copies = [pltpu.make_async_copy(coefficients, gains, semaphores.at[0])]
-    for n, (target, first, node, element) in enumerate(sides):
-        copies.append(
-            pltpu.make_async_copy(
-                start.at[:, first : first + 7], target.at[:, 0:7], semaphores.at[1 + 2 * n]
+    rows_in = []
+    for n, (_, first, node, _) in enumerate(sides):
+        for piece, at, count, to in ((start, first, 7, 0), (source, node, 1, 7)):
+            rows_in.append(
+                pltpu.make_async_copy(
+                    piece.at[:, at : at + count], stages.at[n, :, to : to + count],
+                    semaphores.at[len(rows_in)],
+                )
             )
-        )
-        copies.append(
-            pltpu.make_async_copy(
-                source.at[:, node : node + 1], target.at[:, 7:8], semaphores.at[2 + 2 * n]
-            )
-        )
-    for copy in copies:
+    facts = [
+        pltpu.make_async_copy(coefficients, gains, semaphores.at[4]),
+        pltpu.make_async_copy(outflow, flags, semaphores.at[5]),
+    ]
+    for copy in facts + rows_in:
         copy.start()
-    copies[0].wait()
+    for copy in facts:
+        copy.wait()
     top = top_flags()
     rows = row_ids()
-    for target, first, node, element in sides:
+    for n, (_, _, node, element) in enumerate(sides):
         rows_of = [spread_row(gains[c, 0, element : element + 1, :]) for c in range(3)]
         gain = jnp.where(rows == 0, rows_of[0], jnp.where(rows == 1, rows_of[1], rows_of[2]))
         for i in range(8):
-            target[i, 8] = jnp.where(rows == 7, own_keep(outflow, top, i, node), gain)
-    for copy in copies[1:]:
+            stages[n, i, 8] = jnp.where(rows == 7, own_keep(flags, top, i, node), gain)
+    rows_out = []
+    for n, (target, _, _, _) in enumerate(sides):
+        rows_in[2 * n].wait()
+        rows_in[2 * n + 1].wait()
+        rows_out.append(pltpu.make_async_copy(stages.at[n], target, semaphores.at[6 + n]))
+        rows_out[-1].start()
+    for copy in rows_out:
         copy.wait()
 
 
@@ -269,10 +307,15 @@
     anywhere = whole(pltpu.HBM)
     return pl.pallas_call(
         pack_body,
-        out_shape=(layers(8, 9), layers(8, 9), jax.ShapeDtypeStruct(coefficients.shape, F32)),
-        in_specs=[whole(pltpu.SMEM), anywhere, anywhere, anywhere],
-        out_specs=(whole(), whole(), whole()),
-        scratch_shapes=[pltpu.SemaphoreType.DMA((5,))],
+        out_shape=(layers(8, 9), layers(8, 9)),
+        in_specs=[anywhere, anywhere, anywhere, anywhere],
+        out_specs=(anywhere, anywhere),
+        scratch_shapes=[
+            pltpu.SMEM((8, 32), jnp.int32),
+            pltpu.VMEM((3, 1, 4, 128), F32),
+            pltpu.VMEM((2, 8, 9, 8, 128), F32),
+            pltpu.SemaphoreType.DMA((8,)),
+        ],
         compiler_params=pltpu.CompilerParams(vmem_limit_bytes=PACK_VMEM_BYTES),
         name="pack_first",
     )(outflow, start, source, coefficients)
@@ -449,15 +492,15 @@
 
 
 def own_image_body(
-    place, coefficients, start, source, table, image, source_part, planes
+    wanted, place, coefficients, start, source, table, image, source_part, planes
 ):
     gains = own_gains(coefficients)
     for pair in ((0, 1), (2, 3)):
         own_elements(
             [(e, start, 8 * e, e > 0, False) for e in pair],
-            gains, table, planes, image, 1,
+            gains, table, planes, image, 1, wanted,
         )
-    for i in range(8):
+    for i in wanted:
         share = source_share(place, i)
         source_part[i, 29] = source[i, 31] * share
 
@@ -504,11 +547,13 @@
         field, 0, 8, side_gains(low_flag, from_low), side_gains(high_flag, from_high),
         table, planes, image, wanted,
     )
-    put = put_edges(*outs) if wanted is EDGES else put_inner(*outs)
+    put = put_edges(*outs[:2]) if wanted is EDGES else put_inner(*outs)
     finish_residual(
         wanted, image, source_rows(place, source_part, from_low, from_high), outflow,
         from_low, from_high, put,
     )
+    if wanted is EDGES:
+        hand_over(place, *outs)
 
 
 def forward_layers(source, count, forward_high, forward_low, spectral):
@@ -635,26 +680,22 @@
 
 def edge_solve_body(
     place, reciprocals, forward_high, forward_low, backward, backward_low, partial,
-    low, high, from_low, from_high, out_low, out_high, modes, edges, spectral, halves,
+    low, high, first, second, out_low, out_high, out_first, out_second, spectral, edges, halves,
 ):
-    below, above = ends(place, 0)
+    from_low, from_high = arrived(place, first, second)
 
     def gather(y, carry):
-        edges[0, y] = below * from_low[0, y]
-        edges[1, y] = low[0, y] + below * from_low[1, y]
-        edges[2, y] = high[1, y] + above * from_high[0, y]
-        edges[3, y] = above * from_high[1, y]
+        edges[0, y] = from_low[0, y]
+        edges[1, y] = low[0, y] + from_low[1, y]
+        edges[2, y] = high[1, y] + from_high[0, y]
+        edges[3, y] = from_high[1, y]
         return carry
 
-    lax.fori_loop(0, 31, gather, 0)
+    lax.fori_loop(0, 31, gather, 0, unroll=4)
     forward_layers(edges, 4, forward_high, forward_low, spectral)
 
     def visit(spot):
-        pairs = [(spectral[(n,) + spot()], spectral[(3 - n,) + spot()]) for n in range(2)]
-        values = to_modes(pairs, 0, [partial[(p,) + spot()] for p in range(10)])
-        for p in range(10):
-            values[p] = values[p] * reciprocals[(p,) + spot()]
-            modes[(p,) + spot()] = values[p]
+        values = all_modes(spot, spectral, partial, reciprocals)
         for a in range(2):
             lower, upper = from_modes(values, a)
             store_halves(halves, a, spot, lower)
@@ -662,16 +703,25 @@
 
     over_blocks(visit)
 
-    def back(first, target):
-        backward_layers(halves.at[first : first + 2], 2, backward, backward_low, target)
+    def back(start, target):
+        backward_layers(halves.at[start : start + 2], 2, backward, backward_low, target)
 
     back(0, out_low)
     back(2, out_high)
-
-
-def inner_backward_body(modes, backward, backward_low, out_inner, halves):
+    hand_over(place, out_low, out_high, out_first, out_second)
+
+
+def all_modes(spot, spectral, partial, reciprocals):
+    pairs = [(spectral[(n,) + spot()], spectral[(3 - n,) + spot()]) for n in range(2)]
+    values = to_modes(pairs, 0, [partial[(p,) + spot()] for p in range(10)])
+    return [values[p] * reciprocals[(p,) + spot()] for p in range(10)]
+
+
+def inner_backward_body(
+    spectral, partial, reciprocals, backward, backward_low, out_inner, halves
+):
     def visit(spot):
-        values = [modes[(p,) + spot()] for p in range(10)]
+        values = all_modes(spot, spectral, partial, reciprocals)
         for n in range(3):
             lower, upper = from_modes(values, n + 2)
             store_halves(halves, n, spot, lower)
@@ -681,10 +731,10 @@
     backward_layers(halves, 6, backward, backward_low, out_inner)
 
 
-def residual_body(place, low, inner, high, from_low, from_high, residual, layer, semaphores):
+def residual_body(place, low, inner, high, first, second, residual, layer, semaphores):
     row = row_ids()
     lane = lane_ids()
-    below, above = ends(place, 0)
+    from_low, from_high = arrived(place, first, second)
     into_first = (row == 0) & (lane > 0)
     into_last = (row == 7) & (lane < 127)
     copies = []
@@ -692,9 +742,9 @@
 
         def value_at(y, i=i):
             if i == 0:
-                value = low[0, y] + below * from_low[1, y]
+                value = low[0, y] + from_low[1, y]
             elif i == 7:
-                value = high[1, y] + above * from_high[0, y]
+                value = high[1, y] + from_high[0, y]
             else:
                 value = inner[i - 1, y]
             before = pltpu.roll(pltpu.roll(value, 1, 0), 1, 1)
@@ -726,25 +776,24 @@
     )(place, low, inner, high, *received)
 
 
-def fold_row(ends_flags, i, y, low, inner, high, from_low, from_high):
-    below, above = ends_flags
+def fold_row(i, y, low, inner, high, from_low, from_high):
     if i == 0:
-        return low[1, y] + below * from_low[0, y]
+        return low[1, y] + from_low[0, y]
     if i == 1:
-        return inner[0, y] + below * from_low[1, y]
+        return inner[0, y] + from_low[1, y]
     if i < 6:
         return inner[i - 1, y]
     if i == 6:
-        return inner[5, y] + above * from_high[0, y]
-    return high[0, y] + above * from_high[1, y]
-
-
-def fold_body(count, place, outflow, low, inner, high, from_low, from_high, to_low, to_high):
+        return inner[5, y] + from_high[0, y]
+    return high[0, y] + from_high[1, y]
+
+
+def fold_body(count, place, outflow, low, inner, high, first, second, to_low, to_high):
     top = top_flags()
-    flags = ends(place, 0)
+    parts = (low, inner, high, *arrived(place, first, second))
     for i in range(8):
         for y in (*range(count), *range(31 - count, 31)):
-            value = fold_row(flags, i, y, low, inner, high, from_low, from_high)
+            value = fold_row(i, y, *parts)
             if 3 <= y < 28:
                 value = own_keep(outflow, top, i, column_of(y - 1)) * value
             if y < count:
@@ -755,17 +804,16 @@
 
 def update_body(
     place, outflow, start, coefficients, table, low, inner, high,
-    from_low, from_high, field, image, planes,
+    first, second, field, image, planes,
 ):
     top = top_flags()
-    flags = ends(place, 0)
-    parts = (low, inner, high, from_low, from_high)
+    parts = (low, inner, high, *arrived(place, first, second))
     for i in range(8):
-        field[i, 0] = fold_row(flags, i, 0, *parts)
-        field[i, 30] = fold_row(flags, i, 30, *parts)
+        field[i, 0] = fold_row(i, 0, *parts)
+        field[i, 30] = fold_row(i, 30, *parts)
 
         def row(y, column, i=i):
-            value = own_keep(outflow, top, i, column) * fold_row(flags, i, y, *parts)
+            value = own_keep(outflow, top, i, column) * fold_row(i, y, *parts)
             field[i, y] = start[i, column] + value
 
         row(29, 31)
@@ -833,7 +881,7 @@
 def second_edges_body(
     place, outflow, coefficients, from_low, from_high, table,
     field, middle_image, source_part, low_news, high_news,
-    changed, rows, low, high, planes, image,
+    changed, rows, low, high, first, second, planes, image,
 ):
     second_rows_body(
         place, outflow, from_low, from_high, field, low_news, high_news, rows, changed
@@ -842,6 +890,7 @@
         EDGES, place, outflow, coefficients, from_low, from_high, table,
         rows, middle_image, source_part, planes, image, put_edges(low, high),
     )
+    hand_over(place, low, high, first, second)
 
 
 def second_inner_body(
@@ -856,11 +905,10 @@
 
 
 def last_update_body(
-    place, outflow, field, changed, low, inner, high, from_low, from_high, result
+    place, outflow, field, changed, low, inner, high, first, second, result
 ):
     top = top_flags()
-    flags = ends(place, 0)
-    parts = (low, inner, high, from_low, from_high)
+    parts = (low, inner, high, *arrived(place, first, second))
     for i in range(8):
         for n in range(29):
             column = column_of(n)
@@ -871,7 +919,7 @@
                 value = changed[i, n - 25]
             else:
                 value = field[i, n + 1]
-            value = value + keep * fold_row(flags, i, n + 1, *parts)
+            value = value + keep * fold_row(i, n + 1, *parts)
             result[i, column] = value
             if n % 7 == 0 and 0 < n < 28:
                 result[i, column - 1] = value
@@ -915,6 +963,21 @@
     return lax.ppermute(to_high, axis, upward), lax.ppermute(to_low, axis, downward)
 
 
+def exchange_along_first(first, second):
+    count, across = lax.axis_size("dom"), lax.axis_size("inner")
+    forward = []
+    for c in range(across):
+        for d in range(count):
+            if c % 2 == 0:
+                d_next, c_next = (d + 1, c) if d < count - 1 else (d, c + 1)
+            else:
+                d_next, c_next = (d - 1, c) if d > 0 else (d, c - 1)
+            forward.append((d * across + c, d_next * across + c_next))
+    backward = [(target, source) for source, target in forward]
+    axes = ("dom", "inner")
+    return lax.ppermute(first, axes, forward), lax.ppermute(second, axes, backward)
+
+
 def modes_shape(count, rows, dtype):
     return jax.ShapeDtypeStruct((count, 2, rows, 256), dtype)
 
@@ -922,32 +985,28 @@
 def solve(place, reciprocals, edge_parts, make_inner, beside):
     forward = [jnp.asarray(t) for t in FORWARD]
     backward = [jnp.asarray(t) for t in BACKWARD]
-    low, high = edge_parts
-    received = exchange(low, high, "dom")
+    low, high, first, second = edge_parts
+    received = exchange_along_first(first, second)
     inner = make_inner()
     (partial,) = call(
         inner_forward_body, [modes_shape(10, 112, F32)], 0,
         [pltpu.VMEM((6, 2, 112, 256), F32)], "inner_forward",
         (inner, *forward), 3 * 10**8,
     )
-    out_low, out_high, modes = call(
+    out_low, out_high, first, second, spectral = call(
         edge_solve_body,
-        [layers(2, 31), layers(2, 31), modes_shape(10, 112, F32)],
+        [layers(2, 31)] * 4 + [modes_shape(4, 112, F32)],
         1,
-        [
-            pltpu.VMEM((4, 31, 8, 128), F32),
-            pltpu.VMEM((4, 2, 112, 256), F32),
-            pltpu.VMEM((4, 2, 224, 256), BF16),
-        ],
+        [pltpu.VMEM((4, 31, 8, 128), F32), pltpu.VMEM((4, 2, 224, 256), BF16)],
         "edge_solve",
         (place, reciprocals, *forward, *backward, partial, low, high, *received),
         10**9,
     )
-    returned = exchange(out_low, out_high, "dom")
+    returned = exchange_along_first(first, second)
     (out_inner,) = call(
         inner_backward_body, [layers(6, 31)], 0,
         [pltpu.VMEM((6, 2, 224, 256), BF16)], "inner_backward",
-        (modes, *backward), 3 * 10**8,
+        (spectral, partial, reciprocals, *backward), 3 * 10**8,
     )
     extra = beside(inner, received)
     if extra is not None:
@@ -972,41 +1031,45 @@
             lax.axis_size("inner"),
         ]
     ).astype(jnp.int32)
-    to_low, to_high, coefficients = pack_first(start, source, coefficients, outflow)
-    start, source, to_low, to_high = lax.optimization_barrier((start, source, to_low, to_high))
+    start, source, coefficients, to_low, to_high = lax.optimization_barrier(
+        (start, source, coefficients, *pack_first(start, source, coefficients, outflow))
+    )
     from_low, from_high = exchange(to_low, to_high, "inner")
-    own_image, source_part = call(
-        own_image_body, [layers(8, 31), layers(8, 31)], 1, [plane_scratch()], "own_image",
-        (place, coefficients, start, source, table), 3 * 10**8,
-    )
+
+    def own_image(wanted, name, start, source):
+        return call(
+            functools.partial(own_image_body, wanted), [layers(8, 31), layers(8, 31)], 1,
+            [plane_scratch()], name, (place, coefficients, start, source, table), 10**8,
+        )
+
+    edge_image, edge_source = own_image(EDGES, "own_edges", start, source)
     (reciprocals,) = call(
         reciprocal_body, [modes_shape(10, 112, F32)], 0, [], "reciprocals",
         (coefficients, *[jnp.asarray(t) for t in VALUES]), 10**8,
     )
-    joined = (
-        place, outflow, start, from_low, from_high, table, own_image,
-        source_part,
-    )
+    joined = (place, outflow, start, from_low, from_high, table)
     join_scratch = [
         plane_scratch(), pltpu.VMEM((8, 16, 8, 128), F32), pltpu.VMEM((8, 31, 8, 128), F32)
     ]
-    low, high = call(
-        functools.partial(first_join_body, EDGES), [layers(2, 31), layers(2, 31)], 2,
-        join_scratch, "first_edges", joined, 10**8,
-    )
+    edge_parts = call(
+        functools.partial(first_join_body, EDGES), [layers(2, 31)] * 4, 2,
+        join_scratch, "first_edges", (*joined, edge_image, edge_source), 10**8,
+    )
+    late_start, late_source, *edge_parts = lax.optimization_barrier((start, source, *edge_parts))
+    inner_image, inner_source = own_image(INNER, "own_inner", late_start, late_source)
 
     def first_inner_body(*refs):
-        count = len(joined)
+        count = len(joined) + 2
         parts, (inner, *scratch) = refs[: count + 2], refs[count + 2 :]
         first_join_body(INNER, *parts, inner, *scratch)
 
     def first_inner():
         return call(
             first_inner_body, [layers(6, 31)], 2, join_scratch, "first_inner",
-            (*joined, low, high), 10**8,
+            (*joined, inner_image, inner_source, *edge_parts[:2]), 10**8,
         )[0]
 
-    solved, _ = solve(place, reciprocals, (low, high), first_inner, lambda *_: None)
+    solved, _ = solve(place, reciprocals, edge_parts, first_inner, lambda *_: None)
     news = exchange(*fold(9, place, outflow, solved), "inner")
     field, middle_image = call(
         update_body, [layers(8, 31), layers(8, 15)], 2, [plane_scratch()], "update",
@@ -1016,21 +1079,22 @@
         place, outflow, coefficients, from_low, from_high, table
     )
     join_scratch = [plane_scratch(), pltpu.VMEM((8, 31, 8, 128), F32)]
-    changed, rows, low, high = call(
+    changed, rows, *edge_parts = call(
         second_edges_body,
-        [layers(8, 4), layers(8, 30), layers(2, 31), layers(2, 31)],
+        [layers(8, 4), layers(8, 30)] + [layers(2, 31)] * 4,
         2, join_scratch, "second_edges",
-        (*operands, field, middle_image, source_part, *news), 2 * 10**8,
-    )
+        (*operands, field, middle_image, edge_source, *news), 2 * 10**8,
+    )
+    low, high = edge_parts[:2]
 
     def second_inner():
         return call(
             second_inner_body, [layers(6, 31)], 2, join_scratch, "second_inner",
-            (*operands, rows, middle_image, source_part, low, high), 2 * 10**8,
+            (*operands, rows, middle_image, inner_source, low, high), 2 * 10**8,
         )[0]
 
     solved, residual = solve(
-        place, reciprocals, (low, high), second_inner,
+        place, reciprocals, edge_parts, second_inner,
         lambda inner, received: residual_out(place, low, inner, high, received),
     )
     news = exchange(*fold(2, place, outflow, solved), "inner")

time: 84.9 us -> 79 us (0.931)
  the two profiles are of different devices: /device:TPU:1 before, /device:TPU:25 now
where the time goes in v2:
time: 79 us; the launch traced here: 77.8 us
  Pallas kernels  38.5 us (49%)
  waiting for transfers between devices  20.6 us (26%)
  starting transfers between devices  15.3 us (19%)
  local copies, waits for them, and re-layouts  2.53 us (3%)
  between operations  0.89 us (1%)
    pallas_call x17, Pallas kernels, call(): pl.pallas_call(body, out_shape=tuple(outs), in_specs=[whole(pltpu.SMEM if...  30.8 us
    ppermute x4, starting transfers between devices, exchange_along_first(): lax.ppermute(first, axes, forward)  12.4 us
    ppermute x3, waiting for transfers between devices, exchange(): lax.ppermute(to_low, axis, downward)  7.71 us
    ppermute x4, waiting for transfers between devices, exchange_along_first(): lax.ppermute(second, axes, backward)  7.22 us
    ppermute x4, waiting for transfers between devices, exchange_along_first(): lax.ppermute(first, axes, forward)  4.17 us
    pallas_call x1, Pallas kernels, residual_out(): pl.pallas_call(residual_body, out_shape=layers(8, 32), in_specs=[whole(pl...  4.07 us
    unnamed x28, local copies, waits for them, and re-layouts  2.53 us
    ppermute x3, starting transfers between devices, exchange(): lax.ppermute(to_high, axis, upward)  2.21 us
  transfers between devices with their start and end apart: 14, of which 12 were waited for; matrix products, arithmetic and copies ran while one was open for 0% of the time, Pallas kernels for 30%

profile of v2, /device:TPU:25, one launch (start us, length us, event | category | flops | bytes accessed | tf_op | source)
XLA Modules:
  0.0 77.8 jit_solution(740278220154421955)
XLA Ops:
  0.7 2.0 %pack_first.1 = (f32[8,9,8,128]{3,2,1,0:T(8,128)}, f32[8,9,8,128]{3,2,1,0:T(8,128)}) custom-call(s32[8,32]{1,0:T(8,128)} %outflow.17, f32[8,32,8,128]{3,2,1,0:T(8,128)} %start.5, f32[8,32,8,128]{3,2,1,0:T(8,128)} %source.3, f32[3,1,4,128]{3,2,1,0:T(4,128)} %coefficients.7), custom_call_target="tpu_custom_call" | custom-call | tf_op jit(solution)/shard_map/pack_first/pallas_call | solution.py:308
  2.7 1.8 %collective-permute-start = (f32[8,9,8,128]{3,2,1,0:T(8,128)}, f32[8,9,8,128]{3,2,1,0:T(8,128)S(1)}, u32[]{:S(2)}, u32[]{:S(2)}) collective-permute-start(f32[8,9,8,128]{3,2,1,0:T(8,128)} %get-tuple-element.51), channel_id=1, source_target_pairs={{0,1},{1,2},{2,3},{3,4},{4,5},{5,6},{6,7},{7,0},{8,9},{9,10},{10,1... | collective-permute-start | bytes 884744 | tf_op jit(solution)/shard_map/ppermute | solution.py:963
  6.1 1.9 %own_edges.1 = (f32[8,31,8,128]{3,2,1,0:T(8,128)S(1)}, f32[8,31,8,128]{3,2,1,0:T(8,128)S(1)}) custom-call(s32[4]{0:T(128)S(1)} %pad_add_fusion.place.refs_0_, f32[3,1,4,128]{3,2,1,0:T(4,128)S(1)} %copy-done.10, f32[8,32,8,128]{3,2,1,0:T(8,128)S(1)} %copy-done, f32[8,32,8,128]{3,2,1,0:T(8,128)S(1)} %copy-done.1, bf16[192,192]{1,0:T(8,128)(2,1)S(1)} %copy-done.2), custom_call_target="tpu_custom_call" | custom-call | flops 100000000 | bytes 4282384 | tf_op jit(solution)/shard_map/own_edges/pallas_call | solution.py:256
  8.4 2.4 %collective-permute-done.1.from_high.refs_4_ = f32[8,9,8,128]{3,2,1,0:T(8,128)S(1)} collective-permute-done((f32[8,9,8,128]{3,2,1,0:T(8,128)}, f32[8,9,8,128]{3,2,1,0:T(8,128)S(1)}, u32[]{:S(2)}, u32[]{:S(2)}) %collective-permute-start.1) | collective-permute-done | bytes 294944 | tf_op jit(solution)/shard_map/ppermute | solution.py:963
  13.2 4.0 %collective-permute-start.2 = (f32[2,31,8,128]{3,2,1,0:T(8,128)S(1)}, f32[2,31,8,128]{3,2,1,0:T(8,128)S(1)}, u32[]{:S(2)}, u32[]{:S(2)}) collective-permute-start(f32[2,31,8,128]{3,2,1,0:T(8,128)S(1)} %get-tuple-element.66), channel_id=1, source_target_pairs={{0,8},{8,16},{16,24},{24,32},{32,40},{40,48},{48,56},{56,64},{64,7... | collective-permute-start | bytes 761864 | tf_op jit(solution)/shard_map/ppermute | solution.py:978
  17.6 1.8 %own_inner.1 = (f32[8,31,8,128]{3,2,1,0:T(8,128)S(1)}, f32[8,31,8,128]{3,2,1,0:T(8,128)S(1)}) custom-call(s32[4]{0:T(128)S(1)} %pad_add_fusion.place.refs_0_, f32[3,1,4,128]{3,2,1,0:T(4,128)S(1)} %copy-done.10, f32[8,32,8,128]{3,2,1,0:T(8,128)S(1)} %copy-done, f32[8,32,8,128]{3,2,1,0:T(8,128)S(1)} %copy-done.1, bf16[192,192]{1,0:T(8,128)(2,1)S(1)} %copy-done.3), custom_call_target="tpu_custom_call" | custom-call | flops 100000000 | bytes 4282384 | tf_op jit(solution)/shard_map/own_inner/pallas_call | solution.py:256
  20.9 1.9 %inner_forward.2.partial = f32[10,2,112,256]{3,2,1,0:T(8,128)S(1)} custom-call(f32[6,31,8,128]{3,2,1,0:T(8,128)S(1)} %first_inner.1.inner, bf16[112,160]{1,0:T(8,128)(2,1)S(1)} %copy-done.7, bf16[112,160]{1,0:T(8,128)(2,1)S(1)} %copy-done.6), custom_call_target="tpu_custom_call" | custom-call | flops 300000000 | bytes 3198976 | tf_op jit(solution)/shard_map/inner_forward/pallas_call | solution.py:256
  24.4 3.2 %edge_solve.2 = (f32[2,31,8,128]{3,2,1,0:T(8,128)S(1)}, f32[2,31,8,128]{3,2,1,0:T(8,128)S(1)}, f32[2,31,8,128]{3,2,1,0:T(8,128)S(1)}, f32[2,31,8,128]{3,2,1,0:T(8,128)S(1)}, f32[4,2,112,256]{3,2,1,0:T(8,128)S(1)}) custom-call(s32[4]{0:T(128)S(1)} %pad_add_fusion.place.refs_0_, f32[10,2,112,256]{3,2,1,0:T(8,128)S(1)} %reciprocals.1, ...), custom_call_target="tpu_custom_call" | custom-call | flops 1000000000 | bytes 7895056 | tf_op jit(solution)/shard_map/edge_solve/pallas_call | solution.py:256
  27.6 2.5 %collective-permute-start.4 = (f32[2,31,8,128]{3,2,1,0:T(8,128)S(1)}, f32[2,31,8,128]{3,2,1,0:T(8,128)S(1)}, u32[]{:S(2)}, u32[]{:S(2)}) collective-permute-start(f32[2,31,8,128]{3,2,1,0:T(8,128)S(1)} %get-tuple-element.71), channel_id=1, source_target_pairs={{0,8},{8,16},{16,24},{24,32},{32,40},{40,48},{48,56},{56,64},{64,7... | collective-permute-start | bytes 761864 | tf_op jit(solution)/shard_map/ppermute | solution.py:978
  30.1 2.5 %inner_backward.2.inner = f32[6,31,8,128]{3,2,1,0:T(8,128)S(1)} custom-call(f32[4,2,112,256]{3,2,1,0:T(8,128)S(1)} %get-tuple-element.69.spectral, f32[10,2,112,256]{3,2,1,0:T(8,128)S(1)} %inner_forward.2.partial, f32[10,2,112,256]{3,2,1,0:T(8,128)S(1)} %reciprocals.1, bf16[160,224]{1,0:T(8,128)(2,1)S(1)} %copy-done.5, bf16[160,112]{1,0:T(8,128)(2,1)S(1)} %copy-done.8), custom_call_target="tpu_custom_call" | custom-call | flops 300000000 | bytes 6481920 | tf_op jit(solution)/shard_map/inner_backward/pallas_call | solution.py:256
  32.6 3.1 %collective-permute-done.4.first = f32[2,31,8,128]{3,2,1,0:T(8,128)S(1)} collective-permute-done((f32[2,31,8,128]{3,2,1,0:T(8,128)S(1)}, f32[2,31,8,128]{3,2,1,0:T(8,128)S(1)}, u32[]{:S(2)}, u32[]{:S(2)}) %collective-permute-start.4) | collective-permute-done | bytes 253984 | tf_op jit(solution)/shard_map/ppermute | solution.py:978
  35.6 2.0 %collective-permute-done.5.second = f32[2,31,8,128]{3,2,1,0:T(8,128)S(1)} collective-permute-done((f32[2,31,8,128]{3,2,1,0:T(8,128)S(1)}, f32[2,31,8,128]{3,2,1,0:T(8,128)S(1)}, u32[]{:S(2)}, u32[]{:S(2)}) %collective-permute-start.5) | collective-permute-done | bytes 253984 | tf_op jit(solution)/shard_map/ppermute | solution.py:978
  38.9 2.5 %update.1 = (f32[8,31,8,128]{3,2,1,0:T(8,128)S(1)}, f32[8,15,8,128]{3,2,1,0:T(8,128)S(1)}) custom-call(s32[4]{0:T(128)S(1)} %pad_add_fusion.place.refs_0_, s32[8,32]{1,0:T(8,128)S(1)} %copy-done.9, f32[8,32,8,128]{3,2,1,0:T(8,128)S(1)} %copy-done, f32[3,1,4,128]{3,2,1,0:T(4,128)S(1)} %copy-done.11, bf16[192,192]{1,0:T(8,128)(2,1)S(1)} %copy-done.4, ...), custom_call_target="tpu_custom_call" | custom-call | flops 200000000 | bytes 4488208 | tf_op jit(solution)/shard_map/update/pallas_call | solution.py:256
  42.1 2.7 %collective-permute-done.7.high_news = f32[8,9,8,128]{3,2,1,0:T(8,128)S(1)} collective-permute-done((f32[8,9,8,128]{3,2,1,0:T(8,128)S(1)}, f32[8,9,8,128]{3,2,1,0:T(8,128)S(1)}, u32[]{:S(2)}, u32[]{:S(2)}) %collective-permute-start.7) | collective-permute-done | bytes 294944 | tf_op jit(solution)/shard_map/ppermute | solution.py:963
  44.8 2.1 %second_edges.1 = (f32[8,4,8,128]{3,2,1,0:T(8,128)S(1)}, f32[8,30,8,128]{3,2,1,0:T(8,128)S(1)}, f32[2,31,8,128]{3,2,1,0:T(8,128)S(1)}, f32[2,31,8,128]{3,2,1,0:T...) custom-call(s32[4]{0:T(128)S(1)} %pad_add_fusion.place.refs_0_, s32[8,32]{1,0:T(8,128)S(1)} %copy-done.9, ...), custom_call_target="tpu_custom_call" | custom-call | flops 200000000 | bytes 5987344 | tf_op jit(solution)/shard_map/second_edges/pallas_call | solution.py:256
  46.9 3.8 %collective-permute-start.8 = (f32[2,31,8,128]{3,2,1,0:T(8,128)S(1)}, f32[2,31,8,128]{3,2,1,0:T(8,128)S(1)}, u32[]{:S(2)}, u32[]{:S(2)}) collective-permute-start(f32[2,31,8,128]{3,2,1,0:T(8,128)S(1)} %get-tuple-element.81), channel_id=1, source_target_pairs={{0,8},{8,16},{16,24},{24,32},{32,40},{40,48},{48,56},{56,64},{64,7... | collective-permute-start | bytes 761864 | tf_op jit(solution)/shard_map/ppermute | solution.py:978
  50.7 2.0 %second_inner.1.inner = f32[6,31,8,128]{3,2,1,0:T(8,128)S(1)} custom-call(s32[4]{0:T(128)S(1)} %pad_add_fusion.place.refs_0_, s32[8,32]{1,0:T(8,128)S(1)} %copy-done.9, f32[3,1,4,128]{3,2,1,0:T(4,128)S(1)} %copy-done.11, f32[8,9,8,128]{3,2,1,0:T(8,128)S(1)} %collective-permute-done.from_low.refs_3_, ...), custom_call_target="tpu_custom_call" | custom-call | flops 200000000 | bytes 4504592 | tf_op jit(solution)/shard_map/second_inner/pallas_call | solution.py:256
  52.7 1.9 %inner_forward.3.partial = f32[10,2,112,256]{3,2,1,0:T(8,128)S(1)} custom-call(f32[6,31,8,128]{3,2,1,0:T(8,128)S(1)} %second_inner.1.inner, bf16[112,160]{1,0:T(8,128)(2,1)S(1)} %copy-done.7, bf16[112,160]{1,0:T(8,128)(2,1)S(1)} %copy-done.6), custom_call_target="tpu_custom_call" | custom-call | flops 300000000 | bytes 3198976 | tf_op jit(solution)/shard_map/inner_forward/pallas_call | solution.py:256
  55.7 2.3 %collective-permute-done.9.second = f32[2,31,8,128]{3,2,1,0:T(8,128)S(1)} collective-permute-done((f32[2,31,8,128]{3,2,1,0:T(8,128)S(1)}, f32[2,31,8,128]{3,2,1,0:T(8,128)S(1)}, u32[]{:S(2)}, u32[]{:S(2)}) %collective-permute-start.9) | collective-permute-done | bytes 253984 | tf_op jit(solution)/shard_map/ppermute | solution.py:978
  57.9 3.2 %edge_solve.3 = (f32[2,31,8,128]{3,2,1,0:T(8,128)S(1)}, f32[2,31,8,128]{3,2,1,0:T(8,128)S(1)}, f32[2,31,8,128]{3,2,1,0:T(8,128)S(1)}, f32[2,31,8,128]{3,2,1,0:T(8,128)S(1)}, f32[4,2,112,256]{3,2,1,0:T(8,128)S(1)}) custom-call(s32[4]{0:T(128)S(1)} %pad_add_fusion.place.refs_0_, f32[10,2,112,256]{3,2,1,0:T(8,128)S(1)} %reciprocals.1, ...), custom_call_target="tpu_custom_call" | custom-call | flops 1000000000 | bytes 7895056 | tf_op jit(solution)/shard_map/edge_solve/pallas_call | solution.py:256
  61.1 2.1 %collective-permute-start.10 = (f32[2,31,8,128]{3,2,1,0:T(8,128)S(1)}, f32[2,31,8,128]{3,2,1,0:T(8,128)S(1)}, u32[]{:S(2)}, u32[]{:S(2)}) collective-permute-start(f32[2,31,8,128]{3,2,1,0:T(8,128)S(1)} %get-tuple-element.87), channel_id=1, source_target_pairs={{0,8},{8,16},{16,24},{24,32},{32,40},{40,48},{48,56},{56,64},{64,7... | collective-permute-start | bytes 761864 | tf_op jit(solution)/shard_map/ppermute | solution.py:978
  63.2 4.1 %residual.1 = f32[8,32,8,128]{3,2,1,0:T(8,128)} custom-call(s32[4]{0:T(128)S(1)} %pad_add_fusion.place.refs_0_, f32[2,31,8,128]{3,2,1,0:T(8,128)S(1)} %get-tuple-element.79.low, f32[6,31,8,128]{3,2,1,0:T(8,128)S(1)} %second_inner.1.inner, f32[2,31,8,128]{3,2,1,0:T(8,128)S(1)} %get-tuple-element.80.high, f32[2,31,8,128]{3,2,1,0:T(8,128)S(1)} %collective-permute-done.8.first, ...), custom_call_target="tpu_custom_call" | custom-call | flops 10000000 | bytes 4194304 | tf_op jit(solution)/shard_map/residual/pallas_call | solution.py:767
  67.3 2.5 %inner_backward.3.inner = f32[6,31,8,128]{3,2,1,0:T(8,128)S(1)} custom-call(f32[4,2,112,256]{3,2,1,0:T(8,128)S(1)} %get-tuple-element.84.spectral, f32[10,2,112,256]{3,2,1,0:T(8,128)S(1)} %inner_forward.3.partial, f32[10,2,112,256]{3,2,1,0:T(8,128)S(1)} %reciprocals.1, bf16[160,224]{1,0:T(8,128)(2,1)S(1)} %copy-done.5, bf16[160,112]{1,0:T(8,128)(2,1)S(1)} %copy-done.8), custom_call_target="tpu_custom_call" | custom-call | flops 300000000 | bytes 6481920 | tf_op jit(solution)/shard_map/inner_backward/pallas_call | solution.py:256
  73.6 2.7 %collective-permute-done.13.high_news = f32[8,2,8,128]{3,2,1,0:T(8,128)S(1)} collective-permute-done((f32[8,2,8,128]{3,2,1,0:T(8,128)S(1)}, f32[8,2,8,128]{3,2,1,0:T(8,128)S(1)}, u32[]{:S(2)}, u32[]{:S(2)}) %collective-permute-start.13) | collective-permute-done | bytes 65568 | tf_op jit(solution)/shard_map/ppermute | solution.py:963
  (53 shorter events, 16.2 us)
Async XLA Ops:
  0.6 10.2 %copy-start.9 = (s32[8,32]{1,0:T(8,128)S(1)}, s32[8,32]{1,0:T(8,128)}, u32[]{:S(2)}) copy-start(s32[8,32]{1,0:T(8,128)} %outflow.17) | copy-start | bytes 3076
  0.6 3.9 %copy-start.1 = (f32[8,32,8,128]{3,2,1,0:T(8,128)S(1)}, f32[8,32,8,128]{3,2,1,0:T(8,128)}, u32[]{:S(2)}) copy-start(f32[8,32,8,128]{3,2,1,0:T(8,128)} %source.3) | copy-start | bytes 3145732
  0.6 3.9 %copy-start = (f32[8,32,8,128]{3,2,1,0:T(8,128)S(1)}, f32[8,32,8,128]{3,2,1,0:T(8,128)}, u32[]{:S(2)}) copy-start(f32[8,32,8,128]{3,2,1,0:T(8,128)} %start.5) | copy-start | bytes 3145732
  2.7 5.8 %collective-permute-start = (f32[8,9,8,128]{3,2,1,0:T(8,128)}, f32[8,9,8,128]{3,2,1,0:T(8,128)S(1)}, u32[]{:S(2)}, u32[]{:S(2)}) collective-permute-start(f32[8,9,8,128]{3,2,1,0:T(8,128)} %get-tuple-element.51), channel_id=1, source_target_pairs={{0,1},{1,2},{2,3},{3,4},{4,5},{5,6},{6,7},{7,0},{8,9},{9,10},{10,1... | collective-permute-start | bytes 884744 | tf_op jit(solution)/shard_map/ppermute | solution.py:963
  4.5 6.4 %collective-permute-start.1 = (f32[8,9,8,128]{3,2,1,0:T(8,128)}, f32[8,9,8,128]{3,2,1,0:T(8,128)S(1)}, u32[]{:S(2)}, u32[]{:S(2)}) collective-permute-start(f32[8,9,8,128]{3,2,1,0:T(8,128)} %get-tuple-element.52), channel_id=1, source_target_pairs={{1,0},{2,1},{3,2},{4,3},{5,4},{6,5},{7,6},{0,7},{9,8},{10,9},{11,1... | collective-permute-start | bytes 884744 | tf_op jit(solution)/shard_map/ppermute | solution.py:963
  6.1 11.1 %copy-start.12 = (f32[112,128]{1,0:T(8,128)S(1)}, f32[112,128]{1,0:T(8,128)}, u32[]{:S(2)}) copy-start(f32[112,128]{1,0:T(8,128)} %constant.29.clone.third_values) | copy-start | bytes 172036
  6.1 11.1 %copy-start.13 = (f32[112,128]{1,0:T(8,128)S(1)}, f32[112,128]{1,0:T(8,128)}, u32[]{:S(2)}) copy-start(f32[112,128]{1,0:T(8,128)} %constant.28.clone.second_values) | copy-start | bytes 172036
  13.2 9.7 %collective-permute-start.2 = (f32[2,31,8,128]{3,2,1,0:T(8,128)S(1)}, f32[2,31,8,128]{3,2,1,0:T(8,128)S(1)}, u32[]{:S(2)}, u32[]{:S(2)}) collective-permute-start(f32[2,31,8,128]{3,2,1,0:T(8,128)S(1)} %get-tuple-element.66), channel_id=1, source_target_pairs={{0,8},{8,16},{16,24},{24,32},{32,40},{40,48},{48,56},{56,64},{64,7... | collective-permute-start | bytes 761864 | tf_op jit(solution)/shard_map/ppermute | solution.py:978
  17.2 7.2 %collective-permute-start.3 = (f32[2,31,8,128]{3,2,1,0:T(8,128)S(1)}, f32[2,31,8,128]{3,2,1,0:T(8,128)S(1)}, u32[]{:S(2)}, u32[]{:S(2)}) collective-permute-start(f32[2,31,8,128]{3,2,1,0:T(8,128)S(1)} %get-tuple-element.67), channel_id=1, source_target_pairs={{8,0},{16,8},{24,16},{32,24},{40,32},{48,40},{56,48},{64,56},{72,6... | collective-permute-start | bytes 761864 | tf_op jit(solution)/shard_map/ppermute | solution.py:978
  19.4 1.5 %copy-start.6 = (bf16[112,160]{1,0:T(8,128)(2,1)S(1)}, bf16[112,160]{1,0:T(8,128)(2,1)}, u32[]{:S(2)}) copy-start(bf16[112,160]{1,0:T(8,128)(2,1)} %constant.31.clone.forward_low) | copy-start | bytes 107524
  20.9 3.5 %copy-start.5 = (bf16[160,224]{1,0:T(8,128)(2,1)S(1)}, bf16[160,224]{1,0:T(8,128)(2,1)}, u32[]{:S(2)}) copy-start(bf16[160,224]{1,0:T(8,128)(2,1)} %constant.32.clone.backward) | copy-start | bytes 215044
  20.9 3.5 %copy-start.8 = (bf16[160,112]{1,0:T(8,128)(2,1)S(1)}, bf16[160,112]{1,0:T(8,128)(2,1)}, u32[]{:S(2)}) copy-start(bf16[160,112]{1,0:T(8,128)(2,1)} %constant.33.clone.backward_low) | copy-start | bytes 107524
  27.6 8.0 %collective-permute-start.4 = (f32[2,31,8,128]{3,2,1,0:T(8,128)S(1)}, f32[2,31,8,128]{3,2,1,0:T(8,128)S(1)}, u32[]{:S(2)}, u32[]{:S(2)}) collective-permute-start(f32[2,31,8,128]{3,2,1,0:T(8,128)S(1)} %get-tuple-element.71), channel_id=1, source_target_pairs={{0,8},{8,16},{16,24},{24,32},{32,40},{40,48},{48,56},{56,64},{64,7... | collective-permute-start | bytes 761864 | tf_op jit(solution)/shard_map/ppermute | solution.py:978
  30.1 7.6 %collective-permute-start.5 = (f32[2,31,8,128]{3,2,1,0:T(8,128)S(1)}, f32[2,31,8,128]{3,2,1,0:T(8,128)S(1)}, u32[]{:S(2)}, u32[]{:S(2)}) collective-permute-start(f32[2,31,8,128]{3,2,1,0:T(8,128)S(1)} %get-tuple-element.72), channel_id=1, source_target_pairs={{8,0},{16,8},{24,16},{32,24},{40,32},{48,40},{56,48},{64,56},{72,6... | collective-permute-start | bytes 761864 | tf_op jit(solution)/shard_map/ppermute | solution.py:978
  30.1 8.8 %copy-start.4 = (bf16[192,192]{1,0:T(8,128)(2,1)S(1)}, bf16[192,192]{1,0:T(8,128)(2,1)}, u32[]{:S(2)}) copy-start(bf16[192,192]{1,0:T(8,128)(2,1)} %constant.27.clone.table.refs_5_) | copy-start | bytes 221188
  30.1 8.8 %copy-start.11 = (f32[3,1,4,128]{3,2,1,0:T(4,128)S(1)}, f32[3,1,4,128]{3,2,1,0:T(4,128)}, u32[]{:S(2)}) copy-start(f32[3,1,4,128]{3,2,1,0:T(4,128)} %coefficients.7) | copy-start | bytes 18436
  38.4 3.7 %collective-permute-start.6 = (f32[8,9,8,128]{3,2,1,0:T(8,128)S(1)}, f32[8,9,8,128]{3,2,1,0:T(8,128)S(1)}, u32[]{:S(2)}, u32[]{:S(2)}) collective-permute-start(f32[8,9,8,128]{3,2,1,0:T(8,128)S(1)} %get-tuple-element.75), channel_id=1, source_target_pairs={{0,1},{1,2},{2,3},{3,4},{4,5},{5,6},{6,7},{7,0},{8,9},{9,10},{10,1... | collective-permute-start | bytes 884744 | tf_op jit(solution)/shard_map/ppermute | solution.py:963
  38.4 6.3 %collective-permute-start.7 = (f32[8,9,8,128]{3,2,1,0:T(8,128)S(1)}, f32[8,9,8,128]{3,2,1,0:T(8,128)S(1)}, u32[]{:S(2)}, u32[]{:S(2)}) collective-permute-start(f32[8,9,8,128]{3,2,1,0:T(8,128)S(1)} %get-tuple-element.76), channel_id=1, source_target_pairs={{1,0},{2,1},{3,2},{4,3},{5,4},{6,5},{7,6},{0,7},{9,8},{10,9},{11,1... | collective-permute-start | bytes 884744 | tf_op jit(solution)/shard_map/ppermute | solution.py:963
  46.9 8.8 %collective-permute-start.8 = (f32[2,31,8,128]{3,2,1,0:T(8,128)S(1)}, f32[2,31,8,128]{3,2,1,0:T(8,128)S(1)}, u32[]{:S(2)}, u32[]{:S(2)}) collective-permute-start(f32[2,31,8,128]{3,2,1,0:T(8,128)S(1)} %get-tuple-element.81), channel_id=1, source_target_pairs={{0,8},{8,16},{16,24},{24,32},{32,40},{40,48},{48,56},{56,64},{64,7... | collective-permute-start | bytes 761864 | tf_op jit(solution)/shard_map/ppermute | solution.py:978
  50.7 7.2 %collective-permute-start.9 = (f32[2,31,8,128]{3,2,1,0:T(8,128)S(1)}, f32[2,31,8,128]{3,2,1,0:T(8,128)S(1)}, u32[]{:S(2)}, u32[]{:S(2)}) collective-permute-start(f32[2,31,8,128]{3,2,1,0:T(8,128)S(1)} %get-tuple-element.82), channel_id=1, source_target_pairs={{8,0},{16,8},{24,16},{32,24},{40,32},{48,40},{56,48},{64,56},{72,6... | collective-permute-start | bytes 761864 | tf_op jit(solution)/shard_map/ppermute | solution.py:978
  61.1 8.7 %collective-permute-start.10 = (f32[2,31,8,128]{3,2,1,0:T(8,128)S(1)}, f32[2,31,8,128]{3,2,1,0:T(8,128)S(1)}, u32[]{:S(2)}, u32[]{:S(2)}) collective-permute-start(f32[2,31,8,128]{3,2,1,0:T(8,128)S(1)} %get-tuple-element.87), channel_id=1, source_target_pairs={{0,8},{8,16},{16,24},{24,32},{32,40},{40,48},{48,56},{56,64},{64,7... | collective-permute-start | bytes 761864 | tf_op jit(solution)/shard_map/ppermute | solution.py:978
  63.2 7.9 %collective-permute-start.11 = (f32[2,31,8,128]{3,2,1,0:T(8,128)S(1)}, f32[2,31,8,128]{3,2,1,0:T(8,128)S(1)}, u32[]{:S(2)}, u32[]{:S(2)}) collective-permute-start(f32[2,31,8,128]{3,2,1,0:T(8,128)S(1)} %get-tuple-element.88), channel_id=1, source_target_pairs={{8,0},{16,8},{24,16},{32,24},{40,32},{48,40},{56,48},{64,56},{72,6... | collective-permute-start | bytes 761864 | tf_op jit(solution)/shard_map/ppermute | solution.py:978
  71.8 1.7 %collective-permute-start.12 = (f32[8,2,8,128]{3,2,1,0:T(8,128)S(1)}, f32[8,2,8,128]{3,2,1,0:T(8,128)S(1)}, u32[]{:S(2)}, u32[]{:S(2)}) collective-permute-start(f32[8,2,8,128]{3,2,1,0:T(8,128)S(1)} %get-tuple-element.89), channel_id=1, source_target_pairs={{0,1},{1,2},{2,3},{3,4},{4,5},{5,6},{6,7},{7,0},{8,9},{9,10},{10,1... | collective-permute-start | bytes 196616 | tf_op jit(solution)/shard_map/ppermute | solution.py:963
  72.2 4.0 %collective-permute-start.13 = (f32[8,2,8,128]{3,2,1,0:T(8,128)S(1)}, f32[8,2,8,128]{3,2,1,0:T(8,128)S(1)}, u32[]{:S(2)}, u32[]{:S(2)}) collective-permute-start(f32[8,2,8,128]{3,2,1,0:T(8,128)S(1)} %get-tuple-element.90), channel_id=1, source_target_pairs={{1,0},{2,1},{3,2},{4,3},{5,4},{6,5},{7,6},{0,7},{9,8},{10,9},{11,1... | collective-permute-start | bytes 196616 | tf_op jit(solution)/shard_map/ppermute | solution.py:963
  (4 other events, 4.0 us)

commit v3 on v2

--- a/solution.py
+++ b/solution.py
@@ -122,22 +122,33 @@
     beside[1] = BASIS[9]
     beside[6] = BASIS[0]
     beside[7] = BASIS[1]
-    back = np.zeros((160, 112))
-    back[:80, :100] = np.kron(BASIS, own)
-    back[80:, :100] = np.kron(BASIS, beside)
-    back_high, back_low = two_parts(back)
-    forward_high, forward_low = two_parts(back.T)
-    return (
-        (forward_high, forward_low),
-        (np.concatenate([back_high, back_high], axis=1), back_low),
-    )
+    forward, backward = [], []
+    for modes in (EVEN, ODD):
+        half = HALF_BASIS[:, modes]
+        matrix = np.zeros((80, 64))
+        matrix[:40, :50] = np.kron(half, own)
+        matrix[40:, :50] = np.kron(half, beside)
+        high, low = two_parts(matrix.T)
+        forward.append(np.concatenate([high, high, low], axis=1))
+        high, low = two_parts(matrix)
+        backward.append((np.concatenate([high, high], 1), np.concatenate([low, 0 * low], 1)))
+    pieces = []
+    for part in range(2):
+        even, odd = backward[0][part], backward[1][part]
+        for first in (0, 40):
+            for sign in (1, -1):
+                pieces.append(
+                    np.concatenate([even[first : first + 40], sign * odd[first : first + 40]], 1)
+                )
+    return np.concatenate(forward), np.concatenate(pieces)
 
 
 def value_tables():
-    second_values = np.ones((112, 128), np.float32)
-    third_values = np.ones((112, 128), np.float32)
-    second_values[:100] = np.repeat(EIGEN, 10)[:, None]
-    third_values[:100] = np.tile(EIGEN, 10)[:, None]
+    second_values = np.ones((128, 128), np.float32)
+    third_values = np.ones((128, 128), np.float32)
+    for first, modes in ((0, EVEN), (64, ODD)):
+        second_values[first : first + 50] = np.repeat(EIGEN[modes], 10)[:, None]
+        third_values[first : first + 50] = np.tile(EIGEN, 5)[:, None]
     return second_values, third_values
 
 
@@ -361,7 +372,7 @@
         )
         return carry
 
-    lax.fori_loop(0, len(wanted), step, 0, unroll=2)
+    lax.fori_loop(0, len(wanted), step, 0, unroll=True)
 
 
 def combine(
@@ -392,7 +403,9 @@
             )
 
         row(0, add_first)
-        lax.fori_loop(1, 7, lambda j, c, row=row: (row(j, False), c)[1], 0)
+        lax.fori_loop(
+            1, 7, lambda j, c, row=row: (row(j, False), c)[1], 0, unroll=True
+        )
         row(7, add_last)
 
 
@@ -438,7 +451,7 @@
                 own_row(1 + 7 * e + j, 8 * e + j)
             return carry
 
-        lax.fori_loop(0, 4, step, 0)
+        lax.fori_loop(0, 4, step, 0, unroll=True)
 
 
 def put_edges(low, high):
@@ -492,8 +505,12 @@
 
 
 def own_image_body(
-    wanted, place, coefficients, start, source, table, image, source_part, planes
+    wanted, place, coefficients, start, source, table, image, source_part, *rest
 ):
+    *kept, planes = rest
+    if kept:
+        kept[0][...] = table[...]
+        kept[1][...] = coefficients[...]
     gains = own_gains(coefficients)
     for pair in ((0, 1), (2, 3)):
         own_elements(
@@ -512,7 +529,10 @@
         lax.fori_loop(0, 4, step, 0)
 
 
-def reciprocal_body(coefficients, second_values, third_values, result):
+BLOCK_ENTRIES = ((0, 0), (0, 1), (1, 1))
+
+
+def reciprocal_body(coefficients, second_values, third_values, result, blocks):
     gain = [[coefficients[c, 0, e : e + 1, :] for e in range(4)] for c in range(3)]
 
     def step(block, carry):
@@ -520,14 +540,22 @@
         second = second_values[pl.ds(at, 16), :]
         third = third_values[pl.ds(at, 16), :]
         for e in range(4):
+            spot = (e // 2, pl.ds(at, 16), LANES[e % 2])
             rest = gain[1][e] * second + gain[2][e] * third
+            values = []
             for p in range(10):
-                result[p, e // 2, pl.ds(at, 16), LANES[e % 2]] = 1.0 / (
-                    rest + gain[0][e] * float(EIGEN[p])
-                )
+                values.append(1.0 / (rest + gain[0][e] * float(EIGEN[p])))
+                result[(p,) + spot] = values[p]
+            for parity, modes in enumerate((EVEN, ODD)):
+                for n, (a, b) in enumerate(BLOCK_ENTRIES):
+                    total = None
+                    for p in modes:
+                        term = values[p] * float(HALF_BASIS[a, p] * HALF_BASIS[b, p])
+                        total = term if total is None else total + term
+                    blocks[(3 * parity + n,) + spot] = total
         return carry
 
-    lax.fori_loop(0, 7, step, 0)
+    lax.fori_loop(0, 8, step, 0)
 
 
 def first_join_body(
@@ -556,14 +584,23 @@
         hand_over(place, *outs)
 
 
-def forward_layers(source, count, forward_high, forward_low, spectral):
+def over_layers(count, visit, unrolled):
+    if unrolled:
+        for a in range(count):
+            visit(a)
+    else:
+        lax.fori_loop(0, count // 2, lambda h, c: (visit(2 * h), visit(2 * h + 1), c)[2], 0)
+
+
+def forward_layers(source, count, forward, spectral, unrolled):
     lane = lane_ids()
     row = row_ids()
     lower_half = row < 4
     valid = (lower_half & (lane < 127)) | ((row > 3) & (lane > 0))
 
-    def columns(a, e):
+    def columns(a, e, sign):
         own = [source[a, 7 * e + b] for b in range(10)]
+        own = [own[b] + sign * own[9 - b] for b in range(5)]
         beside = [
             jnp.where(
                 valid,
@@ -574,60 +611,55 @@
         ]
         return jnp.concatenate(own + beside, axis=0)
 
-    def step(half, carry):
-        for part in range(2):
-            a = 2 * half + part
-            for pair in range(2):
-                values = jnp.concatenate([columns(a, 2 * pair), columns(a, 2 * pair + 1)], axis=1)
+    def visit(a):
+        for pair in range(2):
+            for parity, sign in enumerate((1.0, -1.0)):
+                values = jnp.concatenate(
+                    [columns(a, 2 * pair + side, sign) for side in range(2)], axis=1
+                )
                 top, bottom = split(values)
-                spectral[a, pair] = (
-                    dot(forward_high[...], top)
-                    + dot(forward_high[...], bottom)
-                    + dot(forward_low[...], top)
+                spectral[a, pair, 64 * parity : 64 * parity + 64] = dot(
+                    forward[64 * parity : 64 * parity + 64],
+                    jnp.concatenate([top, bottom, top], axis=0),
                 )
-        return carry
-
-    lax.fori_loop(0, count // 2, step, 0)
-
-
-def backward_layers(halves, count, backward, backward_low, target):
+
+    over_layers(count, visit, unrolled)
+
+
+def backward_layers(halves, count, backward, put, unrolled):
     lane = lane_ids()
     row = row_ids()
     lower_half = row < 4
     valid = (lower_half & (lane > 0)) | ((row > 3) & (lane < 127))
 
-    def step(half, carry):
-        for part in range(2):
-            a = 2 * half + part
-            tail = None
-            for pair in range(2):
-                result = dot(backward[...], halves[a, pair]) + dot(
-                    backward_low[...], halves[a, pair, 0:112]
-                )
-                for side in range(2):
-                    e = 2 * pair + side
-                    rows = []
-                    for b in range(10):
-                        main = result[8 * b : 8 * b + 8, LANES[side]]
-                        beside = result[80 + 8 * b : 88 + 8 * b, LANES[side]]
-                        moved = jnp.where(
-                            lower_half, pltpu.roll(beside, 1, 1), pltpu.roll(beside, 127, 1)
-                        )
-                        rows.append(main + jnp.where(valid, moved, 0.0))
-                    if tail is not None:
-                        for b in range(3):
-                            rows[b] = rows[b] + tail[b]
-                    for b in range(7):
-                        target[a, 7 * e + b] = rows[b]
-                    tail = rows[7:]
-            for b in range(3):
-                target[a, 28 + b] = tail[b]
-        return carry
-
-    lax.fori_loop(0, count // 2, step, 0)
-
-
-def from_modes(modes, a):
+    def visit(a):
+        tail = None
+        for pair in range(2):
+            result = dot(backward[...], halves[a, pair])
+            result = result[:160] + result[160:]
+            for side in range(2):
+                e = 2 * pair + side
+                rows = [None] * 10
+                for n in range(10):
+                    main = result[8 * n : 8 * n + 8, LANES[side]]
+                    beside = result[80 + 8 * n : 88 + 8 * n, LANES[side]]
+                    moved = jnp.where(
+                        lower_half, pltpu.roll(beside, 1, 1), pltpu.roll(beside, 127, 1)
+                    )
+                    rows[n if n < 5 else 14 - n] = main + jnp.where(valid, moved, 0.0)
+                if tail is not None:
+                    for b in range(3):
+                        rows[b] = rows[b] + tail[b]
+                for b in range(7):
+                    put(a, 7 * e + b, rows[b])
+                tail = rows[7:]
+        for b in range(3):
+            put(a, 28 + b, tail[b])
+
+    over_layers(count, visit, unrolled)
+
+
+def parity_parts(modes, a):
     even = odd = None
     for p in EVEN:
         term = modes[p] * float(HALF_BASIS[a, p])
@@ -635,6 +667,11 @@
     for p in ODD:
         term = modes[p] * float(HALF_BASIS[a, p])
         odd = term if odd is None else odd + term
+    return even, odd
+
+
+def from_modes(modes, a):
+    even, odd = parity_parts(modes, a)
     return even + odd, even - odd
 
 
@@ -654,60 +691,76 @@
 def over_blocks(visit):
     def step(block, carry):
         at = pl.multiple_of(16 * block, 16)
+        split_at = pl.multiple_of(16 * block + 64 * (block // 4), 16)
         for e in range(4):
-            visit(lambda shift=0, e=e: (e // 2, pl.ds(shift + at, 16), LANES[e % 2]))
+            visit(
+                lambda e=e: (e // 2, pl.ds(at, 16), LANES[e % 2]),
+                lambda shift, e=e: (e // 2, pl.ds(split_at + shift, 16), LANES[e % 2]),
+            )
         return carry
 
-    lax.fori_loop(0, 7, step, 0)
-
-
-def store_halves(halves, layer, spot, value):
+    lax.fori_loop(0, 8, step, 0)
+
+
+def store_halves(halves, layer, half, value):
     top, bottom = split(value)
-    halves[(layer,) + spot()] = top
-    halves[(layer,) + spot(112)] = bottom
-
-
-def inner_forward_body(inner, forward_high, forward_low, partial, spectral):
-    forward_layers(inner, 6, forward_high, forward_low, spectral)
-
-    def visit(spot):
+    halves[(layer,) + half(0)] = top
+    halves[(layer,) + half(64)] = bottom
+
+
+def inner_forward_body(inner, forward, reciprocals, partial, shares, spectral):
+    forward_layers(inner, 6, forward, spectral, False)
+
+    def visit(spot, half):
         pairs = [(spectral[(n,) + spot()], spectral[(5 - n,) + spot()]) for n in range(3)]
-        for p, value in enumerate(to_modes(pairs, 2, [None] * 10)):
-            partial[(p,) + spot()] = value
+        values = to_modes(pairs, 2, [None] * 10)
+        for p in range(10):
+            partial[(p,) + spot()] = values[p]
+            values[p] = values[p] * reciprocals[(p,) + spot()]
+        for a in range(2):
+            for parity, value in enumerate(parity_parts(values, a)):
+                shares[(2 * parity + a,) + spot()] = value
 
     over_blocks(visit)
 
 
 def edge_solve_body(
-    place, reciprocals, forward_high, forward_low, backward, backward_low, partial,
-    low, high, first, second, out_low, out_high, out_first, out_second, spectral, edges, halves,
+    place, blocks, forward, backward, shares, low, high, first, second,
+    out_low, out_high, out_first, out_second, spectral, edges, halves,
 ):
     from_low, from_high = arrived(place, first, second)
-
-    def gather(y, carry):
+    for y in range(31):
         edges[0, y] = from_low[0, y]
         edges[1, y] = low[0, y] + from_low[1, y]
         edges[2, y] = high[1, y] + from_high[0, y]
         edges[3, y] = from_high[1, y]
-        return carry
-
-    lax.fori_loop(0, 31, gather, 0, unroll=4)
-    forward_layers(edges, 4, forward_high, forward_low, spectral)
-
-    def visit(spot):
-        values = all_modes(spot, spectral, partial, reciprocals)
+    forward_layers(edges, 4, forward, spectral, True)
+
+    def visit(spot, half):
+        layer = [spectral[(n,) + spot()] for n in range(4)]
+        parts = []
+        for parity, sign in enumerate((1.0, -1.0)):
+            outer, next_outer = layer[0] + sign * layer[3], layer[1] + sign * layer[2]
+            at_00, at_01, at_11 = [blocks[(3 * parity + n,) + spot()] for n in range(3)]
+            parts.append(
+                (
+                    shares[(2 * parity,) + spot()] + (at_00 * outer + at_01 * next_outer),
+                    shares[(2 * parity + 1,) + spot()] + (at_01 * outer + at_11 * next_outer),
+                )
+            )
         for a in range(2):
-            lower, upper = from_modes(values, a)
-            store_halves(halves, a, spot, lower)
-            store_halves(halves, 3 - a, spot, upper)
+            store_halves(halves, a, half, parts[0][a] + parts[1][a])
+            store_halves(halves, 3 - a, half, parts[0][a] - parts[1][a])
 
     over_blocks(visit)
 
-    def back(start, target):
-        backward_layers(halves.at[start : start + 2], 2, backward, backward_low, target)
-
-    back(0, out_low)
-    back(2, out_high)
+    def put(a, y, value):
+        if a < 2:
+            out_low[a, y] = value
+        else:
+            out_high[a - 2, y] = value
+
+    backward_layers(halves, 4, backward, put, True)
     hand_over(place, out_low, out_high, out_first, out_second)
 
 
@@ -717,18 +770,20 @@
     return [values[p] * reciprocals[(p,) + spot()] for p in range(10)]
 
 
-def inner_backward_body(
-    spectral, partial, reciprocals, backward, backward_low, out_inner, halves
-):
-    def visit(spot):
+def inner_backward_body(spectral, partial, reciprocals, backward, out_inner, halves):
+    def visit(spot, half):
         values = all_modes(spot, spectral, partial, reciprocals)
         for n in range(3):
             lower, upper = from_modes(values, n + 2)
-            store_halves(halves, n, spot, lower)
-            store_halves(halves, 5 - n, spot, upper)
+            store_halves(halves, n, half, lower)
+            store_halves(halves, 5 - n, half, upper)
 
     over_blocks(visit)
-    backward_layers(halves, 6, backward, backward_low, out_inner)
+
+    def put(a, y, value):
+        out_inner[a, y] = value
+
+    backward_layers(halves, 6, backward, put, False)
 
 
 def residual_body(place, low, inner, high, first, second, residual, layer, semaphores):
@@ -751,12 +806,11 @@
             after = pltpu.roll(pltpu.roll(value, 7, 0), 127, 1)
             return value + jnp.where(into_first, before, jnp.where(into_last, after, 0.0))
 
-        def step(e, carry, i=i, value_at=value_at):
-            for j in range(8):
-                layer[i, 8 * e + j] = value_at(1 + 7 * e + j)
-            return carry
-
-        lax.fori_loop(0, 4, step, 0)
+        for n in range(29):
+            value = value_at(n + 1)
+            layer[i, column_of(n)] = value
+            if n % 7 == 0 and 0 < n < 28:
+                layer[i, column_of(n) - 1] = value
         copies.append(pltpu.make_async_copy(layer.at[i], residual.at[i], semaphores.at[i]))
         copies[-1].start()
     for copy in copies:
@@ -905,10 +959,12 @@
 
 
 def last_update_body(
-    place, outflow, field, changed, low, inner, high, first, second, result
+    place, outflow, field, changed, low, inner, high, first, second,
+    result, edges, layer, semaphores,
 ):
     top = top_flags()
     parts = (low, inner, high, *arrived(place, first, second))
+    copies = []
     for i in range(8):
         for n in range(29):
             column = column_of(n)
@@ -920,40 +976,66 @@
             else:
                 value = field[i, n + 1]
             value = value + keep * fold_row(i, n + 1, *parts)
-            result[i, column] = value
+            layer[i, column] = value
             if n % 7 == 0 and 0 < n < 28:
-                result[i, column - 1] = value
-
-
-def last_join_body(place, outflow, before, low_news, high_news, result, edges, semaphores):
-    copies = [
-        pltpu.make_async_copy(before.at[:, 2:30], result.at[:, 2:30], semaphores.at[0]),
-        pltpu.make_async_copy(edges.at[:, 0:2], result.at[:, 0:2], semaphores.at[1]),
-        pltpu.make_async_copy(edges.at[:, 2:4], result.at[:, 30:32], semaphores.at[2]),
-    ]
-    copies[0].start()
+                layer[i, column - 1] = value
+            if n < 2:
+                edges[i, n] = value
+            if n > 26:
+                edges[i, n - 25] = value
+        copies.append(
+            pltpu.make_async_copy(layer.at[i], result.at[i], semaphores.at[i])
+        )
+        copies[-1].start()
+    for copy in copies:
+        copy.wait()
+
+
+def last_update(place, outflow, field, changed, solved):
+    return pl.pallas_call(
+        last_update_body,
+        out_shape=(layers(8, 32), layers(8, 4)),
+        in_specs=[whole(pltpu.SMEM)] * 2 + [whole()] * 7,
+        out_specs=(whole(pltpu.HBM), whole()),
+        scratch_shapes=[pltpu.VMEM((8, 32, 8, 128), F32), pltpu.SemaphoreType.DMA((8,))],
+        compiler_params=pltpu.CompilerParams(vmem_limit_bytes=VMEM_BYTES),
+        cost_estimate=pl.CostEstimate(flops=10**7, bytes_accessed=2**22, transcendentals=0),
+        name="last_update",
+    )(place, outflow, field, changed, *solved)
+
+
+def last_join_body(
+    place, outflow, edges, low_news, high_news, before, result, rows, semaphores
+):
     top = top_flags()
+    copies = []
     low_flag, high_flag = ends(place, 1)
     for first, at, flag, news in ((0, 0, low_flag, low_news), (30, 2, high_flag, high_news)):
         for i in range(8):
             for n in range(2):
                 keep = own_keep(outflow, top, i, first + n)
-                edges[i, at + n] = before[i, first + n] + keep * (flag * news[i, n])
-        copies[1 + at // 2].start()
+                rows[i, at + n] = edges[i, at + n] + keep * (flag * news[i, n])
+        copies.append(
+            pltpu.make_async_copy(
+                rows.at[:, at : at + 2], result.at[:, first : first + 2], semaphores.at[at // 2]
+            )
+        )
+        copies[-1].start()
     for copy in copies:
         copy.wait()
 
 
-def last_join(place, outflow, before, low_news, high_news):
+def last_join(place, outflow, edges, low_news, high_news, before):
     return pl.pallas_call(
         last_join_body,
         out_shape=layers(8, 32),
-        in_specs=[whole(pltpu.SMEM), whole(pltpu.SMEM), whole(), whole(), whole()],
+        in_specs=[whole(pltpu.SMEM)] * 2 + [whole()] * 3 + [whole(pltpu.HBM)],
         out_specs=whole(pltpu.HBM),
-        scratch_shapes=[pltpu.VMEM((8, 4, 8, 128), F32), pltpu.SemaphoreType.DMA((3,))],
+        scratch_shapes=[pltpu.VMEM((8, 4, 8, 128), F32), pltpu.SemaphoreType.DMA((2,))],
+        input_output_aliases={5: 0},
         compiler_params=pltpu.CompilerParams(vmem_limit_bytes=VMEM_BYTES),
         name="last_join",
-    )(place, outflow, before, low_news, high_news)
+    )(place, outflow, edges, low_news, high_news, before)
 
 
 def exchange(to_low, to_high, axis):
@@ -983,30 +1065,29 @@
 
 
 def solve(place, reciprocals, edge_parts, make_inner, beside):
-    forward = [jnp.asarray(t) for t in FORWARD]
-    backward = [jnp.asarray(t) for t in BACKWARD]
+    forward, backward = jnp.asarray(FORWARD), jnp.asarray(BACKWARD)
     low, high, first, second = edge_parts
     received = exchange_along_first(first, second)
     inner = make_inner()
-    (partial,) = call(
-        inner_forward_body, [modes_shape(10, 112, F32)], 0,
-        [pltpu.VMEM((6, 2, 112, 256), F32)], "inner_forward",
-        (inner, *forward), 3 * 10**8,
+    partial, shares = call(
+        inner_forward_body, [modes_shape(10, 128, F32), modes_shape(4, 128, F32)], 0,
+        [pltpu.VMEM((6, 2, 128, 256), F32)], "inner_forward",
+        (inner, forward, reciprocals[0]), 3 * 10**8,
     )
     out_low, out_high, first, second, spectral = call(
         edge_solve_body,
-        [layers(2, 31)] * 4 + [modes_shape(4, 112, F32)],
+        [layers(2, 31)] * 4 + [modes_shape(4, 128, F32)],
         1,
-        [pltpu.VMEM((4, 31, 8, 128), F32), pltpu.VMEM((4, 2, 224, 256), BF16)],
+        [pltpu.VMEM((4, 31, 8, 128), F32), pltpu.VMEM((4, 2, 256, 256), BF16)],
         "edge_solve",
-        (place, reciprocals, *forward, *backward, partial, low, high, *received),
+        (place, reciprocals[1], forward, backward, shares, low, high, *received),
         10**9,
     )
     returned = exchange_along_first(first, second)
     (out_inner,) = call(
         inner_backward_body, [layers(6, 31)], 0,
-        [pltpu.VMEM((6, 2, 224, 256), BF16)], "inner_backward",
-        (spectral, partial, reciprocals, *backward), 3 * 10**8,
+        [pltpu.VMEM((6, 2, 256, 256), BF16)], "inner_backward",
+        (spectral, partial, reciprocals[0], backward), 3 * 10**8,
     )
     extra = beside(inner, received)
     if extra is not None:
@@ -1036,15 +1117,19 @@
     )
     from_low, from_high = exchange(to_low, to_high, "inner")
 
-    def own_image(wanted, name, start, source):
+    def own_image(wanted, name, coefficients, start, source, table, kept):
         return call(
-            functools.partial(own_image_body, wanted), [layers(8, 31), layers(8, 31)], 1,
+            functools.partial(own_image_body, wanted), [layers(8, 31), layers(8, 31), *kept], 1,
             [plane_scratch()], name, (place, coefficients, start, source, table), 10**8,
         )
 
-    edge_image, edge_source = own_image(EDGES, "own_edges", start, source)
-    (reciprocals,) = call(
-        reciprocal_body, [modes_shape(10, 112, F32)], 0, [], "reciprocals",
+    edge_image, edge_source, table, coefficients = own_image(
+        EDGES, "own_edges", coefficients, start, source, table,
+        [jax.ShapeDtypeStruct(a.shape, a.dtype) for a in (table, coefficients)],
+    )
+    reciprocals = call(
+        reciprocal_body, [modes_shape(10, 128, F32), modes_shape(6, 128, F32)], 0, [],
+        "reciprocals",
         (coefficients, *[jnp.asarray(t) for t in VALUES]), 10**8,
     )
     joined = (place, outflow, start, from_low, from_high, table)
@@ -1056,7 +1141,9 @@
         join_scratch, "first_edges", (*joined, edge_image, edge_source), 10**8,
     )
     late_start, late_source, *edge_parts = lax.optimization_barrier((start, source, *edge_parts))
-    inner_image, inner_source = own_image(INNER, "own_inner", late_start, late_source)
+    inner_image, inner_source = own_image(
+        INNER, "own_inner", coefficients, late_start, late_source, table, []
+    )
 
     def first_inner_body(*refs):
         count = len(joined) + 2
@@ -1098,11 +1185,8 @@
         lambda inner, received: residual_out(place, low, inner, high, received),
     )
     news = exchange(*fold(2, place, outflow, solved), "inner")
-    (iterate,) = call(
-        last_update_body, [layers(8, 32)], 2, [], "last_update",
-        (place, outflow, field, changed, *solved), 10**7,
-    )
-    return last_join(place, outflow, iterate, *news), residual
+    iterate, edges = last_update(place, outflow, field, changed, solved)
+    return last_join(place, outflow, edges, *news, iterate), residual
 
 
 def solution(mesh):

time: 79 us -> 73.7 us (0.933)
  Pallas kernels: 38.5 us -> 31.5 us
  waiting for transfers between devices: 20.6 us -> 23.6 us
  local copies, waits for them, and re-layouts: 2.53 us -> 1.62 us
    pallas_call x17 -> x16, Pallas kernels: 30.8 us -> 24.6 us  [call(): pl.pallas_call(body, out_shape=tuple(outs), in_specs=[whole(pltpu.SMEM if...]
    pallas_call x1, Pallas kernels: 4.07 us -> 1.84 us  [residual_out(): pl.pallas_call(residual_body, out_shape=layers(8, 32), in_specs=[whole(pl...]
    ppermute x4, waiting for transfers between devices: 4.17 us -> 5.95 us  [exchange_along_first(): lax.ppermute(first, axes, forward)]
    pallas_call x0 -> x1, Pallas kernels: none -> 1.68 us  [last_update(): pl.pallas_call(last_update_body, out_shape=(layers(8, 32), layers(8, 4)),...]
    ppermute x4, waiting for transfers between devices: 7.22 us -> 8.36 us  [exchange_along_first(): lax.ppermute(second, axes, backward)]
    ppermute x3, waiting for transfers between devices: 1.46 us -> 2.59 us  [exchange(): lax.ppermute(to_high, axis, upward)]
    ppermute x3, waiting for transfers between devices: 7.71 us -> 6.71 us  [exchange(): lax.ppermute(to_low, axis, downward)]
    unnamed x28 -> x18, local copies, waits for them, and re-layouts: 2.53 us -> 1.62 us
  transfers between devices with their start and end apart: 14 -> 14, of which waited for: 12 -> 13; matrix products, arithmetic and copies ran while one was open for 0% -> 0% of each run, Pallas kernels for 30% -> 28%
where the time goes in v3:
time: 73.7 us; the launch traced here: 72.9 us
  Pallas kernels  31.5 us (43%)
  waiting for transfers between devices  23.6 us (32%)
  starting transfers between devices  15.3 us (21%)
  local copies, waits for them, and re-layouts  1.62 us (2%)
  between operations  0.87 us (1%)
    pallas_call x16, Pallas kernels, call(): pl.pallas_call(body, out_shape=tuple(outs), in_specs=[whole(pltpu.SMEM if...  24.6 us
    ppermute x4, starting transfers between devices, exchange_along_first(): lax.ppermute(first, axes, forward)  12.5 us
    ppermute x4, waiting for transfers between devices, exchange_along_first(): lax.ppermute(second, axes, backward)  8.36 us
    ppermute x3, waiting for transfers between devices, exchange(): lax.ppermute(to_low, axis, downward)  6.71 us
    ppermute x4, waiting for transfers between devices, exchange_along_first(): lax.ppermute(first, axes, forward)  5.95 us
    ppermute x3, waiting for transfers between devices, exchange(): lax.ppermute(to_high, axis, upward)  2.59 us
    pallas_call x1, Pallas kernels, pack_first(): pl.pallas_call(pack_body, out_shape=(layers(8, 9), layers(8, 9)), in_spec...  2.01 us
    pallas_call x1, Pallas kernels, residual_out(): pl.pallas_call(residual_body, out_shape=layers(8, 32), in_specs=[whole(pl...  1.84 us
  transfers between devices with their start and end apart: 14, of which 13 were waited for; matrix products, arithmetic and copies ran while one was open for 0% of the time, Pallas kernels for 28%

profile of v3, /device:TPU:25, one launch (start us, length us, event | category | flops | bytes accessed | tf_op | source)
XLA Modules:
  0.0 72.9 jit_solution(7895644287614440512)
XLA Ops:
  0.7 2.0 %pack_first.1 = (f32[8,9,8,128]{3,2,1,0:T(8,128)}, f32[8,9,8,128]{3,2,1,0:T(8,128)}) custom-call(s32[8,32]{1,0:T(8,128)} %outflow.17, f32[8,32,8,128]{3,2,1,0:T(8,128)} %start.5, f32[8,32,8,128]{3,2,1,0:T(8,128)} %source.3, f32[3,1,4,128]{3,2,1,0:T(4,128)} %coefficients.2), custom_call_target="tpu_custom_call" | custom-call | tf_op jit(solution)/shard_map/pack_first/pallas_call | solution.py:319
  2.7 1.8 %collective-permute-start = (f32[8,9,8,128]{3,2,1,0:T(8,128)}, f32[8,9,8,128]{3,2,1,0:T(8,128)S(1)}, u32[]{:S(2)}, u32[]{:S(2)}) collective-permute-start(f32[8,9,8,128]{3,2,1,0:T(8,128)} %get-tuple-element.65), channel_id=1, source_target_pairs={{0,1},{1,2},{2,3},{3,4},{4,5},{5,6},{6,7},{7,0},{8,9},{9,10},{10,1... | collective-permute-start | bytes 884744 | tf_op jit(solution)/shard_map/ppermute | solution.py:1045
  8.4 2.4 %collective-permute-done.1.from_high.refs_4_ = f32[8,9,8,128]{3,2,1,0:T(8,128)S(1)} collective-permute-done((f32[8,9,8,128]{3,2,1,0:T(8,128)}, f32[8,9,8,128]{3,2,1,0:T(8,128)S(1)}, u32[]{:S(2)}, u32[]{:S(2)}) %collective-permute-start.1) | collective-permute-done | bytes 294944 | tf_op jit(solution)/shard_map/ppermute | solution.py:1045
  11.7 4.0 %collective-permute-start.2 = (f32[2,31,8,128]{3,2,1,0:T(8,128)S(1)}, f32[2,31,8,128]{3,2,1,0:T(8,128)S(1)}, u32[]{:S(2)}, u32[]{:S(2)}) collective-permute-start(f32[2,31,8,128]{3,2,1,0:T(8,128)S(1)} %get-tuple-element.81), channel_id=1, source_target_pairs={{0,8},{8,16},{16,24},{24,32},{32,40},{40,48},{48,56},{56,64},{64,7... | collective-permute-start | bytes 761864 | tf_op jit(solution)/shard_map/ppermute | solution.py:1060
  18.5 2.2 %inner_forward.2 = (f32[10,2,128,256]{3,2,1,0:T(8,128)S(1)}, f32[4,2,128,256]{3,2,1,0:T(8,128)S(1)}) custom-call(f32[6,31,8,128]{3,2,1,0:T(8,128)S(1)} %first_inner.1.inner, bf16[128,240]{1,0:T(8,128)(2,1)S(1)} %copy-done.3, f32[10,2,128,256]{3,2,1,0:T(8,128)S(1)} %get-tuple-element.79.reciprocals), custom_call_target="tpu_custom_call" | custom-call | flops 300000000 | bytes 7176192 | tf_op jit(solution)/shard_map/inner_forward/pallas_call | solution.py:267
  21.0 1.9 %collective-permute-done.3.second = f32[2,31,8,128]{3,2,1,0:T(8,128)S(1)} collective-permute-done((f32[2,31,8,128]{3,2,1,0:T(8,128)S(1)}, f32[2,31,8,128]{3,2,1,0:T(8,128)S(1)}, u32[]{:S(2)}, u32[]{:S(2)}) %collective-permute-start.3) | collective-permute-done | bytes 253984 | tf_op jit(solution)/shard_map/ppermute | solution.py:1060
  23.0 2.4 %edge_solve.2 = (f32[2,31,8,128]{3,2,1,0:T(8,128)S(1)}, f32[2,31,8,128]{3,2,1,0:T(8,128)S(1)}, f32[2,31,8,128]{3,2,1,0:T(8,128)S(1)}, f32[2,31,8,128]{3,2,1,0:T(8,128)S(1)}, f32[4,2,128,256]{3,2,1,0:T(8,128)S(1)}) custom-call(s32[4]{0:T(128)S(1)} %pad_add_fusion.place.refs_0_, f32[6,2,128,256]{3,2,1,0:T(8,128)S(1)} %get-tuple-element.64.blocks, ...), custom_call_target="tpu_custom_call" | custom-call | flops 1000000000 | bytes 6152208 | tf_op jit(solution)/shard_map/edge_solve/pallas_call | solution.py:267
  25.4 2.5 %collective-permute-start.4 = (f32[2,31,8,128]{3,2,1,0:T(8,128)S(1)}, f32[2,31,8,128]{3,2,1,0:T(8,128)S(1)}, u32[]{:S(2)}, u32[]{:S(2)}) collective-permute-start(f32[2,31,8,128]{3,2,1,0:T(8,128)S(1)} %get-tuple-element.87), channel_id=1, source_target_pairs={{0,8},{8,16},{16,24},{24,32},{32,40},{40,48},{48,56},{56,64},{64,7... | collective-permute-start | bytes 761864 | tf_op jit(solution)/shard_map/ppermute | solution.py:1060
  27.8 2.7 %inner_backward.2.inner = f32[6,31,8,128]{3,2,1,0:T(8,128)S(1)} custom-call(f32[4,2,128,256]{3,2,1,0:T(8,128)S(1)} %get-tuple-element.84.spectral, f32[10,2,128,256]{3,2,1,0:T(8,128)S(1)} %get-tuple-element.85.partial, f32[10,2,128,256]{3,2,1,0:T(8,128)S(1)} %get-tuple-element.79.reciprocals, bf16[320,256]{1,0:T(8,128)(2,1)S(1)} %copy-done.2), custom_call_target="tpu_custom_call" | custom-call | flops 300000000 | bytes 7380992 | tf_op jit(solution)/shard_map/inner_backward/pallas_call | solution.py:267
  30.6 2.8 %collective-permute-done.4.first = f32[2,31,8,128]{3,2,1,0:T(8,128)S(1)} collective-permute-done((f32[2,31,8,128]{3,2,1,0:T(8,128)S(1)}, f32[2,31,8,128]{3,2,1,0:T(8,128)S(1)}, u32[]{:S(2)}, u32[]{:S(2)}) %collective-permute-start.4) | collective-permute-done | bytes 253984 | tf_op jit(solution)/shard_map/ppermute | solution.py:1060
  33.4 2.0 %collective-permute-done.5.second = f32[2,31,8,128]{3,2,1,0:T(8,128)S(1)} collective-permute-done((f32[2,31,8,128]{3,2,1,0:T(8,128)S(1)}, f32[2,31,8,128]{3,2,1,0:T(8,128)S(1)}, u32[]{:S(2)}, u32[]{:S(2)}) %collective-permute-start.5) | collective-permute-done | bytes 253984 | tf_op jit(solution)/shard_map/ppermute | solution.py:1060
  36.7 1.8 %update.1 = (f32[8,31,8,128]{3,2,1,0:T(8,128)S(1)}, f32[8,15,8,128]{3,2,1,0:T(8,128)S(1)}) custom-call(s32[4]{0:T(128)S(1)} %pad_add_fusion.place.refs_0_, s32[8,32]{1,0:T(8,128)S(1)} %copy-done.4, f32[8,32,8,128]{3,2,1,0:T(8,128)S(1)} %copy-done, f32[3,1,4,128]{3,2,1,0:T(4,128)S(1)} %get-tuple-element.62.coefficients, ...), custom_call_target="tpu_custom_call" | custom-call | flops 200000000 | bytes 4488208 | tf_op jit(solution)/shard_map/update/pallas_call | solution.py:267
  39.8 2.7 %collective-permute-done.7.high_news = f32[8,9,8,128]{3,2,1,0:T(8,128)S(1)} collective-permute-done((f32[8,9,8,128]{3,2,1,0:T(8,128)S(1)}, f32[8,9,8,128]{3,2,1,0:T(8,128)S(1)}, u32[]{:S(2)}, u32[]{:S(2)}) %collective-permute-start.7) | collective-permute-done | bytes 294944 | tf_op jit(solution)/shard_map/ppermute | solution.py:1045
  43.6 3.8 %collective-permute-start.8 = (f32[2,31,8,128]{3,2,1,0:T(8,128)S(1)}, f32[2,31,8,128]{3,2,1,0:T(8,128)S(1)}, u32[]{:S(2)}, u32[]{:S(2)}) collective-permute-start(f32[2,31,8,128]{3,2,1,0:T(8,128)S(1)} %get-tuple-element.98), channel_id=1, source_target_pairs={{0,8},{8,16},{16,24},{24,32},{32,40},{40,48},{48,56},{56,64},{64,7... | collective-permute-start | bytes 761864 | tf_op jit(solution)/shard_map/ppermute | solution.py:1060
  48.4 2.2 %inner_forward.3 = (f32[10,2,128,256]{3,2,1,0:T(8,128)S(1)}, f32[4,2,128,256]{3,2,1,0:T(8,128)S(1)}) custom-call(f32[6,31,8,128]{3,2,1,0:T(8,128)S(1)} %second_inner.1.inner, bf16[128,240]{1,0:T(8,128)(2,1)S(1)} %copy-done.3, f32[10,2,128,256]{3,2,1,0:T(8,128)S(1)} %get-tuple-element.79.reciprocals), custom_call_target="tpu_custom_call" | custom-call | flops 300000000 | bytes 7176192 | tf_op jit(solution)/shard_map/inner_forward/pallas_call | solution.py:267
  50.7 1.7 %collective-permute-done.8.first = f32[2,31,8,128]{3,2,1,0:T(8,128)S(1)} collective-permute-done((f32[2,31,8,128]{3,2,1,0:T(8,128)S(1)}, f32[2,31,8,128]{3,2,1,0:T(8,128)S(1)}, u32[]{:S(2)}, u32[]{:S(2)}) %collective-permute-start.8) | collective-permute-done | bytes 253984 | tf_op jit(solution)/shard_map/ppermute | solution.py:1060
  52.4 2.2 %collective-permute-done.9.second = f32[2,31,8,128]{3,2,1,0:T(8,128)S(1)} collective-permute-done((f32[2,31,8,128]{3,2,1,0:T(8,128)S(1)}, f32[2,31,8,128]{3,2,1,0:T(8,128)S(1)}, u32[]{:S(2)}, u32[]{:S(2)}) %collective-permute-start.9) | collective-permute-done | bytes 253984 | tf_op jit(solution)/shard_map/ppermute | solution.py:1060
  54.7 2.4 %edge_solve.3 = (f32[2,31,8,128]{3,2,1,0:T(8,128)S(1)}, f32[2,31,8,128]{3,2,1,0:T(8,128)S(1)}, f32[2,31,8,128]{3,2,1,0:T(8,128)S(1)}, f32[2,31,8,128]{3,2,1,0:T(8,128)S(1)}, f32[4,2,128,256]{3,2,1,0:T(8,128)S(1)}) custom-call(s32[4]{0:T(128)S(1)} %pad_add_fusion.place.refs_0_, f32[6,2,128,256]{3,2,1,0:T(8,128)S(1)} %get-tuple-element.64.blocks, ...), custom_call_target="tpu_custom_call" | custom-call | flops 1000000000 | bytes 6152208 | tf_op jit(solution)/shard_map/edge_solve/pallas_call | solution.py:267
  57.1 2.1 %collective-permute-start.10 = (f32[2,31,8,128]{3,2,1,0:T(8,128)S(1)}, f32[2,31,8,128]{3,2,1,0:T(8,128)S(1)}, u32[]{:S(2)}, u32[]{:S(2)}) collective-permute-start(f32[2,31,8,128]{3,2,1,0:T(8,128)S(1)} %get-tuple-element.105), channel_id=1, source_target_pairs={{0,8},{8,16},{16,24},{24,32},{32,40},{40,48},{48,56},{56,64},{64,7... | collective-permute-start | bytes 761864 | tf_op jit(solution)/shard_map/ppermute | solution.py:1060
  59.2 1.8 %residual.1 = f32[8,32,8,128]{3,2,1,0:T(8,128)} custom-call(s32[4]{0:T(128)S(1)} %pad_add_fusion.place.refs_0_, f32[2,31,8,128]{3,2,1,0:T(8,128)S(1)} %get-tuple-element.95.low, f32[6,31,8,128]{3,2,1,0:T(8,128)S(1)} %second_inner.1.inner, f32[2,31,8,128]{3,2,1,0:T(8,128)S(1)} %get-tuple-element.96.high, f32[2,31,8,128]{3,2,1,0:T(8,128)S(1)} %collective-permute-done.8.first, ...), custom_call_target="tpu_custom_call" | custom-call | flops 10000000 | bytes 4194304 | tf_op jit(solution)/shard_map/residual/pallas_call | solution.py:821
  61.1 2.7 %inner_backward.3.inner = f32[6,31,8,128]{3,2,1,0:T(8,128)S(1)} custom-call(f32[4,2,128,256]{3,2,1,0:T(8,128)S(1)} %get-tuple-element.101.spectral, f32[10,2,128,256]{3,2,1,0:T(8,128)S(1)} %get-tuple-element.102.partial, f32[10,2,128,256]{3,2,1,0:T(8,128)S(1)} %get-tuple-element.79.reciprocals, bf16[320,256]{1,0:T(8,128)(2,1)S(1)} %copy-done.2), custom_call_target="tpu_custom_call" | custom-call | flops 300000000 | bytes 7380992 | tf_op jit(solution)/shard_map/inner_backward/pallas_call | solution.py:267
  64.9 2.2 %collective-permute-done.11.second = f32[2,31,8,128]{3,2,1,0:T(8,128)S(1)} collective-permute-done((f32[2,31,8,128]{3,2,1,0:T(8,128)S(1)}, f32[2,31,8,128]{3,2,1,0:T(8,128)S(1)}, u32[]{:S(2)}, u32[]{:S(2)}) %collective-permute-start.11) | collective-permute-done | bytes 253984 | tf_op jit(solution)/shard_map/ppermute | solution.py:1060
  68.3 1.7 %last_update.1 = (f32[8,32,8,128]{3,2,1,0:T(8,128)}, f32[8,4,8,128]{3,2,1,0:T(8,128)S(1)}) custom-call(s32[4]{0:T(128)S(1)} %pad_add_fusion.place.refs_0_, s32[8,32]{1,0:T(8,128)S(1)} %copy-done.4, f32[8,31,8,128]{3,2,1,0:T(8,128)S(1)} %get-tuple-element.89.field, f32[8,4,8,128]{3,2,1,0:T(8,128)S(1)} %get-tuple-element.93.changed, ...), custom_call_target="tpu_custom_call" | custom-call | flops 10000000 | bytes 4194304 | tf_op jit(solution)/shard_map/last_update/pallas_call | solution.py:995
  70.0 1.7 %collective-permute-done.13.high_news = f32[8,2,8,128]{3,2,1,0:T(8,128)S(1)} collective-permute-done((f32[8,2,8,128]{3,2,1,0:T(8,128)S(1)}, f32[8,2,8,128]{3,2,1,0:T(8,128)S(1)}, u32[]{:S(2)}, u32[]{:S(2)}) %collective-permute-start.13) | collective-permute-done | bytes 65568 | tf_op jit(solution)/shard_map/ppermute | solution.py:1045
  (43 shorter events, 16.1 us)
Async XLA Ops:
  0.6 10.2 %copy-start.4 = (s32[8,32]{1,0:T(8,128)S(1)}, s32[8,32]{1,0:T(8,128)}, u32[]{:S(2)}) copy-start(s32[8,32]{1,0:T(8,128)} %outflow.17) | copy-start | bytes 3076
  0.6 3.9 %copy-start.1 = (f32[8,32,8,128]{3,2,1,0:T(8,128)S(1)}, f32[8,32,8,128]{3,2,1,0:T(8,128)}, u32[]{:S(2)}) copy-start(f32[8,32,8,128]{3,2,1,0:T(8,128)} %source.3) | copy-start | bytes 3145732
  0.6 3.9 %copy-start = (f32[8,32,8,128]{3,2,1,0:T(8,128)S(1)}, f32[8,32,8,128]{3,2,1,0:T(8,128)}, u32[]{:S(2)}) copy-start(f32[8,32,8,128]{3,2,1,0:T(8,128)} %start.5) | copy-start | bytes 3145732
  2.7 5.8 %collective-permute-start = (f32[8,9,8,128]{3,2,1,0:T(8,128)}, f32[8,9,8,128]{3,2,1,0:T(8,128)S(1)}, u32[]{:S(2)}, u32[]{:S(2)}) collective-permute-start(f32[8,9,8,128]{3,2,1,0:T(8,128)} %get-tuple-element.65), channel_id=1, source_target_pairs={{0,1},{1,2},{2,3},{3,4},{4,5},{5,6},{6,7},{7,0},{8,9},{9,10},{10,1... | collective-permute-start | bytes 884744 | tf_op jit(solution)/shard_map/ppermute | solution.py:1045
  4.5 6.4 %collective-permute-start.1 = (f32[8,9,8,128]{3,2,1,0:T(8,128)}, f32[8,9,8,128]{3,2,1,0:T(8,128)S(1)}, u32[]{:S(2)}, u32[]{:S(2)}) collective-permute-start(f32[8,9,8,128]{3,2,1,0:T(8,128)} %get-tuple-element.66), channel_id=1, source_target_pairs={{1,0},{2,1},{3,2},{4,3},{5,4},{6,5},{7,6},{0,7},{9,8},{10,9},{11,1... | collective-permute-start | bytes 884744 | tf_op jit(solution)/shard_map/ppermute | solution.py:1045
  4.5 0.9 %copy-start.5 = (bf16[192,192]{1,0:T(8,128)(2,1)S(1)}, bf16[192,192]{1,0:T(8,128)(2,1)}, u32[]{:S(2)}) copy-start(bf16[192,192]{1,0:T(8,128)(2,1)} %constant.23.clone.table) | copy-start | bytes 221188
  5.4 0.7 copy-start.6
  6.1 9.6 %copy-start.7 = (f32[128,128]{1,0:T(8,128)S(1)}, f32[128,128]{1,0:T(8,128)}, u32[]{:S(2)}) copy-start(f32[128,128]{1,0:T(8,128)} %constant.25.clone.third_values) | copy-start | bytes 196612
  6.1 9.6 %copy-start.8 = (f32[128,128]{1,0:T(8,128)S(1)}, f32[128,128]{1,0:T(8,128)}, u32[]{:S(2)}) copy-start(f32[128,128]{1,0:T(8,128)} %constant.24.clone.second_values) | copy-start | bytes 196612
  11.7 9.3 %collective-permute-start.2 = (f32[2,31,8,128]{3,2,1,0:T(8,128)S(1)}, f32[2,31,8,128]{3,2,1,0:T(8,128)S(1)}, u32[]{:S(2)}, u32[]{:S(2)}) collective-permute-start(f32[2,31,8,128]{3,2,1,0:T(8,128)S(1)} %get-tuple-element.81), channel_id=1, source_target_pairs={{0,8},{8,16},{16,24},{24,32},{32,40},{40,48},{48,56},{56,64},{64,7... | collective-permute-start | bytes 761864 | tf_op jit(solution)/shard_map/ppermute | solution.py:1060
  15.7 7.2 %collective-permute-start.3 = (f32[2,31,8,128]{3,2,1,0:T(8,128)S(1)}, f32[2,31,8,128]{3,2,1,0:T(8,128)S(1)}, u32[]{:S(2)}, u32[]{:S(2)}) collective-permute-start(f32[2,31,8,128]{3,2,1,0:T(8,128)S(1)} %get-tuple-element.82), channel_id=1, source_target_pairs={{8,0},{16,8},{24,16},{32,24},{40,32},{48,40},{56,48},{64,56},{72,6... | collective-permute-start | bytes 761864 | tf_op jit(solution)/shard_map/ppermute | solution.py:1060
  17.6 0.9 %copy-start.3 = (bf16[128,240]{1,0:T(8,128)(2,1)S(1)}, bf16[128,240]{1,0:T(8,128)(2,1)}, u32[]{:S(2)}) copy-start(bf16[128,240]{1,0:T(8,128)(2,1)} %constant.26.clone.forward) | copy-start | bytes 184324
  18.5 4.5 %copy-start.2 = (bf16[320,256]{1,0:T(8,128)(2,1)S(1)}, bf16[320,256]{1,0:T(8,128)(2,1)}, u32[]{:S(2)}) copy-start(bf16[320,256]{1,0:T(8,128)(2,1)} %constant.27.clone.backward) | copy-start | bytes 491524
  25.4 8.0 %collective-permute-start.4 = (f32[2,31,8,128]{3,2,1,0:T(8,128)S(1)}, f32[2,31,8,128]{3,2,1,0:T(8,128)S(1)}, u32[]{:S(2)}, u32[]{:S(2)}) collective-permute-start(f32[2,31,8,128]{3,2,1,0:T(8,128)S(1)} %get-tuple-element.87), channel_id=1, source_target_pairs={{0,8},{8,16},{16,24},{24,32},{32,40},{40,48},{48,56},{56,64},{64,7... | collective-permute-start | bytes 761864 | tf_op jit(solution)/shard_map/ppermute | solution.py:1060
  27.8 7.6 %collective-permute-start.5 = (f32[2,31,8,128]{3,2,1,0:T(8,128)S(1)}, f32[2,31,8,128]{3,2,1,0:T(8,128)S(1)}, u32[]{:S(2)}, u32[]{:S(2)}) collective-permute-start(f32[2,31,8,128]{3,2,1,0:T(8,128)S(1)} %get-tuple-element.88), channel_id=1, source_target_pairs={{8,0},{16,8},{24,16},{32,24},{40,32},{48,40},{56,48},{64,56},{72,6... | collective-permute-start | bytes 761864 | tf_op jit(solution)/shard_map/ppermute | solution.py:1060
  36.1 3.7 %collective-permute-start.6 = (f32[8,9,8,128]{3,2,1,0:T(8,128)S(1)}, f32[8,9,8,128]{3,2,1,0:T(8,128)S(1)}, u32[]{:S(2)}, u32[]{:S(2)}) collective-permute-start(f32[8,9,8,128]{3,2,1,0:T(8,128)S(1)} %get-tuple-element.91), channel_id=1, source_target_pairs={{0,1},{1,2},{2,3},{3,4},{4,5},{5,6},{6,7},{7,0},{8,9},{9,10},{10,1... | collective-permute-start | bytes 884744 | tf_op jit(solution)/shard_map/ppermute | solution.py:1045
  36.2 6.3 %collective-permute-start.7 = (f32[8,9,8,128]{3,2,1,0:T(8,128)S(1)}, f32[8,9,8,128]{3,2,1,0:T(8,128)S(1)}, u32[]{:S(2)}, u32[]{:S(2)}) collective-permute-start(f32[8,9,8,128]{3,2,1,0:T(8,128)S(1)} %get-tuple-element.92), channel_id=1, source_target_pairs={{1,0},{2,1},{3,2},{4,3},{5,4},{6,5},{7,6},{0,7},{9,8},{10,9},{11,1... | collective-permute-start | bytes 884744 | tf_op jit(solution)/shard_map/ppermute | solution.py:1045
  43.6 8.9 %collective-permute-start.8 = (f32[2,31,8,128]{3,2,1,0:T(8,128)S(1)}, f32[2,31,8,128]{3,2,1,0:T(8,128)S(1)}, u32[]{:S(2)}, u32[]{:S(2)}) collective-permute-start(f32[2,31,8,128]{3,2,1,0:T(8,128)S(1)} %get-tuple-element.98), channel_id=1, source_target_pairs={{0,8},{8,16},{16,24},{24,32},{32,40},{40,48},{48,56},{56,64},{64,7... | collective-permute-start | bytes 761864 | tf_op jit(solution)/shard_map/ppermute | solution.py:1060
  47.4 7.2 %collective-permute-start.9 = (f32[2,31,8,128]{3,2,1,0:T(8,128)S(1)}, f32[2,31,8,128]{3,2,1,0:T(8,128)S(1)}, u32[]{:S(2)}, u32[]{:S(2)}) collective-permute-start(f32[2,31,8,128]{3,2,1,0:T(8,128)S(1)} %get-tuple-element.99), channel_id=1, source_target_pairs={{8,0},{16,8},{24,16},{32,24},{40,32},{48,40},{56,48},{64,56},{72,6... | collective-permute-start | bytes 761864 | tf_op jit(solution)/shard_map/ppermute | solution.py:1060
  57.1 7.9 %collective-permute-start.10 = (f32[2,31,8,128]{3,2,1,0:T(8,128)S(1)}, f32[2,31,8,128]{3,2,1,0:T(8,128)S(1)}, u32[]{:S(2)}, u32[]{:S(2)}) collective-permute-start(f32[2,31,8,128]{3,2,1,0:T(8,128)S(1)} %get-tuple-element.105), channel_id=1, source_target_pairs={{0,8},{8,16},{16,24},{24,32},{32,40},{40,48},{48,56},{56,64},{64,7... | collective-permute-start | bytes 761864 | tf_op jit(solution)/shard_map/ppermute | solution.py:1060
  59.2 7.9 %collective-permute-start.11 = (f32[2,31,8,128]{3,2,1,0:T(8,128)S(1)}, f32[2,31,8,128]{3,2,1,0:T(8,128)S(1)}, u32[]{:S(2)}, u32[]{:S(2)}) collective-permute-start(f32[2,31,8,128]{3,2,1,0:T(8,128)S(1)} %get-tuple-element.106), channel_id=1, source_target_pairs={{8,0},{16,8},{24,16},{32,24},{40,32},{48,40},{56,48},{64,56},{72,6... | collective-permute-start | bytes 761864 | tf_op jit(solution)/shard_map/ppermute | solution.py:1060
  67.7 2.2 %collective-permute-start.12 = (f32[8,2,8,128]{3,2,1,0:T(8,128)S(1)}, f32[8,2,8,128]{3,2,1,0:T(8,128)S(1)}, u32[]{:S(2)}, u32[]{:S(2)}) collective-permute-start(f32[8,2,8,128]{3,2,1,0:T(8,128)S(1)} %get-tuple-element.108), channel_id=1, source_target_pairs={{0,1},{1,2},{2,3},{3,4},{4,5},{5,6},{6,7},{7,0},{8,9},{9,10},{10,1... | collective-permute-start | bytes 196616 | tf_op jit(solution)/shard_map/ppermute | solution.py:1045
  67.8 3.9 %collective-permute-start.13 = (f32[8,2,8,128]{3,2,1,0:T(8,128)S(1)}, f32[8,2,8,128]{3,2,1,0:T(8,128)S(1)}, u32[]{:S(2)}, u32[]{:S(2)}) collective-permute-start(f32[8,2,8,128]{3,2,1,0:T(8,128)S(1)} %get-tuple-element.109), channel_id=1, source_target_pairs={{1,0},{2,1},{3,2},{4,3},{5,4},{6,5},{7,6},{0,7},{9,8},{10,9},{11,1... | collective-permute-start | bytes 196616 | tf_op jit(solution)/shard_map/ppermute | solution.py:1045

commit v4 on v3

--- a/solution.py
+++ b/solution.py
@@ -107,12 +107,12 @@
 def operator_tables():
     along_second = np.kron(STIFF, np.diag(WEIGHT))
     along_third = np.kron(np.diag(WEIGHT), STIFF)
-    sets = []
-    for places in (range(8), (0, 1, 6, 7)):
-        rows = [8 * j + k for j in places for k in range(8)]
-        high, low = two_parts(np.concatenate([along_second[rows], along_third[rows]]))
-        sets.append(np.concatenate([high, high, low], axis=1))
-    return np.concatenate(sets)
+    high, low = two_parts(np.concatenate([along_second, along_third]))
+    own = np.concatenate([high, high, low], axis=1)
+    high, low = two_parts(np.kron(np.diag(WEIGHT[6:8]), STIFF))
+    side = np.zeros((16, 192), own.dtype)
+    side[:, :48] = np.concatenate([high, high, low], axis=1)
+    return np.concatenate([own, side])
 
 
 def transform_tables():
@@ -153,8 +153,8 @@
 
 
 OPERATOR = operator_tables()
-OWN_ROWS = (0, 128)
-SIDE_ROWS = (128, 192)
+GHOST_SOURCE = 3
+FACTS = 4
 FORWARD, BACKWARD = transform_tables()
 VALUES = value_tables()
 LANES = (slice(0, 128), slice(128, 256))
@@ -225,7 +225,7 @@
 
 
 def ghost_keep(message, i):
-    return jnp.where(row_ids() == 7, message[i, 8], 1.0)
+    return jnp.where(row_ids() == 7, message[i, FACTS], 1.0)
 
 
 def weight_at(j):
@@ -278,17 +278,24 @@
     )(*args)
 
 
-def pack_body(outflow, start, source, coefficients, low, high, flags, gains, stages, semaphores):
-    sides = ((low, 1, 1, 0), (high, 24, 30, 3))
+def pack_body(
+    outflow, start, source, coefficients, low, high, flags, gains, nodes, stages, semaphores
+):
+    sides = ((low, 0, 1, 0, UPPER_POINTS), (high, 24, 30, 3, LOWER_POINTS))
     rows_in = []
-    for n, (_, first, node, _) in enumerate(sides):
-        for piece, at, count, to in ((start, first, 7, 0), (source, node, 1, 7)):
-            rows_in.append(
-                pltpu.make_async_copy(
-                    piece.at[:, at : at + count], stages.at[n, :, to : to + count],
-                    semaphores.at[len(rows_in)],
-                )
+    for n, (_, first, node, _, _) in enumerate(sides):
+        rows_in.append(
+            pltpu.make_async_copy(
+                start.at[:, first : first + 8], nodes.at[n], semaphores.at[2 * n]
             )
+        )
+        rows_in.append(
+            pltpu.make_async_copy(
+                source.at[:, node : node + 1],
+                stages.at[n, :, GHOST_SOURCE : GHOST_SOURCE + 1],
+                semaphores.at[2 * n + 1],
+            )
+        )
     facts = [
         pltpu.make_async_copy(coefficients, gains, semaphores.at[4]),
         pltpu.make_async_copy(outflow, flags, semaphores.at[5]),
@@ -298,16 +305,21 @@
     for copy in facts:
         copy.wait()
     top = top_flags()
-    rows = row_ids()
-    for n, (_, _, node, element) in enumerate(sides):
+    row = row_ids()
+    for n, (_, _, node, element, _) in enumerate(sides):
         rows_of = [spread_row(gains[c, 0, element : element + 1, :]) for c in range(3)]
-        gain = jnp.where(rows == 0, rows_of[0], jnp.where(rows == 1, rows_of[1], rows_of[2]))
+        gain = jnp.where(row == 0, rows_of[0], jnp.where(row == 1, rows_of[1], rows_of[2]))
         for i in range(8):
-            stages[n, i, 8] = jnp.where(rows == 7, own_keep(flags, top, i, node), gain)
+            stages[n, i, FACTS] = jnp.where(row == 7, own_keep(flags, top, i, node), gain)
     rows_out = []
-    for n, (target, _, _, _) in enumerate(sides):
+    for n, (target, _, _, _, points) in enumerate(sides):
         rows_in[2 * n].wait()
         rows_in[2 * n + 1].wait()
+        for i in range(8):
+            stages[n, i, 0] = nodes[n, i, 6 if 0 in points else 1]
+            rows = contract(points, [nodes[n, i, point] for point in points])
+            stages[n, i, 1] = rows[0]
+            stages[n, i, 2] = rows[1]
         rows_out.append(pltpu.make_async_copy(stages.at[n], target, semaphores.at[6 + n]))
         rows_out[-1].start()
     for copy in rows_out:
@@ -318,13 +330,14 @@
     anywhere = whole(pltpu.HBM)
     return pl.pallas_call(
         pack_body,
-        out_shape=(layers(8, 9), layers(8, 9)),
+        out_shape=(layers(8, 5), layers(8, 5)),
         in_specs=[anywhere, anywhere, anywhere, anywhere],
         out_specs=(anywhere, anywhere),
         scratch_shapes=[
             pltpu.SMEM((8, 32), jnp.int32),
             pltpu.VMEM((3, 1, 4, 128), F32),
-            pltpu.VMEM((2, 8, 9, 8, 128), F32),
+            pltpu.VMEM((2, 8, 8, 8, 128), F32),
+            pltpu.VMEM((2, 8, 5, 8, 128), F32),
             pltpu.SemaphoreType.DMA((8,)),
         ],
         compiler_params=pltpu.CompilerParams(vmem_limit_bytes=PACK_VMEM_BYTES),
@@ -355,7 +368,7 @@
     return outs
 
 
-def products(pair, table, rows, planes, wanted):
+def products(pair, table, planes, wanted):
     def step(n, carry):
         if wanted is EVERY:
             i = n
@@ -367,9 +380,7 @@
             [field[i, at : at + 8].reshape(64, 128) for field, at in pair], axis=1
         )
         high, low = split(values)
-        planes[i, 0 : rows[1] - rows[0]] = dot(
-            table[rows[0] : rows[1]], jnp.concatenate([high, low, high], axis=0)
-        )
+        planes[i] = dot(table[0:128], jnp.concatenate([high, low, high], axis=0))
         return carry
 
     lax.fori_loop(0, len(wanted), step, 0, unroll=True)
@@ -389,7 +400,7 @@
 
 
 def own_elements(pair, gains, table, planes, image, offset, wanted=EVERY):
-    products([(field, at) for _, field, at, _, _ in pair], table, OWN_ROWS, planes, wanted)
+    products([(field, at) for _, field, at, _, _ in pair], table, planes, wanted)
     for (e, field, at, add_first, add_last), lane in zip(pair, LANES):
         gain = gains(e)
         plane = gain[0] * row_weights()
@@ -414,24 +425,56 @@
 
 
 def side_gains(flag, message):
-    return [spread_row(message[0, 8, c : c + 1, :] * flag) for c in range(3)]
-
-
-def side_elements(
-    field, low_at, high_at, low_gain, high_gain, table, planes, image, wanted
-):
-    products([(field, low_at), (field, high_at)], table, SIDE_ROWS, planes, wanted)
-    low_plane = low_gain[0] * row_weights()
-    high_plane = high_gain[0] * row_weights()
-    for q in range(2):
-        combine(
-            field, low_at + 6 + q, low_gain, low_plane * weight_at(6 + q), planes,
-            LANES[0], 16 + 8 * q, 48 + 8 * q, image, q, q == 1, wanted,
+    return [spread_row(message[0, FACTS, c : c + 1, :] * flag) for c in range(3)]
+
+
+def contract(points, rows):
+    targets = (6, 7) if 0 in points else (1, 0)
+    totals = []
+    for target in targets:
+        total = None
+        for point, row in zip(points, rows):
+            term = row * float(STIFF[target, point])
+            total = term if total is None else total + term
+        totals.append(total)
+    return totals
+
+
+LOWER_POINTS = tuple(range(6))
+UPPER_POINTS = tuple(range(2, 8))
+
+
+def side_elements(low_rows, high_rows, low_gain, high_gain, table, planes, image, wanted):
+    sides = (low_rows, high_rows)
+    for i in wanted:
+        values = jnp.concatenate(
+            [jnp.concatenate(rows(i)[:2], axis=0) for rows in sides], axis=1
         )
-        combine(
-            field, high_at + q, high_gain, high_plane * weight_at(q), planes,
-            LANES[1], 8 * q, 32 + 8 * q, image, 29 + q, q == 0, wanted,
+        high, low = split(values)
+        planes[i, 0:16] = dot(
+            table[128:144, 0:48], jnp.concatenate([high, low, high], axis=0)
         )
+    weights = row_weights()
+    targets = ((0, 1), (30, 29))
+    for rows, gain, lane, target in zip(sides, (low_gain, high_gain), LANES, targets):
+        second_gain = gain[1] * weights
+        for q in range(2):
+            plane = gain[0] * (weights * float(WEIGHT[6 + q]))
+            terms = first_direction([rows(a)[q] for a in range(8)], wanted)
+            for i in wanted:
+                ghost, shared, *contracted = rows(i)
+                second = (
+                    contracted[q]
+                    + ghost * float(STIFF[6 + q, 6])
+                    + shared * float(STIFF[6 + q, 7])
+                )
+                third = planes[i, 8 * q : 8 * q + 8, lane]
+                value = plane * terms[i] + float(WEIGHT[i]) * (
+                    second_gain * second + gain[2] * third
+                )
+                if q == 1:
+                    value = value + image[i, target[q]]
+                image[i, target[q]] = value
 
 
 def finish_residual(wanted, image, source_row, outflow, from_low, from_high, put):
@@ -492,9 +535,9 @@
 
     def source_row(i, y):
         if isinstance(y, int) and y == 0:
-            return from_low[i, 7] * (source_share(place, i) * low_flag)
+            return from_low[i, GHOST_SOURCE] * (source_share(place, i) * low_flag)
         if isinstance(y, int) and y == 30:
-            return from_high[i, 7] * (source_share(place, i) * high_flag)
+            return from_high[i, GHOST_SOURCE] * (source_share(place, i) * high_flag)
         return source_part[i, y]
 
     return source_row
@@ -563,16 +606,13 @@
     own_image, source_part, *rest,
 ):
     low_flag, high_flag = ends(place, 1)
-    *outs, planes, field, image = rest
-    for i in range(8):
-        field[i, 0:7] = from_low[i, 0:7]
-        field[i, 7] = start[i, 0]
-        field[i, 8] = start[i, 31]
-        field[i, 9:16] = from_high[i, 0:7]
+    *outs, planes, image = rest
     for i in wanted:
         image[i, 1:30] = own_image[i, 1:30]
     side_elements(
-        field, 0, 8, side_gains(low_flag, from_low), side_gains(high_flag, from_high),
+        lambda i: (from_low[i, 0], start[i, 0], from_low[i, 1], from_low[i, 2]),
+        lambda i: (from_high[i, 0], start[i, 31], from_high[i, 1], from_high[i, 2]),
+        side_gains(low_flag, from_low), side_gains(high_flag, from_high),
         table, planes, image, wanted,
     )
     put = put_edges(*outs[:2]) if wanted is EDGES else put_inner(*outs)
@@ -845,15 +885,18 @@
 def fold_body(count, place, outflow, low, inner, high, first, second, to_low, to_high):
     top = top_flags()
     parts = (low, inner, high, *arrived(place, first, second))
+    sides = ((to_low, 0, 1, UPPER_POINTS), (to_high, 31 - count, 22, LOWER_POINTS))
     for i in range(8):
-        for y in (*range(count), *range(31 - count, 31)):
-            value = fold_row(i, y, *parts)
-            if 3 <= y < 28:
-                value = own_keep(outflow, top, i, column_of(y - 1)) * value
-            if y < count:
-                to_low[i, y] = value
-            else:
-                to_high[i, y - 31 + count] = value
+        for target, start, base, points in sides:
+            for n in range(count):
+                target[i, n] = fold_row(i, start + n, *parts)
+            if count == 3:
+                rows = []
+                for point in points:
+                    y = base + point
+                    keep = own_keep(outflow, top, i, column_of(y - 1))
+                    rows.append(keep * fold_row(i, y, *parts))
+                target[i, 3], target[i, 4] = contract(points, rows)
 
 
 def update_body(
@@ -890,25 +933,25 @@
     top = top_flags()
     low_flag, high_flag = ends(place, 1)
     for i in range(8):
-        rows[i, 0:6] = from_low[i, 0:6] + low_news[i, 0:6]
-        rows[i, 6] = from_low[i, 6] + ghost_keep(from_low, i) * (
-            field[i, 0] + low_flag * low_news[i, 6]
-        )
         for n in range(2):
-            news = own_keep(outflow, top, i, n) * (low_flag * low_news[i, 7 + n])
+            news = own_keep(outflow, top, i, n) * (low_flag * low_news[i, 1 + n])
             value = field[i, 1 + n] + news
-            rows[i, 7 + n] = value
+            rows[i, n] = value
             changed[i, n] = value
             news = own_keep(outflow, top, i, 30 + n) * (high_flag * high_news[i, n])
             value = field[i, 28 + n] + news
-            rows[i, 21 + n] = value
+            rows[i, 14 + n] = value
             changed[i, 2 + n] = value
-        rows[i, 9:15] = field[i, 3:9]
-        rows[i, 15:21] = field[i, 22:28]
-        rows[i, 23] = from_high[i, 0] + ghost_keep(from_high, i) * (
+        rows[i, 2:8] = field[i, 3:9]
+        rows[i, 8:14] = field[i, 22:28]
+        rows[i, 16] = from_low[i, 0] + ghost_keep(from_low, i) * (
+            field[i, 0] + low_flag * low_news[i, 0]
+        )
+        rows[i, 19] = from_high[i, 0] + ghost_keep(from_high, i) * (
             field[i, 30] + high_flag * high_news[i, 2]
         )
-        rows[i, 24:30] = from_high[i, 1:7] + high_news[i, 3:9]
+        rows[i, 17:19] = from_low[i, 1:3] + low_news[i, 3:5]
+        rows[i, 20:22] = from_high[i, 1:3] + high_news[i, 3:5]
 
 
 def second_residual(
@@ -919,11 +962,13 @@
     for i in wanted:
         image[i, 8:23] = middle_image[i]
     own_elements(
-        [(0, rows, 7, False, True), (3, rows, 15, True, False)],
+        [(0, rows, 0, False, True), (3, rows, 8, True, False)],
         own_gains(coefficients), table, planes, image, 1, wanted,
     )
     side_elements(
-        rows, 0, 22, side_gains(low_flag, from_low), side_gains(high_flag, from_high),
+        lambda i: (rows[i, 16], rows[i, 0], rows[i, 17], rows[i, 18]),
+        lambda i: (rows[i, 19], rows[i, 15], rows[i, 20], rows[i, 21]),
+        side_gains(low_flag, from_low), side_gains(high_flag, from_high),
         table, planes, image, wanted,
     )
     finish_residual(
@@ -1096,8 +1141,9 @@
 
 
 def fold(count, place, outflow, parts):
+    message = layers(8, 5 if count == 3 else count)
     return call(
-        functools.partial(fold_body, count), [layers(8, count), layers(8, count)], 2, [],
+        functools.partial(fold_body, count), [message, message], 2, [],
         "fold", (place, outflow, *parts), 10**6,
     )
 
@@ -1133,9 +1179,7 @@
         (coefficients, *[jnp.asarray(t) for t in VALUES]), 10**8,
     )
     joined = (place, outflow, start, from_low, from_high, table)
-    join_scratch = [
-        plane_scratch(), pltpu.VMEM((8, 16, 8, 128), F32), pltpu.VMEM((8, 31, 8, 128), F32)
-    ]
+    join_scratch = [plane_scratch(), pltpu.VMEM((8, 31, 8, 128), F32)]
     edge_parts = call(
         functools.partial(first_join_body, EDGES), [layers(2, 31)] * 4, 2,
         join_scratch, "first_edges", (*joined, edge_image, edge_source), 10**8,
@@ -1157,7 +1201,7 @@
         )[0]
 
     solved, _ = solve(place, reciprocals, edge_parts, first_inner, lambda *_: None)
-    news = exchange(*fold(9, place, outflow, solved), "inner")
+    news = exchange(*fold(3, place, outflow, solved), "inner")
     field, middle_image = call(
         update_body, [layers(8, 31), layers(8, 15)], 2, [plane_scratch()], "update",
         (place, outflow, start, coefficients, table, *solved), 2 * 10**8,
@@ -1168,7 +1212,7 @@
     join_scratch = [plane_scratch(), pltpu.VMEM((8, 31, 8, 128), F32)]
     changed, rows, *edge_parts = call(
         second_edges_body,
-        [layers(8, 4), layers(8, 30)] + [layers(2, 31)] * 4,
+        [layers(8, 4), layers(8, 22)] + [layers(2, 31)] * 4,
         2, join_scratch, "second_edges",
         (*operands, field, middle_image, edge_source, *news), 2 * 10**8,
     )

time: 73.7 us -> 70.8 us (0.961)
  waiting for transfers between devices: 23.6 us -> 20.8 us
    ppermute x3, waiting for transfers between devices: 2.59 us -> 0.01 us  [exchange(): lax.ppermute(to_high, axis, upward)]
  transfers between devices with their start and end apart: 14 -> 14, of which waited for: 13 -> 11; matrix products, arithmetic and copies ran while one was open for 0% -> 0% of each run, Pallas kernels for 28% -> 29%
where the time goes in v4:
time: 70.8 us; the launch traced here: 70 us
  Pallas kernels  31.4 us (44%)
  waiting for transfers between devices  20.8 us (29%)
  starting transfers between devices  15.3 us (22%)
  local copies, waits for them, and re-layouts  1.63 us (2%)
  between operations  0.88 us (1%)
    pallas_call x16, Pallas kernels, call(): pl.pallas_call(body, out_shape=tuple(outs), in_specs=[whole(pltpu.SMEM if...  24.6 us
    ppermute x4, starting transfers between devices, exchange_along_first(): lax.ppermute(first, axes, forward)  12.5 us
    ppermute x4, waiting for transfers between devices, exchange_along_first(): lax.ppermute(second, axes, backward)  8.36 us
    ppermute x3, waiting for transfers between devices, exchange(): lax.ppermute(to_low, axis, downward)  6.45 us
    ppermute x4, waiting for transfers between devices, exchange_along_first(): lax.ppermute(first, axes, forward)  5.96 us
    pallas_call x1, Pallas kernels, pack_first(): pl.pallas_call(pack_body, out_shape=(layers(8, 5), layers(8, 5)), in_spec...  1.98 us
    pallas_call x1, Pallas kernels, residual_out(): pl.pallas_call(residual_body, out_shape=layers(8, 32), in_specs=[whole(pl...  1.84 us
    ppermute x3, starting transfers between devices, exchange(): lax.ppermute(to_high, axis, upward)  1.81 us
  transfers between devices with their start and end apart: 14, of which 11 were waited for; matrix products, arithmetic and copies ran while one was open for 0% of the time, Pallas kernels for 29%

profile of v4, /device:TPU:25, one launch (start us, length us, event | category | flops | bytes accessed | tf_op | source)
XLA Modules:
  0.0 70.0 jit_solution(8076946985726484975)
XLA Ops:
  0.7 2.0 %pack_first.1 = (f32[8,5,8,128]{3,2,1,0:T(8,128)}, f32[8,5,8,128]{3,2,1,0:T(8,128)}) custom-call(s32[8,32]{1,0:T(8,128)} %outflow.17, f32[8,32,8,128]{3,2,1,0:T(8,128)} %start.5, f32[8,32,8,128]{3,2,1,0:T(8,128)} %source.3, f32[3,1,4,128]{3,2,1,0:T(4,128)} %coefficients.2), custom_call_target="tpu_custom_call" | custom-call | tf_op jit(solution)/shard_map/pack_first/pallas_call | solution.py:331
  2.6 1.8 %collective-permute-start = (f32[8,5,8,128]{3,2,1,0:T(8,128)}, f32[8,5,8,128]{3,2,1,0:T(8,128)S(1)}, u32[]{:S(2)}, u32[]{:S(2)}) collective-permute-start(f32[8,5,8,128]{3,2,1,0:T(8,128)} %get-tuple-element.65), channel_id=1, source_target_pairs={{0,1},{1,2},{2,3},{3,4},{4,5},{5,6},{6,7},{7,0},{8,9},{9,10},{10,1... | collective-permute-start | bytes 491528 | tf_op jit(solution)/shard_map/ppermute | solution.py:1090
  7.2 2.2 %collective-permute-done.1.from_high.refs_4_ = f32[8,5,8,128]{3,2,1,0:T(8,128)S(1)} collective-permute-done((f32[8,5,8,128]{3,2,1,0:T(8,128)}, f32[8,5,8,128]{3,2,1,0:T(8,128)S(1)}, u32[]{:S(2)}, u32[]{:S(2)}) %collective-permute-start.1) | collective-permute-done | bytes 163872 | tf_op jit(solution)/shard_map/ppermute | solution.py:1090
  10.2 4.0 %collective-permute-start.2 = (f32[2,31,8,128]{3,2,1,0:T(8,128)S(1)}, f32[2,31,8,128]{3,2,1,0:T(8,128)S(1)}, u32[]{:S(2)}, u32[]{:S(2)}) collective-permute-start(f32[2,31,8,128]{3,2,1,0:T(8,128)S(1)} %get-tuple-element.81), channel_id=1, source_target_pairs={{0,8},{8,16},{16,24},{24,32},{32,40},{40,48},{48,56},{56,64},{64,7... | collective-permute-start | bytes 761864 | tf_op jit(solution)/shard_map/ppermute | solution.py:1105
  17.0 2.3 %inner_forward.2 = (f32[10,2,128,256]{3,2,1,0:T(8,128)S(1)}, f32[4,2,128,256]{3,2,1,0:T(8,128)S(1)}) custom-call(f32[6,31,8,128]{3,2,1,0:T(8,128)S(1)} %first_inner.1.inner, bf16[128,240]{1,0:T(8,128)(2,1)S(1)} %copy-done.3, f32[10,2,128,256]{3,2,1,0:T(8,128)S(1)} %get-tuple-element.79.reciprocals), custom_call_target="tpu_custom_call" | custom-call | flops 300000000 | bytes 7176192 | tf_op jit(solution)/shard_map/inner_forward/pallas_call | solution.py:267
  19.6 1.9 %collective-permute-done.3.second = f32[2,31,8,128]{3,2,1,0:T(8,128)S(1)} collective-permute-done((f32[2,31,8,128]{3,2,1,0:T(8,128)S(1)}, f32[2,31,8,128]{3,2,1,0:T(8,128)S(1)}, u32[]{:S(2)}, u32[]{:S(2)}) %collective-permute-start.3) | collective-permute-done | bytes 253984 | tf_op jit(solution)/shard_map/ppermute | solution.py:1105
  21.5 2.4 %edge_solve.2 = (f32[2,31,8,128]{3,2,1,0:T(8,128)S(1)}, f32[2,31,8,128]{3,2,1,0:T(8,128)S(1)}, f32[2,31,8,128]{3,2,1,0:T(8,128)S(1)}, f32[2,31,8,128]{3,2,1,0:T(8,128)S(1)}, f32[4,2,128,256]{3,2,1,0:T(8,128)S(1)}) custom-call(s32[4]{0:T(128)S(1)} %pad_add_fusion.place.refs_0_, f32[6,2,128,256]{3,2,1,0:T(8,128)S(1)} %get-tuple-element.64.blocks, ...), custom_call_target="tpu_custom_call" | custom-call | flops 1000000000 | bytes 6152208 | tf_op jit(solution)/shard_map/edge_solve/pallas_call | solution.py:267
  23.9 2.5 %collective-permute-start.4 = (f32[2,31,8,128]{3,2,1,0:T(8,128)S(1)}, f32[2,31,8,128]{3,2,1,0:T(8,128)S(1)}, u32[]{:S(2)}, u32[]{:S(2)}) collective-permute-start(f32[2,31,8,128]{3,2,1,0:T(8,128)S(1)} %get-tuple-element.87), channel_id=1, source_target_pairs={{0,8},{8,16},{16,24},{24,32},{32,40},{40,48},{48,56},{56,64},{64,7... | collective-permute-start | bytes 761864 | tf_op jit(solution)/shard_map/ppermute | solution.py:1105
  26.3 2.7 %inner_backward.2.inner = f32[6,31,8,128]{3,2,1,0:T(8,128)S(1)} custom-call(f32[4,2,128,256]{3,2,1,0:T(8,128)S(1)} %get-tuple-element.84.spectral, f32[10,2,128,256]{3,2,1,0:T(8,128)S(1)} %get-tuple-element.85.partial, f32[10,2,128,256]{3,2,1,0:T(8,128)S(1)} %get-tuple-element.79.reciprocals, bf16[320,256]{1,0:T(8,128)(2,1)S(1)} %copy-done.2), custom_call_target="tpu_custom_call" | custom-call | flops 300000000 | bytes 7380992 | tf_op jit(solution)/shard_map/inner_backward/pallas_call | solution.py:267
  29.1 2.8 %collective-permute-done.4.first = f32[2,31,8,128]{3,2,1,0:T(8,128)S(1)} collective-permute-done((f32[2,31,8,128]{3,2,1,0:T(8,128)S(1)}, f32[2,31,8,128]{3,2,1,0:T(8,128)S(1)}, u32[]{:S(2)}, u32[]{:S(2)}) %collective-permute-start.4) | collective-permute-done | bytes 253984 | tf_op jit(solution)/shard_map/ppermute | solution.py:1105
  31.9 2.0 %collective-permute-done.5.second = f32[2,31,8,128]{3,2,1,0:T(8,128)S(1)} collective-permute-done((f32[2,31,8,128]{3,2,1,0:T(8,128)S(1)}, f32[2,31,8,128]{3,2,1,0:T(8,128)S(1)}, u32[]{:S(2)}, u32[]{:S(2)}) %collective-permute-start.5) | collective-permute-done | bytes 253984 | tf_op jit(solution)/shard_map/ppermute | solution.py:1105
  35.2 1.8 %update.1 = (f32[8,31,8,128]{3,2,1,0:T(8,128)S(1)}, f32[8,15,8,128]{3,2,1,0:T(8,128)S(1)}) custom-call(s32[4]{0:T(128)S(1)} %pad_add_fusion.place.refs_0_, s32[8,32]{1,0:T(8,128)S(1)} %copy-done.4, f32[8,32,8,128]{3,2,1,0:T(8,128)S(1)} %copy-done, f32[3,1,4,128]{3,2,1,0:T(4,128)S(1)} %get-tuple-element.62.coefficients, ...), custom_call_target="tpu_custom_call" | custom-call | flops 200000000 | bytes 4451344 | tf_op jit(solution)/shard_map/update/pallas_call | solution.py:267
  37.0 2.6 %collective-permute-done.7.high_news = f32[8,5,8,128]{3,2,1,0:T(8,128)S(1)} collective-permute-done((f32[8,5,8,128]{3,2,1,0:T(8,128)S(1)}, f32[8,5,8,128]{3,2,1,0:T(8,128)S(1)}, u32[]{:S(2)}, u32[]{:S(2)}) %collective-permute-start.7) | collective-permute-done | bytes 163872 | tf_op jit(solution)/shard_map/ppermute | solution.py:1090
  40.7 3.8 %collective-permute-start.8 = (f32[2,31,8,128]{3,2,1,0:T(8,128)S(1)}, f32[2,31,8,128]{3,2,1,0:T(8,128)S(1)}, u32[]{:S(2)}, u32[]{:S(2)}) collective-permute-start(f32[2,31,8,128]{3,2,1,0:T(8,128)S(1)} %get-tuple-element.98), channel_id=1, source_target_pairs={{0,8},{8,16},{16,24},{24,32},{32,40},{40,48},{48,56},{56,64},{64,7... | collective-permute-start | bytes 761864 | tf_op jit(solution)/shard_map/ppermute | solution.py:1105
  45.6 2.3 %inner_forward.3 = (f32[10,2,128,256]{3,2,1,0:T(8,128)S(1)}, f32[4,2,128,256]{3,2,1,0:T(8,128)S(1)}) custom-call(f32[6,31,8,128]{3,2,1,0:T(8,128)S(1)} %second_inner.1.inner, bf16[128,240]{1,0:T(8,128)(2,1)S(1)} %copy-done.3, f32[10,2,128,256]{3,2,1,0:T(8,128)S(1)} %get-tuple-element.79.reciprocals), custom_call_target="tpu_custom_call" | custom-call | flops 300000000 | bytes 7176192 | tf_op jit(solution)/shard_map/inner_forward/pallas_call | solution.py:267
  47.8 1.7 %collective-permute-done.8.first = f32[2,31,8,128]{3,2,1,0:T(8,128)S(1)} collective-permute-done((f32[2,31,8,128]{3,2,1,0:T(8,128)S(1)}, f32[2,31,8,128]{3,2,1,0:T(8,128)S(1)}, u32[]{:S(2)}, u32[]{:S(2)}) %collective-permute-start.8) | collective-permute-done | bytes 253984 | tf_op jit(solution)/shard_map/ppermute | solution.py:1105
  49.6 2.2 %collective-permute-done.9.second = f32[2,31,8,128]{3,2,1,0:T(8,128)S(1)} collective-permute-done((f32[2,31,8,128]{3,2,1,0:T(8,128)S(1)}, f32[2,31,8,128]{3,2,1,0:T(8,128)S(1)}, u32[]{:S(2)}, u32[]{:S(2)}) %collective-permute-start.9) | collective-permute-done | bytes 253984 | tf_op jit(solution)/shard_map/ppermute | solution.py:1105
  51.8 2.4 %edge_solve.3 = (f32[2,31,8,128]{3,2,1,0:T(8,128)S(1)}, f32[2,31,8,128]{3,2,1,0:T(8,128)S(1)}, f32[2,31,8,128]{3,2,1,0:T(8,128)S(1)}, f32[2,31,8,128]{3,2,1,0:T(8,128)S(1)}, f32[4,2,128,256]{3,2,1,0:T(8,128)S(1)}) custom-call(s32[4]{0:T(128)S(1)} %pad_add_fusion.place.refs_0_, f32[6,2,128,256]{3,2,1,0:T(8,128)S(1)} %get-tuple-element.64.blocks, ...), custom_call_target="tpu_custom_call" | custom-call | flops 1000000000 | bytes 6152208 | tf_op jit(solution)/shard_map/edge_solve/pallas_call | solution.py:267
  54.2 2.2 %collective-permute-start.10 = (f32[2,31,8,128]{3,2,1,0:T(8,128)S(1)}, f32[2,31,8,128]{3,2,1,0:T(8,128)S(1)}, u32[]{:S(2)}, u32[]{:S(2)}) collective-permute-start(f32[2,31,8,128]{3,2,1,0:T(8,128)S(1)} %get-tuple-element.105), channel_id=1, source_target_pairs={{0,8},{8,16},{16,24},{24,32},{32,40},{40,48},{48,56},{56,64},{64,7... | collective-permute-start | bytes 761864 | tf_op jit(solution)/shard_map/ppermute | solution.py:1105
  56.3 1.8 %residual.1 = f32[8,32,8,128]{3,2,1,0:T(8,128)} custom-call(s32[4]{0:T(128)S(1)} %pad_add_fusion.place.refs_0_, f32[2,31,8,128]{3,2,1,0:T(8,128)S(1)} %get-tuple-element.95.low, f32[6,31,8,128]{3,2,1,0:T(8,128)S(1)} %second_inner.1.inner, f32[2,31,8,128]{3,2,1,0:T(8,128)S(1)} %get-tuple-element.96.high, f32[2,31,8,128]{3,2,1,0:T(8,128)S(1)} %collective-permute-done.8.first, ...), custom_call_target="tpu_custom_call" | custom-call | flops 10000000 | bytes 4194304 | tf_op jit(solution)/shard_map/residual/pallas_call | solution.py:861
  58.2 2.7 %inner_backward.3.inner = f32[6,31,8,128]{3,2,1,0:T(8,128)S(1)} custom-call(f32[4,2,128,256]{3,2,1,0:T(8,128)S(1)} %get-tuple-element.101.spectral, f32[10,2,128,256]{3,2,1,0:T(8,128)S(1)} %get-tuple-element.102.partial, f32[10,2,128,256]{3,2,1,0:T(8,128)S(1)} %get-tuple-element.79.reciprocals, bf16[320,256]{1,0:T(8,128)(2,1)S(1)} %copy-done.2), custom_call_target="tpu_custom_call" | custom-call | flops 300000000 | bytes 7380992 | tf_op jit(solution)/shard_map/inner_backward/pallas_call | solution.py:267
  62.0 2.2 %collective-permute-done.11.second = f32[2,31,8,128]{3,2,1,0:T(8,128)S(1)} collective-permute-done((f32[2,31,8,128]{3,2,1,0:T(8,128)S(1)}, f32[2,31,8,128]{3,2,1,0:T(8,128)S(1)}, u32[]{:S(2)}, u32[]{:S(2)}) %collective-permute-start.11) | collective-permute-done | bytes 253984 | tf_op jit(solution)/shard_map/ppermute | solution.py:1105
  65.4 1.7 %last_update.1 = (f32[8,32,8,128]{3,2,1,0:T(8,128)}, f32[8,4,8,128]{3,2,1,0:T(8,128)S(1)}) custom-call(s32[4]{0:T(128)S(1)} %pad_add_fusion.place.refs_0_, s32[8,32]{1,0:T(8,128)S(1)} %copy-done.4, f32[8,31,8,128]{3,2,1,0:T(8,128)S(1)} %get-tuple-element.89.field, f32[8,4,8,128]{3,2,1,0:T(8,128)S(1)} %get-tuple-element.93.changed, ...), custom_call_target="tpu_custom_call" | custom-call | flops 10000000 | bytes 4194304 | tf_op jit(solution)/shard_map/last_update/pallas_call | solution.py:1040
  67.1 1.7 %collective-permute-done.13.high_news = f32[8,2,8,128]{3,2,1,0:T(8,128)S(1)} collective-permute-done((f32[8,2,8,128]{3,2,1,0:T(8,128)S(1)}, f32[8,2,8,128]{3,2,1,0:T(8,128)S(1)}, u32[]{:S(2)}, u32[]{:S(2)}) %collective-permute-start.13) | collective-permute-done | bytes 65568 | tf_op jit(solution)/shard_map/ppermute | solution.py:1090
  (43 shorter events, 13.5 us)
Async XLA Ops:
  0.6 8.8 %copy-start.4 = (s32[8,32]{1,0:T(8,128)S(1)}, s32[8,32]{1,0:T(8,128)}, u32[]{:S(2)}) copy-start(s32[8,32]{1,0:T(8,128)} %outflow.17) | copy-start | bytes 3076
  0.6 3.9 %copy-start.1 = (f32[8,32,8,128]{3,2,1,0:T(8,128)S(1)}, f32[8,32,8,128]{3,2,1,0:T(8,128)}, u32[]{:S(2)}) copy-start(f32[8,32,8,128]{3,2,1,0:T(8,128)} %source.3) | copy-start | bytes 3145732
  0.6 3.9 %copy-start = (f32[8,32,8,128]{3,2,1,0:T(8,128)S(1)}, f32[8,32,8,128]{3,2,1,0:T(8,128)}, u32[]{:S(2)}) copy-start(f32[8,32,8,128]{3,2,1,0:T(8,128)} %start.5) | copy-start | bytes 3145732
  2.6 4.5 %collective-permute-start = (f32[8,5,8,128]{3,2,1,0:T(8,128)}, f32[8,5,8,128]{3,2,1,0:T(8,128)S(1)}, u32[]{:S(2)}, u32[]{:S(2)}) collective-permute-start(f32[8,5,8,128]{3,2,1,0:T(8,128)} %get-tuple-element.65), channel_id=1, source_target_pairs={{0,1},{1,2},{2,3},{3,4},{4,5},{5,6},{6,7},{7,0},{8,9},{9,10},{10,1... | collective-permute-start | bytes 491528 | tf_op jit(solution)/shard_map/ppermute | solution.py:1090
  4.4 5.0 %collective-permute-start.1 = (f32[8,5,8,128]{3,2,1,0:T(8,128)}, f32[8,5,8,128]{3,2,1,0:T(8,128)S(1)}, u32[]{:S(2)}, u32[]{:S(2)}) collective-permute-start(f32[8,5,8,128]{3,2,1,0:T(8,128)} %get-tuple-element.66), channel_id=1, source_target_pairs={{1,0},{2,1},{3,2},{4,3},{5,4},{6,5},{7,6},{0,7},{9,8},{10,9},{11,1... | collective-permute-start | bytes 491528 | tf_op jit(solution)/shard_map/ppermute | solution.py:1090
  4.5 0.9 %copy-start.5 = (bf16[144,192]{1,0:T(8,128)(2,1)S(1)}, bf16[144,192]{1,0:T(8,128)(2,1)}, u32[]{:S(2)}) copy-start(bf16[144,192]{1,0:T(8,128)(2,1)} %constant.23.clone.table) | copy-start | bytes 165892
  5.4 0.7 copy-start.6
  6.1 8.1 %copy-start.7 = (f32[128,128]{1,0:T(8,128)S(1)}, f32[128,128]{1,0:T(8,128)}, u32[]{:S(2)}) copy-start(f32[128,128]{1,0:T(8,128)} %constant.25.clone.third_values) | copy-start | bytes 196612
  6.1 8.1 %copy-start.8 = (f32[128,128]{1,0:T(8,128)S(1)}, f32[128,128]{1,0:T(8,128)}, u32[]{:S(2)}) copy-start(f32[128,128]{1,0:T(8,128)} %constant.24.clone.second_values) | copy-start | bytes 196612
  10.2 9.3 %collective-permute-start.2 = (f32[2,31,8,128]{3,2,1,0:T(8,128)S(1)}, f32[2,31,8,128]{3,2,1,0:T(8,128)S(1)}, u32[]{:S(2)}, u32[]{:S(2)}) collective-permute-start(f32[2,31,8,128]{3,2,1,0:T(8,128)S(1)} %get-tuple-element.81), channel_id=1, source_target_pairs={{0,8},{8,16},{16,24},{24,32},{32,40},{40,48},{48,56},{56,64},{64,7... | collective-permute-start | bytes 761864 | tf_op jit(solution)/shard_map/ppermute | solution.py:1105
  14.2 7.2 %collective-permute-start.3 = (f32[2,31,8,128]{3,2,1,0:T(8,128)S(1)}, f32[2,31,8,128]{3,2,1,0:T(8,128)S(1)}, u32[]{:S(2)}, u32[]{:S(2)}) collective-permute-start(f32[2,31,8,128]{3,2,1,0:T(8,128)S(1)} %get-tuple-element.82), channel_id=1, source_target_pairs={{8,0},{16,8},{24,16},{32,24},{40,32},{48,40},{56,48},{64,56},{72,6... | collective-permute-start | bytes 761864 | tf_op jit(solution)/shard_map/ppermute | solution.py:1105
  16.1 0.8 %copy-start.3 = (bf16[128,240]{1,0:T(8,128)(2,1)S(1)}, bf16[128,240]{1,0:T(8,128)(2,1)}, u32[]{:S(2)}) copy-start(bf16[128,240]{1,0:T(8,128)(2,1)} %constant.26.clone.forward) | copy-start | bytes 184324
  17.0 4.5 %copy-start.2 = (bf16[320,256]{1,0:T(8,128)(2,1)S(1)}, bf16[320,256]{1,0:T(8,128)(2,1)}, u32[]{:S(2)}) copy-start(bf16[320,256]{1,0:T(8,128)(2,1)} %constant.27.clone.backward) | copy-start | bytes 491524
  23.9 8.0 %collective-permute-start.4 = (f32[2,31,8,128]{3,2,1,0:T(8,128)S(1)}, f32[2,31,8,128]{3,2,1,0:T(8,128)S(1)}, u32[]{:S(2)}, u32[]{:S(2)}) collective-permute-start(f32[2,31,8,128]{3,2,1,0:T(8,128)S(1)} %get-tuple-element.87), channel_id=1, source_target_pairs={{0,8},{8,16},{16,24},{24,32},{32,40},{40,48},{48,56},{56,64},{64,7... | collective-permute-start | bytes 761864 | tf_op jit(solution)/shard_map/ppermute | solution.py:1105
  26.3 7.6 %collective-permute-start.5 = (f32[2,31,8,128]{3,2,1,0:T(8,128)S(1)}, f32[2,31,8,128]{3,2,1,0:T(8,128)S(1)}, u32[]{:S(2)}, u32[]{:S(2)}) collective-permute-start(f32[2,31,8,128]{3,2,1,0:T(8,128)S(1)} %get-tuple-element.88), channel_id=1, source_target_pairs={{8,0},{16,8},{24,16},{32,24},{40,32},{48,40},{56,48},{64,56},{72,6... | collective-permute-start | bytes 761864 | tf_op jit(solution)/shard_map/ppermute | solution.py:1105
  34.7 2.3 %collective-permute-start.6 = (f32[8,5,8,128]{3,2,1,0:T(8,128)S(1)}, f32[8,5,8,128]{3,2,1,0:T(8,128)S(1)}, u32[]{:S(2)}, u32[]{:S(2)}) collective-permute-start(f32[8,5,8,128]{3,2,1,0:T(8,128)S(1)} %get-tuple-element.91), channel_id=1, source_target_pairs={{0,1},{1,2},{2,3},{3,4},{4,5},{5,6},{6,7},{7,0},{8,9},{9,10},{10,1... | collective-permute-start | bytes 491528 | tf_op jit(solution)/shard_map/ppermute | solution.py:1090
  34.7 4.9 %collective-permute-start.7 = (f32[8,5,8,128]{3,2,1,0:T(8,128)S(1)}, f32[8,5,8,128]{3,2,1,0:T(8,128)S(1)}, u32[]{:S(2)}, u32[]{:S(2)}) collective-permute-start(f32[8,5,8,128]{3,2,1,0:T(8,128)S(1)} %get-tuple-element.92), channel_id=1, source_target_pairs={{1,0},{2,1},{3,2},{4,3},{5,4},{6,5},{7,6},{0,7},{9,8},{10,9},{11,1... | collective-permute-start | bytes 491528 | tf_op jit(solution)/shard_map/ppermute | solution.py:1090
  40.7 8.9 %collective-permute-start.8 = (f32[2,31,8,128]{3,2,1,0:T(8,128)S(1)}, f32[2,31,8,128]{3,2,1,0:T(8,128)S(1)}, u32[]{:S(2)}, u32[]{:S(2)}) collective-permute-start(f32[2,31,8,128]{3,2,1,0:T(8,128)S(1)} %get-tuple-element.98), channel_id=1, source_target_pairs={{0,8},{8,16},{16,24},{24,32},{32,40},{40,48},{48,56},{56,64},{64,7... | collective-permute-start | bytes 761864 | tf_op jit(solution)/shard_map/ppermute | solution.py:1105
  44.5 7.2 %collective-permute-start.9 = (f32[2,31,8,128]{3,2,1,0:T(8,128)S(1)}, f32[2,31,8,128]{3,2,1,0:T(8,128)S(1)}, u32[]{:S(2)}, u32[]{:S(2)}) collective-permute-start(f32[2,31,8,128]{3,2,1,0:T(8,128)S(1)} %get-tuple-element.99), channel_id=1, source_target_pairs={{8,0},{16,8},{24,16},{32,24},{40,32},{48,40},{56,48},{64,56},{72,6... | collective-permute-start | bytes 761864 | tf_op jit(solution)/shard_map/ppermute | solution.py:1105
  54.2 7.9 %collective-permute-start.10 = (f32[2,31,8,128]{3,2,1,0:T(8,128)S(1)}, f32[2,31,8,128]{3,2,1,0:T(8,128)S(1)}, u32[]{:S(2)}, u32[]{:S(2)}) collective-permute-start(f32[2,31,8,128]{3,2,1,0:T(8,128)S(1)} %get-tuple-element.105), channel_id=1, source_target_pairs={{0,8},{8,16},{16,24},{24,32},{32,40},{40,48},{48,56},{56,64},{64,7... | collective-permute-start | bytes 761864 | tf_op jit(solution)/shard_map/ppermute | solution.py:1105
  56.3 7.9 %collective-permute-start.11 = (f32[2,31,8,128]{3,2,1,0:T(8,128)S(1)}, f32[2,31,8,128]{3,2,1,0:T(8,128)S(1)}, u32[]{:S(2)}, u32[]{:S(2)}) collective-permute-start(f32[2,31,8,128]{3,2,1,0:T(8,128)S(1)} %get-tuple-element.106), channel_id=1, source_target_pairs={{8,0},{16,8},{24,16},{32,24},{40,32},{48,40},{56,48},{64,56},{72,6... | collective-permute-start | bytes 761864 | tf_op jit(solution)/shard_map/ppermute | solution.py:1105
  64.9 2.2 %collective-permute-start.12 = (f32[8,2,8,128]{3,2,1,0:T(8,128)S(1)}, f32[8,2,8,128]{3,2,1,0:T(8,128)S(1)}, u32[]{:S(2)}, u32[]{:S(2)}) collective-permute-start(f32[8,2,8,128]{3,2,1,0:T(8,128)S(1)} %get-tuple-element.108), channel_id=1, source_target_pairs={{0,1},{1,2},{2,3},{3,4},{4,5},{5,6},{6,7},{7,0},{8,9},{9,10},{10,1... | collective-permute-start | bytes 196616 | tf_op jit(solution)/shard_map/ppermute | solution.py:1090
  64.9 3.9 %collective-permute-start.13 = (f32[8,2,8,128]{3,2,1,0:T(8,128)S(1)}, f32[8,2,8,128]{3,2,1,0:T(8,128)S(1)}, u32[]{:S(2)}, u32[]{:S(2)}) collective-permute-start(f32[8,2,8,128]{3,2,1,0:T(8,128)S(1)} %get-tuple-element.109), channel_id=1, source_target_pairs={{1,0},{2,1},{3,2},{4,3},{5,4},{6,5},{7,6},{0,7},{9,8},{10,9},{11,1... | collective-permute-start | bytes 196616 | tf_op jit(solution)/shard_map/ppermute | solution.py:1090

commit v5 on v4

--- a/solution.py
+++ b/solution.py
@@ -224,6 +224,15 @@
     return 1.0 - outflow[i, column].astype(F32) * top
 
 
+def keep_at(keeps, i, column):
+    return jnp.where(row_ids() == 7, spread_row(keeps[i, column : column + 1, :]), 1.0)
+
+
+def keep_rows(outflow):
+    last = lax.broadcasted_iota(jnp.int32, (1, 1, 128), 2) == 127
+    return 1.0 - jnp.where(last, outflow.astype(F32)[:, :, None], 0.0)
+
+
 def ghost_keep(message, i):
     return jnp.where(row_ids() == 7, message[i, FACTS], 1.0)
 
@@ -262,7 +271,17 @@
     return jax.ShapeDtypeStruct((count, rows, 8, 128), F32)
 
 
+class Place:
+    def __init__(self, sizes):
+        self.sizes = sizes
+
+    def __getitem__(self, index):
+        return self.sizes[index // 2] if index % 2 else lax.axis_index(("dom", "inner")[index // 2])
+
+
 def call(body, outs, scalars, scratch, name, args, flops):
+    if isinstance(args[0], Place):
+        body, args, scalars = functools.partial(body, args[0]), args[1:], scalars - 1
     bytes_accessed = sum(4 * math.prod(a.shape) for a in (*args, *outs))
     return pl.pallas_call(
         body,
@@ -477,24 +496,19 @@
                 image[i, target[q]] = value
 
 
-def finish_residual(wanted, image, source_row, outflow, from_low, from_high, put):
-    top = top_flags()
+def finish_residual(wanted, image, source_row, keeps, from_low, from_high, put):
     for i in wanted:
 
         def own_row(y, column, i=i):
             value = source_row(i, y) - image[i, y]
-            put(i, y, own_keep(outflow, top, i, column) * value)
+            put(i, y, keep_at(keeps, i, column) * value)
 
         put(i, 0, ghost_keep(from_low, i) * (source_row(i, 0) - image[i, 0]))
         put(i, 30, ghost_keep(from_high, i) * (source_row(i, 30) - image[i, 30]))
         own_row(29, 31)
 
-        def step(e, carry, own_row=own_row):
-            for j in range(7):
-                own_row(1 + 7 * e + j, 8 * e + j)
-            return carry
-
-        lax.fori_loop(0, 4, step, 0, unroll=True)
+        for n in range(28):
+            own_row(n + 1, column_of(n))
 
 
 def put_edges(low, high):
@@ -602,7 +616,7 @@
 
 
 def first_join_body(
-    wanted, place, outflow, start, from_low, from_high, table,
+    wanted, place, keeps, start, from_low, from_high, table,
     own_image, source_part, *rest,
 ):
     low_flag, high_flag = ends(place, 1)
@@ -617,7 +631,7 @@
     )
     put = put_edges(*outs[:2]) if wanted is EDGES else put_inner(*outs)
     finish_residual(
-        wanted, image, source_rows(place, source_part, from_low, from_high), outflow,
+        wanted, image, source_rows(place, source_part, from_low, from_high), keeps,
         from_low, from_high, put,
     )
     if wanted is EDGES:
@@ -859,15 +873,15 @@
 
 def residual_out(place, low, inner, high, received):
     return pl.pallas_call(
-        residual_body,
+        functools.partial(residual_body, place),
         out_shape=layers(8, 32),
-        in_specs=[whole(pltpu.SMEM)] + [whole()] * 5,
+        in_specs=[whole()] * 5,
         out_specs=whole(pltpu.HBM),
         scratch_shapes=[pltpu.VMEM((8, 32, 8, 128), F32), pltpu.SemaphoreType.DMA((8,))],
         cost_estimate=pl.CostEstimate(flops=10**7, bytes_accessed=2**22, transcendentals=0),
         compiler_params=pltpu.CompilerParams(vmem_limit_bytes=VMEM_BYTES),
         name="residual",
-    )(place, low, inner, high, *received)
+    )(low, inner, high, *received)
 
 
 def fold_row(i, y, low, inner, high, from_low, from_high):
@@ -882,45 +896,59 @@
     return high[0, y] + from_high[1, y]
 
 
-def fold_body(count, place, outflow, low, inner, high, first, second, to_low, to_high):
-    top = top_flags()
+def fold_body(count, wanted, place, keeps, low, inner, high, first, second, to_low, to_high):
     parts = (low, inner, high, *arrived(place, first, second))
+    fold_news(count, wanted, keeps, parts, to_low, to_high)
+
+
+def fold_inner_body(keeps, inner, to_low, to_high):
+    parts = (None, inner, None, None, None)
+    fold_news(3, INNER, keeps, parts, to_low, to_high)
+
+
+def fold_news(count, wanted, keeps, parts, to_low, to_high):
     sides = ((to_low, 0, 1, UPPER_POINTS), (to_high, 31 - count, 22, LOWER_POINTS))
-    for i in range(8):
+    for at, i in enumerate(wanted):
         for target, start, base, points in sides:
             for n in range(count):
-                target[i, n] = fold_row(i, start + n, *parts)
+                target[at, n] = fold_row(i, start + n, *parts)
             if count == 3:
                 rows = []
                 for point in points:
                     y = base + point
-                    keep = own_keep(outflow, top, i, column_of(y - 1))
+                    keep = keep_at(keeps, i, column_of(y - 1))
                     rows.append(keep * fold_row(i, y, *parts))
-                target[i, 3], target[i, 4] = contract(points, rows)
+                target[at, 3], target[at, 4] = contract(points, rows)
+
+
+class EveryLayer:
+    def __init__(self, edges, inner):
+        self.edges, self.inner = edges, inner
+
+    def __getitem__(self, index):
+        i, *rest = index
+        if i in EDGES:
+            return self.edges[(EDGES.index(i), *rest)]
+        return self.inner[(i - 2, *rest)]
 
 
 def update_body(
-    place, outflow, start, coefficients, table, low, inner, high,
+    place, keeps, start, coefficients, table, low, inner, high,
     first, second, field, image, planes,
 ):
-    top = top_flags()
     parts = (low, inner, high, *arrived(place, first, second))
     for i in range(8):
         field[i, 0] = fold_row(i, 0, *parts)
         field[i, 30] = fold_row(i, 30, *parts)
 
         def row(y, column, i=i):
-            value = own_keep(outflow, top, i, column) * fold_row(i, y, *parts)
+            value = keep_at(keeps, i, column) * fold_row(i, y, *parts)
             field[i, y] = start[i, column] + value
 
         row(29, 31)
 
-        def step(e, carry, row=row):
-            for j in range(7):
-                row(1 + 7 * e + j, 8 * e + j)
-            return carry
-
-        lax.fori_loop(0, 4, step, 0)
+        for n in range(28):
+            row(n + 1, column_of(n))
     own_elements(
         [(1, field, 8, False, False), (2, field, 15, True, False)],
         own_gains(coefficients), table, planes, image, -7,
@@ -928,17 +956,16 @@
 
 
 def second_rows_body(
-    place, outflow, from_low, from_high, field, low_news, high_news, rows, changed
+    place, keeps, from_low, from_high, field, low_news, high_news, rows, changed
 ):
-    top = top_flags()
     low_flag, high_flag = ends(place, 1)
     for i in range(8):
         for n in range(2):
-            news = own_keep(outflow, top, i, n) * (low_flag * low_news[i, 1 + n])
+            news = keep_at(keeps, i, n) * (low_flag * low_news[i, 1 + n])
             value = field[i, 1 + n] + news
             rows[i, n] = value
             changed[i, n] = value
-            news = own_keep(outflow, top, i, 30 + n) * (high_flag * high_news[i, n])
+            news = keep_at(keeps, i, 30 + n) * (high_flag * high_news[i, n])
             value = field[i, 28 + n] + news
             rows[i, 14 + n] = value
             changed[i, 2 + n] = value
@@ -955,7 +982,7 @@
 
 
 def second_residual(
-    wanted, place, outflow, coefficients, from_low, from_high, table,
+    wanted, place, keeps, coefficients, from_low, from_high, table,
     rows, middle_image, source_part, planes, image, put,
 ):
     low_flag, high_flag = ends(place, 1)
@@ -972,48 +999,49 @@
         table, planes, image, wanted,
     )
     finish_residual(
-        wanted, image, source_rows(place, source_part, from_low, from_high), outflow,
+        wanted, image, source_rows(place, source_part, from_low, from_high), keeps,
         from_low, from_high, put,
     )
 
 
 def second_edges_body(
-    place, outflow, coefficients, from_low, from_high, table,
-    field, middle_image, source_part, low_news, high_news,
+    place, keeps, coefficients, from_low, from_high, table,
+    field, middle_image, source_part, low_edges, high_edges, low_inner, high_inner,
     changed, rows, low, high, first, second, planes, image,
 ):
+    low_news = EveryLayer(low_edges, low_inner)
+    high_news = EveryLayer(high_edges, high_inner)
     second_rows_body(
-        place, outflow, from_low, from_high, field, low_news, high_news, rows, changed
+        place, keeps, from_low, from_high, field, low_news, high_news, rows, changed
     )
     second_residual(
-        EDGES, place, outflow, coefficients, from_low, from_high, table,
+        EDGES, place, keeps, coefficients, from_low, from_high, table,
         rows, middle_image, source_part, planes, image, put_edges(low, high),
     )
     hand_over(place, low, high, first, second)
 
 
 def second_inner_body(
-    place, outflow, coefficients, from_low, from_high, table,
+    place, keeps, coefficients, from_low, from_high, table,
     rows, middle_image, source_part, low, high, inner, planes, image,
 ):
     second_residual(
-        INNER, place, outflow, coefficients, from_low, from_high, table,
+        INNER, place, keeps, coefficients, from_low, from_high, table,
         rows, middle_image, source_part, planes, image,
         put_inner(low, high, inner),
     )
 
 
 def last_update_body(
-    place, outflow, field, changed, low, inner, high, first, second,
+    place, keeps, field, changed, low, inner, high, first, second,
     result, edges, layer, semaphores,
 ):
-    top = top_flags()
     parts = (low, inner, high, *arrived(place, first, second))
     copies = []
     for i in range(8):
         for n in range(29):
             column = column_of(n)
-            keep = own_keep(outflow, top, i, column)
+            keep = keep_at(keeps, i, column)
             if n < 2:
                 value = changed[i, n]
             elif n > 26:
@@ -1036,29 +1064,28 @@
         copy.wait()
 
 
-def last_update(place, outflow, field, changed, solved):
+def last_update(place, keeps, field, changed, solved):
     return pl.pallas_call(
-        last_update_body,
+        functools.partial(last_update_body, place),
         out_shape=(layers(8, 32), layers(8, 4)),
-        in_specs=[whole(pltpu.SMEM)] * 2 + [whole()] * 7,
+        in_specs=[whole()] * 8,
         out_specs=(whole(pltpu.HBM), whole()),
         scratch_shapes=[pltpu.VMEM((8, 32, 8, 128), F32), pltpu.SemaphoreType.DMA((8,))],
         compiler_params=pltpu.CompilerParams(vmem_limit_bytes=VMEM_BYTES),
         cost_estimate=pl.CostEstimate(flops=10**7, bytes_accessed=2**22, transcendentals=0),
         name="last_update",
-    )(place, outflow, field, changed, *solved)
+    )(keeps, field, changed, *solved)
 
 
 def last_join_body(
-    place, outflow, edges, low_news, high_news, before, result, rows, semaphores
+    place, keeps, edges, low_news, high_news, before, result, rows, semaphores
 ):
-    top = top_flags()
     copies = []
     low_flag, high_flag = ends(place, 1)
     for first, at, flag, news in ((0, 0, low_flag, low_news), (30, 2, high_flag, high_news)):
         for i in range(8):
             for n in range(2):
-                keep = own_keep(outflow, top, i, first + n)
+                keep = keep_at(keeps, i, first + n)
                 rows[i, at + n] = edges[i, at + n] + keep * (flag * news[i, n])
         copies.append(
             pltpu.make_async_copy(
@@ -1070,17 +1097,17 @@
         copy.wait()
 
 
-def last_join(place, outflow, edges, low_news, high_news, before):
+def last_join(place, keeps, edges, low_news, high_news, before):
     return pl.pallas_call(
-        last_join_body,
+        functools.partial(last_join_body, place),
         out_shape=layers(8, 32),
-        in_specs=[whole(pltpu.SMEM)] * 2 + [whole()] * 3 + [whole(pltpu.HBM)],
+        in_specs=[whole()] * 4 + [whole(pltpu.HBM)],
         out_specs=whole(pltpu.HBM),
         scratch_shapes=[pltpu.VMEM((8, 4, 8, 128), F32), pltpu.SemaphoreType.DMA((2,))],
-        input_output_aliases={5: 0},
+        input_output_aliases={4: 0},
         compiler_params=pltpu.CompilerParams(vmem_limit_bytes=VMEM_BYTES),
         name="last_join",
-    )(place, outflow, edges, low_news, high_news, before)
+    )(keeps, edges, low_news, high_news, before)
 
 
 def exchange(to_low, to_high, axis):
@@ -1140,27 +1167,28 @@
     return (out_low, out_inner, out_high, *returned), extra
 
 
-def fold(count, place, outflow, parts):
-    message = layers(8, 5 if count == 3 else count)
+def fold(count, wanted, place, keeps, parts):
+    message = layers(len(wanted), 5 if count == 3 else count)
     return call(
-        functools.partial(fold_body, count), [message, message], 2, [],
-        "fold", (place, outflow, *parts), 10**6,
+        functools.partial(fold_body, count, wanted), [message, message], 1, [],
+        "fold", (place, keeps, *parts), 10**6,
+    )
+
+
+def fold_inner(keeps, inner):
+    return call(
+        fold_inner_body, [layers(4, 5), layers(4, 5)], 0, [], "fold_inner",
+        (keeps, inner), 10**6,
     )
 
 
 def shards(start, source, coefficients, outflow):
     table = jnp.asarray(OPERATOR)
-    place = jnp.stack(
-        [
-            lax.axis_index("dom"),
-            lax.axis_size("dom"),
-            lax.axis_index("inner"),
-            lax.axis_size("inner"),
-        ]
-    ).astype(jnp.int32)
-    start, source, coefficients, to_low, to_high = lax.optimization_barrier(
-        (start, source, coefficients, *pack_first(start, source, coefficients, outflow))
-    )
+    place = Place((lax.axis_size("dom"), lax.axis_size("inner")))
+    start, source, coefficients, outflow, to_low, to_high = lax.optimization_barrier(
+        (start, source, coefficients, outflow, *pack_first(start, source, coefficients, outflow))
+    )
+    keeps = keep_rows(outflow)
     from_low, from_high = exchange(to_low, to_high, "inner")
 
     def own_image(wanted, name, coefficients, start, source, table, kept):
@@ -1178,10 +1206,10 @@
         "reciprocals",
         (coefficients, *[jnp.asarray(t) for t in VALUES]), 10**8,
     )
-    joined = (place, outflow, start, from_low, from_high, table)
+    joined = (place, keeps, start, from_low, from_high, table)
     join_scratch = [plane_scratch(), pltpu.VMEM((8, 31, 8, 128), F32)]
     edge_parts = call(
-        functools.partial(first_join_body, EDGES), [layers(2, 31)] * 4, 2,
+        functools.partial(first_join_body, EDGES), [layers(2, 31)] * 4, 1,
         join_scratch, "first_edges", (*joined, edge_image, edge_source), 10**8,
     )
     late_start, late_source, *edge_parts = lax.optimization_barrier((start, source, *edge_parts))
@@ -1196,31 +1224,32 @@
 
     def first_inner():
         return call(
-            first_inner_body, [layers(6, 31)], 2, join_scratch, "first_inner",
+            first_inner_body, [layers(6, 31)], 1, join_scratch, "first_inner",
             (*joined, inner_image, inner_source, *edge_parts[:2]), 10**8,
         )[0]
 
     solved, _ = solve(place, reciprocals, edge_parts, first_inner, lambda *_: None)
-    news = exchange(*fold(3, place, outflow, solved), "inner")
+    inner_news = exchange(*fold_inner(keeps, solved[1]), "inner")
+    news = exchange(*fold(3, EDGES, place, keeps, solved), "inner")
     field, middle_image = call(
-        update_body, [layers(8, 31), layers(8, 15)], 2, [plane_scratch()], "update",
-        (place, outflow, start, coefficients, table, *solved), 2 * 10**8,
+        update_body, [layers(8, 31), layers(8, 15)], 1, [plane_scratch()], "update",
+        (place, keeps, start, coefficients, table, *solved), 2 * 10**8,
     )
     operands = (
-        place, outflow, coefficients, from_low, from_high, table
+        place, keeps, coefficients, from_low, from_high, table
     )
     join_scratch = [plane_scratch(), pltpu.VMEM((8, 31, 8, 128), F32)]
     changed, rows, *edge_parts = call(
         second_edges_body,
         [layers(8, 4), layers(8, 22)] + [layers(2, 31)] * 4,
-        2, join_scratch, "second_edges",
-        (*operands, field, middle_image, edge_source, *news), 2 * 10**8,
+        1, join_scratch, "second_edges",
+        (*operands, field, middle_image, edge_source, *news, *inner_news), 2 * 10**8,
     )
     low, high = edge_parts[:2]
 
     def second_inner():
         return call(
-            second_inner_body, [layers(6, 31)], 2, join_scratch, "second_inner",
+            second_inner_body, [layers(6, 31)], 1, join_scratch, "second_inner",
             (*operands, rows, middle_image, inner_source, low, high), 2 * 10**8,
         )[0]
 
@@ -1228,9 +1257,9 @@
         place, reciprocals, edge_parts, second_inner,
         lambda inner, received: residual_out(place, low, inner, high, received),
     )
-    news = exchange(*fold(2, place, outflow, solved), "inner")
-    iterate, edges = last_update(place, outflow, field, changed, solved)
-    return last_join(place, outflow, edges, *news, iterate), residual
+    news = exchange(*fold(2, EVERY, place, keeps, solved), "inner")
+    iterate, edges = last_update(place, keeps, field, changed, solved)
+    return last_join(place, keeps, edges, *news, iterate), residual
 
 
 def solution(mesh):

time: 70.8 us -> 65.7 us (0.928)
  Pallas kernels: 31.4 us -> 22.5 us
  waiting for transfers between devices: 20.8 us -> 22.1 us
  starting transfers between devices: 15.3 us -> 16.4 us
  other arithmetic: 0.08 us -> 0.79 us
    pallas_call x16 -> x17, Pallas kernels: 24.6 us -> 17.5 us  [call(): pl.pallas_call(body, out_shape=tuple(outs), in_specs=[whole(pltpu.SMEM if...]
    pallas_call x3, Pallas kernels: 4.81 us -> 3.06 us  [the longest x1 1.3 us: residual_out(): pl.pallas_call(functools.partial(residual_body, place), out_shape=layers(...]
    ppermute x3 -> x4, starting transfers between devices: 1.81 us -> 3.25 us  [exchange(): lax.ppermute(to_high, axis, upward)]
    unnamed x18 -> x16, local copies, waits for them, and re-layouts: 1.63 us -> 2.22 us
    ppermute x3 -> x4, waiting for transfers between devices: 6.45 us -> 6.99 us  [exchange(): lax.ppermute(to_low, axis, downward)]
  transfers between devices with their start and end apart: 14 -> 16, of which waited for: 11 -> 12; matrix products, arithmetic and copies ran while one was open for 0% -> 1% of each run, Pallas kernels for 29% -> 24%
where the time goes in v5:
time: 65.7 us; the launch traced here: 64.9 us
  Pallas kernels  22.5 us (34%)
  waiting for transfers between devices  22.1 us (34%)
  starting transfers between devices  16.4 us (25%)
  local copies, waits for them, and re-layouts  2.22 us (3%)
  between operations  0.89 us (1%)
  other arithmetic  0.79 us (1%)
    pallas_call x17, Pallas kernels, call(): pl.pallas_call(body, out_shape=tuple(outs), in_specs=[whole(pltpu.SMEM if...  17.5 us
    ppermute x4, starting transfers between devices, exchange_along_first(): lax.ppermute(first, axes, forward)  12.1 us
    ppermute x4, waiting for transfers between devices, exchange_along_first(): lax.ppermute(second, axes, backward)  8.6 us
    ppermute x4, waiting for transfers between devices, exchange(): lax.ppermute(to_low, axis, downward)  6.99 us
    ppermute x4, waiting for transfers between devices, exchange_along_first(): lax.ppermute(first, axes, forward)  6.18 us
    ppermute x4, starting transfers between devices, exchange(): lax.ppermute(to_high, axis, upward)  3.25 us
    unnamed x16, local copies, waits for them, and re-layouts  2.22 us
    pallas_call x1, Pallas kernels, pack_first(): pl.pallas_call(pack_body, out_shape=(layers(8, 5), layers(8, 5)), in_spec...  1.98 us
  transfers between devices with their start and end apart: 16, of which 12 were waited for; matrix products, arithmetic and copies ran while one was open for 1% of the time, Pallas kernels for 24%

profile of v5, /device:TPU:25, one launch (start us, length us, event | category | flops | bytes accessed | tf_op | source)
XLA Modules:
  0.0 64.9 jit_solution(3088947652625568012)
XLA Ops:
  0.6 2.0 %pack_first.1 = (f32[8,5,8,128]{3,2,1,0:T(8,128)}, f32[8,5,8,128]{3,2,1,0:T(8,128)}) custom-call(s32[8,32]{1,0:T(8,128)} %outflow.1, f32[8,32,8,128]{3,2,1,0:T(8,128)} %start.5, f32[8,32,8,128]{3,2,1,0:T(8,128)} %source.3, f32[3,1,4,128]{3,2,1,0:T(4,128)} %coefficients.2), custom_call_target="tpu_custom_call" | custom-call | tf_op jit(solution)/shard_map/pack_first/pallas_call | solution.py:350
  2.6 1.8 %collective-permute-start = (f32[8,5,8,128]{3,2,1,0:T(8,128)}, f32[8,5,8,128]{3,2,1,0:T(8,128)S(1)}, u32[]{:S(2)}, u32[]{:S(2)}) collective-permute-start(f32[8,5,8,128]{3,2,1,0:T(8,128)} %get-tuple-element.69), channel_id=1, source_target_pairs={{0,1},{1,2},{2,3},{3,4},{4,5},{5,6},{6,7},{7,0},{8,9},{9,10},{10,1... | collective-permute-start | bytes 491528 | tf_op jit(solution)/shard_map/ppermute | solution.py:1117
  7.4 2.0 %collective-permute-done.1.from_high.refs_3_ = f32[8,5,8,128]{3,2,1,0:T(8,128)S(1)} collective-permute-done((f32[8,5,8,128]{3,2,1,0:T(8,128)}, f32[8,5,8,128]{3,2,1,0:T(8,128)S(1)}, u32[]{:S(2)}, u32[]{:S(2)}) %collective-permute-start.1) | collective-permute-done | bytes 163872 | tf_op jit(solution)/shard_map/ppermute | solution.py:1117
  9.6 4.0 %collective-permute-start.2 = (f32[2,31,8,128]{3,2,1,0:T(8,128)S(1)}, f32[2,31,8,128]{3,2,1,0:T(8,128)S(1)}, u32[]{:S(2)}, u32[]{:S(2)}) collective-permute-start(f32[2,31,8,128]{3,2,1,0:T(8,128)S(1)} %get-tuple-element.85), channel_id=1, source_target_pairs={{0,8},{8,16},{16,24},{24,32},{32,40},{40,48},{48,56},{56,64},{64,7... | collective-permute-start | bytes 761864 | tf_op jit(solution)/shard_map/ppermute | solution.py:1132
  15.8 2.2 %inner_forward.2 = (f32[10,2,128,256]{3,2,1,0:T(8,128)S(1)}, f32[4,2,128,256]{3,2,1,0:T(8,128)S(1)}) custom-call(f32[6,31,8,128]{3,2,1,0:T(8,128)S(1)} %first_inner.1.inner, bf16[128,240]{1,0:T(8,128)(2,1)S(1)} %copy-done.3, f32[10,2,128,256]{3,2,1,0:T(8,128)S(1)} %get-tuple-element.83.reciprocals), custom_call_target="tpu_custom_call" | custom-call | flops 300000000 | bytes 7176192 | tf_op jit(solution)/shard_map/inner_forward/pallas_call | solution.py:286
  18.9 1.9 %collective-permute-done.3.second = f32[2,31,8,128]{3,2,1,0:T(8,128)S(1)} collective-permute-done((f32[2,31,8,128]{3,2,1,0:T(8,128)S(1)}, f32[2,31,8,128]{3,2,1,0:T(8,128)S(1)}, u32[]{:S(2)}, u32[]{:S(2)}) %collective-permute-start.3) | collective-permute-done | bytes 253984 | tf_op jit(solution)/shard_map/ppermute | solution.py:1132
  20.8 1.8 %edge_solve.2 = (f32[2,31,8,128]{3,2,1,0:T(8,128)S(1)}, f32[2,31,8,128]{3,2,1,0:T(8,128)S(1)}, f32[2,31,8,128]{3,2,1,0:T(8,128)S(1)}, f32[2,31,8,128]{3,2,1,0:T(8,128)S(1)}, f32[4,2,128,256]{3,2,1,0:T(8,128)S(1)}) custom-call(f32[6,2,128,256]{3,2,1,0:T(8,128)S(1)} %get-tuple-element.68.blocks, bf16[128,240]{1,0:T(8,128)(2,1)S(1)} %copy-done.3, ...), custom_call_target="tpu_custom_call" | custom-call | flops 1000000000 | bytes 6152192 | tf_op jit(solution)/shard_map/edge_solve/pallas_call | solution.py:286
  22.7 2.5 %collective-permute-start.4 = (f32[2,31,8,128]{3,2,1,0:T(8,128)S(1)}, f32[2,31,8,128]{3,2,1,0:T(8,128)S(1)}, u32[]{:S(2)}, u32[]{:S(2)}) collective-permute-start(f32[2,31,8,128]{3,2,1,0:T(8,128)S(1)} %get-tuple-element.91), channel_id=1, source_target_pairs={{0,8},{8,16},{16,24},{24,32},{32,40},{40,48},{48,56},{56,64},{64,7... | collective-permute-start | bytes 761864 | tf_op jit(solution)/shard_map/ppermute | solution.py:1132
  25.1 2.7 %inner_backward.2.inner = f32[6,31,8,128]{3,2,1,0:T(8,128)S(1)} custom-call(f32[4,2,128,256]{3,2,1,0:T(8,128)S(1)} %get-tuple-element.88.spectral, f32[10,2,128,256]{3,2,1,0:T(8,128)S(1)} %get-tuple-element.89.partial, f32[10,2,128,256]{3,2,1,0:T(8,128)S(1)} %get-tuple-element.83.reciprocals, bf16[320,256]{1,0:T(8,128)(2,1)S(1)} %copy-done.2), custom_call_target="tpu_custom_call" | custom-call | flops 300000000 | bytes 7380992 | tf_op jit(solution)/shard_map/inner_backward/pallas_call | solution.py:286
  27.9 1.4 %collective-permute-start.8 = (f32[4,5,8,128]{3,2,1,0:T(8,128)S(1)}, f32[4,5,8,128]{3,2,1,0:T(8,128)S(1)}, u32[]{:S(2)}, u32[]{:S(2)}) collective-permute-start(f32[4,5,8,128]{3,2,1,0:T(8,128)S(1)} %get-tuple-element.97), channel_id=1, source_target_pairs={{0,1},{1,2},{2,3},{3,4},{4,5},{5,6},{6,7},{7,0},{8,9},{9,10},{10,1... | collective-permute-start | bytes 245768 | tf_op jit(solution)/shard_map/ppermute | solution.py:1117
  29.4 1.3 %collective-permute-done.4.first = f32[2,31,8,128]{3,2,1,0:T(8,128)S(1)} collective-permute-done((f32[2,31,8,128]{3,2,1,0:T(8,128)S(1)}, f32[2,31,8,128]{3,2,1,0:T(8,128)S(1)}, u32[]{:S(2)}, u32[]{:S(2)}) %collective-permute-start.4) | collective-permute-done | bytes 253984 | tf_op jit(solution)/shard_map/ppermute | solution.py:1132
  30.7 2.0 %collective-permute-done.5.second = f32[2,31,8,128]{3,2,1,0:T(8,128)S(1)} collective-permute-done((f32[2,31,8,128]{3,2,1,0:T(8,128)S(1)}, f32[2,31,8,128]{3,2,1,0:T(8,128)S(1)}, u32[]{:S(2)}, u32[]{:S(2)}) %collective-permute-start.5) | collective-permute-done | bytes 253984 | tf_op jit(solution)/shard_map/ppermute | solution.py:1132
  34.3 2.7 %collective-permute-done.7.high_edges = f32[4,5,8,128]{3,2,1,0:T(8,128)S(1)} collective-permute-done((f32[4,5,8,128]{3,2,1,0:T(8,128)S(1)}, f32[4,5,8,128]{3,2,1,0:T(8,128)S(1)}, u32[]{:S(2)}, u32[]{:S(2)}) %collective-permute-start.7) | collective-permute-done | bytes 81952 | tf_op jit(solution)/shard_map/ppermute | solution.py:1117
  37.5 3.7 %collective-permute-start.10 = (f32[2,31,8,128]{3,2,1,0:T(8,128)S(1)}, f32[2,31,8,128]{3,2,1,0:T(8,128)S(1)}, u32[]{:S(2)}, u32[]{:S(2)}) collective-permute-start(f32[2,31,8,128]{3,2,1,0:T(8,128)S(1)} %get-tuple-element.104), channel_id=1, source_target_pairs={{0,8},{8,16},{16,24},{24,32},{32,40},{40,48},{48,56},{56,64},{64,7... | collective-permute-start | bytes 761864 | tf_op jit(solution)/shard_map/ppermute | solution.py:1132
  41.6 2.2 %inner_forward.3 = (f32[10,2,128,256]{3,2,1,0:T(8,128)S(1)}, f32[4,2,128,256]{3,2,1,0:T(8,128)S(1)}) custom-call(f32[6,31,8,128]{3,2,1,0:T(8,128)S(1)} %second_inner.1.inner, bf16[128,240]{1,0:T(8,128)(2,1)S(1)} %copy-done.3, f32[10,2,128,256]{3,2,1,0:T(8,128)S(1)} %get-tuple-element.83.reciprocals), custom_call_target="tpu_custom_call" | custom-call | flops 300000000 | bytes 7176192 | tf_op jit(solution)/shard_map/inner_forward/pallas_call | solution.py:286
  43.8 2.1 %collective-permute-done.10.first = f32[2,31,8,128]{3,2,1,0:T(8,128)S(1)} collective-permute-done((f32[2,31,8,128]{3,2,1,0:T(8,128)S(1)}, f32[2,31,8,128]{3,2,1,0:T(8,128)S(1)}, u32[]{:S(2)}, u32[]{:S(2)}) %collective-permute-start.10) | collective-permute-done | bytes 253984 | tf_op jit(solution)/shard_map/ppermute | solution.py:1132
  46.0 2.5 %collective-permute-done.11.second = f32[2,31,8,128]{3,2,1,0:T(8,128)S(1)} collective-permute-done((f32[2,31,8,128]{3,2,1,0:T(8,128)S(1)}, f32[2,31,8,128]{3,2,1,0:T(8,128)S(1)}, u32[]{:S(2)}, u32[]{:S(2)}) %collective-permute-start.11) | collective-permute-done | bytes 253984 | tf_op jit(solution)/shard_map/ppermute | solution.py:1132
  48.4 1.8 %edge_solve.3 = (f32[2,31,8,128]{3,2,1,0:T(8,128)S(1)}, f32[2,31,8,128]{3,2,1,0:T(8,128)S(1)}, f32[2,31,8,128]{3,2,1,0:T(8,128)S(1)}, f32[2,31,8,128]{3,2,1,0:T(8,128)S(1)}, f32[4,2,128,256]{3,2,1,0:T(8,128)S(1)}) custom-call(f32[6,2,128,256]{3,2,1,0:T(8,128)S(1)} %get-tuple-element.68.blocks, bf16[128,240]{1,0:T(8,128)(2,1)S(1)} %copy-done.3, ...), custom_call_target="tpu_custom_call" | custom-call | flops 1000000000 | bytes 6152192 | tf_op jit(solution)/shard_map/edge_solve/pallas_call | solution.py:286
  50.2 1.9 %collective-permute-start.12 = (f32[2,31,8,128]{3,2,1,0:T(8,128)S(1)}, f32[2,31,8,128]{3,2,1,0:T(8,128)S(1)}, u32[]{:S(2)}, u32[]{:S(2)}) collective-permute-start(f32[2,31,8,128]{3,2,1,0:T(8,128)S(1)} %get-tuple-element.111), channel_id=1, source_target_pairs={{0,8},{8,16},{16,24},{24,32},{32,40},{40,48},{48,56},{56,64},{64,7... | collective-permute-start | bytes 761864 | tf_op jit(solution)/shard_map/ppermute | solution.py:1132
  52.2 1.3 %residual.1 = f32[8,32,8,128]{3,2,1,0:T(8,128)} custom-call(f32[2,31,8,128]{3,2,1,0:T(8,128)S(1)} %get-tuple-element.101.low, f32[6,31,8,128]{3,2,1,0:T(8,128)S(1)} %second_inner.1.inner, f32[2,31,8,128]{3,2,1,0:T(8,128)S(1)} %get-tuple-element.102.high, f32[2,31,8,128]{3,2,1,0:T(8,128)S(1)} %collective-permute-done.10.first, ...), custom_call_target="tpu_custom_call" | custom-call | flops 10000000 | bytes 4194304 | tf_op jit(solution)/shard_map/residual/pallas_call | solution.py:875
  53.5 2.7 %inner_backward.3.inner = f32[6,31,8,128]{3,2,1,0:T(8,128)S(1)} custom-call(f32[4,2,128,256]{3,2,1,0:T(8,128)S(1)} %get-tuple-element.107.spectral, f32[10,2,128,256]{3,2,1,0:T(8,128)S(1)} %get-tuple-element.108.partial, f32[10,2,128,256]{3,2,1,0:T(8,128)S(1)} %get-tuple-element.83.reciprocals, bf16[320,256]{1,0:T(8,128)(2,1)S(1)} %copy-done.2), custom_call_target="tpu_custom_call" | custom-call | flops 300000000 | bytes 7380992 | tf_op jit(solution)/shard_map/inner_backward/pallas_call | solution.py:286
  56.2 1.9 %collective-permute-done.12.first = f32[2,31,8,128]{3,2,1,0:T(8,128)S(1)} collective-permute-done((f32[2,31,8,128]{3,2,1,0:T(8,128)S(1)}, f32[2,31,8,128]{3,2,1,0:T(8,128)S(1)}, u32[]{:S(2)}, u32[]{:S(2)}) %collective-permute-start.12) | collective-permute-done | bytes 253984 | tf_op jit(solution)/shard_map/ppermute | solution.py:1132
  58.1 2.2 %collective-permute-done.13.second = f32[2,31,8,128]{3,2,1,0:T(8,128)S(1)} collective-permute-done((f32[2,31,8,128]{3,2,1,0:T(8,128)S(1)}, f32[2,31,8,128]{3,2,1,0:T(8,128)S(1)}, u32[]{:S(2)}, u32[]{:S(2)}) %collective-permute-start.13) | collective-permute-done | bytes 253984 | tf_op jit(solution)/shard_map/ppermute | solution.py:1132
  61.9 2.3 %collective-permute-done.15.high_news = f32[8,2,8,128]{3,2,1,0:T(8,128)S(1)} collective-permute-done((f32[8,2,8,128]{3,2,1,0:T(8,128)S(1)}, f32[8,2,8,128]{3,2,1,0:T(8,128)S(1)}, u32[]{:S(2)}, u32[]{:S(2)}) %collective-permute-start.15) | collective-permute-done | bytes 65568 | tf_op jit(solution)/shard_map/ppermute | solution.py:1117
  (48 shorter events, 10.9 us)
Async XLA Ops:
  0.6 4.5 %copy-start.1 = (f32[8,32,8,128]{3,2,1,0:T(8,128)S(1)}, f32[8,32,8,128]{3,2,1,0:T(8,128)}, u32[]{:S(2)}) copy-start(f32[8,32,8,128]{3,2,1,0:T(8,128)} %source.3) | copy-start | bytes 3145732
  0.6 4.5 %copy-start = (f32[8,32,8,128]{3,2,1,0:T(8,128)S(1)}, f32[8,32,8,128]{3,2,1,0:T(8,128)}, u32[]{:S(2)}) copy-start(f32[8,32,8,128]{3,2,1,0:T(8,128)} %start.5) | copy-start | bytes 3145732
  2.6 4.7 %collective-permute-start = (f32[8,5,8,128]{3,2,1,0:T(8,128)}, f32[8,5,8,128]{3,2,1,0:T(8,128)S(1)}, u32[]{:S(2)}, u32[]{:S(2)}) collective-permute-start(f32[8,5,8,128]{3,2,1,0:T(8,128)} %get-tuple-element.69), channel_id=1, source_target_pairs={{0,1},{1,2},{2,3},{3,4},{4,5},{5,6},{6,7},{7,0},{8,9},{9,10},{10,1... | collective-permute-start | bytes 491528 | tf_op jit(solution)/shard_map/ppermute | solution.py:1117
  4.4 5.0 %collective-permute-start.1 = (f32[8,5,8,128]{3,2,1,0:T(8,128)}, f32[8,5,8,128]{3,2,1,0:T(8,128)S(1)}, u32[]{:S(2)}, u32[]{:S(2)}) collective-permute-start(f32[8,5,8,128]{3,2,1,0:T(8,128)} %get-tuple-element.70), channel_id=1, source_target_pairs={{1,0},{2,1},{3,2},{4,3},{5,4},{6,5},{7,6},{0,7},{9,8},{10,9},{11,1... | collective-permute-start | bytes 491528 | tf_op jit(solution)/shard_map/ppermute | solution.py:1117
  5.1 0.9 %copy-start.4 = (bf16[144,192]{1,0:T(8,128)(2,1)S(1)}, bf16[144,192]{1,0:T(8,128)(2,1)}, u32[]{:S(2)}) copy-start(bf16[144,192]{1,0:T(8,128)(2,1)} %constant.16.clone.table) | copy-start | bytes 165892
  6.0 0.7 %copy-start.5 = (f32[3,1,4,128]{3,2,1,0:T(4,128)S(1)}, f32[3,1,4,128]{3,2,1,0:T(4,128)}, u32[]{:S(2)}) copy-start(f32[3,1,4,128]{3,2,1,0:T(4,128)} %coefficients.2) | copy-start | bytes 18436
  6.7 6.9 %copy-start.6 = (f32[128,128]{1,0:T(8,128)S(1)}, f32[128,128]{1,0:T(8,128)}, u32[]{:S(2)}) copy-start(f32[128,128]{1,0:T(8,128)} %constant.18.clone.third_values) | copy-start | bytes 196612
  6.7 6.9 %copy-start.7 = (f32[128,128]{1,0:T(8,128)S(1)}, f32[128,128]{1,0:T(8,128)}, u32[]{:S(2)}) copy-start(f32[128,128]{1,0:T(8,128)} %constant.17.clone.second_values) | copy-start | bytes 196612
  9.6 9.3 %collective-permute-start.2 = (f32[2,31,8,128]{3,2,1,0:T(8,128)S(1)}, f32[2,31,8,128]{3,2,1,0:T(8,128)S(1)}, u32[]{:S(2)}, u32[]{:S(2)}) collective-permute-start(f32[2,31,8,128]{3,2,1,0:T(8,128)S(1)} %get-tuple-element.85), channel_id=1, source_target_pairs={{0,8},{8,16},{16,24},{24,32},{32,40},{40,48},{48,56},{56,64},{64,7... | collective-permute-start | bytes 761864 | tf_op jit(solution)/shard_map/ppermute | solution.py:1132
  13.6 7.2 %collective-permute-start.3 = (f32[2,31,8,128]{3,2,1,0:T(8,128)S(1)}, f32[2,31,8,128]{3,2,1,0:T(8,128)S(1)}, u32[]{:S(2)}, u32[]{:S(2)}) collective-permute-start(f32[2,31,8,128]{3,2,1,0:T(8,128)S(1)} %get-tuple-element.86), channel_id=1, source_target_pairs={{8,0},{16,8},{24,16},{32,24},{40,32},{48,40},{56,48},{64,56},{72,6... | collective-permute-start | bytes 761864 | tf_op jit(solution)/shard_map/ppermute | solution.py:1132
  14.9 0.8 %copy-start.3 = (bf16[128,240]{1,0:T(8,128)(2,1)S(1)}, bf16[128,240]{1,0:T(8,128)(2,1)}, u32[]{:S(2)}) copy-start(bf16[128,240]{1,0:T(8,128)(2,1)} %constant.19.clone.forward) | copy-start | bytes 184324
  15.2 5.7 %copy-start.2 = (bf16[320,256]{1,0:T(8,128)(2,1)S(1)}, bf16[320,256]{1,0:T(8,128)(2,1)}, u32[]{:S(2)}) copy-start(bf16[320,256]{1,0:T(8,128)(2,1)} %constant.20.clone.backward) | copy-start | bytes 491524
  22.7 8.0 %collective-permute-start.4 = (f32[2,31,8,128]{3,2,1,0:T(8,128)S(1)}, f32[2,31,8,128]{3,2,1,0:T(8,128)S(1)}, u32[]{:S(2)}, u32[]{:S(2)}) collective-permute-start(f32[2,31,8,128]{3,2,1,0:T(8,128)S(1)} %get-tuple-element.91), channel_id=1, source_target_pairs={{0,8},{8,16},{16,24},{24,32},{32,40},{40,48},{48,56},{56,64},{64,7... | collective-permute-start | bytes 761864 | tf_op jit(solution)/shard_map/ppermute | solution.py:1132
  25.1 7.6 %collective-permute-start.5 = (f32[2,31,8,128]{3,2,1,0:T(8,128)S(1)}, f32[2,31,8,128]{3,2,1,0:T(8,128)S(1)}, u32[]{:S(2)}, u32[]{:S(2)}) collective-permute-start(f32[2,31,8,128]{3,2,1,0:T(8,128)S(1)} %get-tuple-element.92), channel_id=1, source_target_pairs={{8,0},{16,8},{24,16},{32,24},{40,32},{48,40},{56,48},{64,56},{72,6... | collective-permute-start | bytes 761864 | tf_op jit(solution)/shard_map/ppermute | solution.py:1132
  27.9 6.0 %collective-permute-start.8 = (f32[4,5,8,128]{3,2,1,0:T(8,128)S(1)}, f32[4,5,8,128]{3,2,1,0:T(8,128)S(1)}, u32[]{:S(2)}, u32[]{:S(2)}) collective-permute-start(f32[4,5,8,128]{3,2,1,0:T(8,128)S(1)} %get-tuple-element.97), channel_id=1, source_target_pairs={{0,1},{1,2},{2,3},{3,4},{4,5},{5,6},{6,7},{7,0},{8,9},{9,10},{10,1... | collective-permute-start | bytes 245768 | tf_op jit(solution)/shard_map/ppermute | solution.py:1117
  29.4 4.6 %collective-permute-start.9 = (f32[4,5,8,128]{3,2,1,0:T(8,128)S(1)}, f32[4,5,8,128]{3,2,1,0:T(8,128)S(1)}, u32[]{:S(2)}, u32[]{:S(2)}) collective-permute-start(f32[4,5,8,128]{3,2,1,0:T(8,128)S(1)} %get-tuple-element.98), channel_id=1, source_target_pairs={{1,0},{2,1},{3,2},{4,3},{5,4},{6,5},{7,6},{0,7},{9,8},{10,9},{11,1... | collective-permute-start | bytes 245768 | tf_op jit(solution)/shard_map/ppermute | solution.py:1117
  32.8 1.5 %collective-permute-start.6 = (f32[4,5,8,128]{3,2,1,0:T(8,128)S(1)}, f32[4,5,8,128]{3,2,1,0:T(8,128)S(1)}, u32[]{:S(2)}, u32[]{:S(2)}) collective-permute-start(f32[4,5,8,128]{3,2,1,0:T(8,128)S(1)} %get-tuple-element.95), channel_id=1, source_target_pairs={{0,1},{1,2},{2,3},{3,4},{4,5},{5,6},{6,7},{7,0},{8,9},{9,10},{10,1... | collective-permute-start | bytes 245768 | tf_op jit(solution)/shard_map/ppermute | solution.py:1117
  32.8 4.2 %collective-permute-start.7 = (f32[4,5,8,128]{3,2,1,0:T(8,128)S(1)}, f32[4,5,8,128]{3,2,1,0:T(8,128)S(1)}, u32[]{:S(2)}, u32[]{:S(2)}) collective-permute-start(f32[4,5,8,128]{3,2,1,0:T(8,128)S(1)} %get-tuple-element.96), channel_id=1, source_target_pairs={{1,0},{2,1},{3,2},{4,3},{5,4},{6,5},{7,6},{0,7},{9,8},{10,9},{11,1... | collective-permute-start | bytes 245768 | tf_op jit(solution)/shard_map/ppermute | solution.py:1117
  37.5 8.5 %collective-permute-start.10 = (f32[2,31,8,128]{3,2,1,0:T(8,128)S(1)}, f32[2,31,8,128]{3,2,1,0:T(8,128)S(1)}, u32[]{:S(2)}, u32[]{:S(2)}) collective-permute-start(f32[2,31,8,128]{3,2,1,0:T(8,128)S(1)} %get-tuple-element.104), channel_id=1, source_target_pairs={{0,8},{8,16},{16,24},{24,32},{32,40},{40,48},{48,56},{56,64},{64,7... | collective-permute-start | bytes 761864 | tf_op jit(solution)/shard_map/ppermute | solution.py:1132
  41.2 7.2 %collective-permute-start.11 = (f32[2,31,8,128]{3,2,1,0:T(8,128)S(1)}, f32[2,31,8,128]{3,2,1,0:T(8,128)S(1)}, u32[]{:S(2)}, u32[]{:S(2)}) collective-permute-start(f32[2,31,8,128]{3,2,1,0:T(8,128)S(1)} %get-tuple-element.105), channel_id=1, source_target_pairs={{8,0},{16,8},{24,16},{32,24},{40,32},{48,40},{56,48},{64,56},{72,6... | collective-permute-start | bytes 761864 | tf_op jit(solution)/shard_map/ppermute | solution.py:1132
  50.2 7.8 %collective-permute-start.12 = (f32[2,31,8,128]{3,2,1,0:T(8,128)S(1)}, f32[2,31,8,128]{3,2,1,0:T(8,128)S(1)}, u32[]{:S(2)}, u32[]{:S(2)}) collective-permute-start(f32[2,31,8,128]{3,2,1,0:T(8,128)S(1)} %get-tuple-element.111), channel_id=1, source_target_pairs={{0,8},{8,16},{16,24},{24,32},{32,40},{40,48},{48,56},{56,64},{64,7... | collective-permute-start | bytes 761864 | tf_op jit(solution)/shard_map/ppermute | solution.py:1132
  52.2 8.1 %collective-permute-start.13 = (f32[2,31,8,128]{3,2,1,0:T(8,128)S(1)}, f32[2,31,8,128]{3,2,1,0:T(8,128)S(1)}, u32[]{:S(2)}, u32[]{:S(2)}) collective-permute-start(f32[2,31,8,128]{3,2,1,0:T(8,128)S(1)} %get-tuple-element.112), channel_id=1, source_target_pairs={{8,0},{16,8},{24,16},{32,24},{40,32},{48,40},{56,48},{64,56},{72,6... | collective-permute-start | bytes 761864 | tf_op jit(solution)/shard_map/ppermute | solution.py:1132
  60.3 1.6 %collective-permute-start.14 = (f32[8,2,8,128]{3,2,1,0:T(8,128)S(1)}, f32[8,2,8,128]{3,2,1,0:T(8,128)S(1)}, u32[]{:S(2)}, u32[]{:S(2)}) collective-permute-start(f32[8,2,8,128]{3,2,1,0:T(8,128)S(1)} %get-tuple-element.114), channel_id=1, source_target_pairs={{0,1},{1,2},{2,3},{3,4},{4,5},{5,6},{6,7},{7,0},{8,9},{9,10},{10,1... | collective-permute-start | bytes 196616 | tf_op jit(solution)/shard_map/ppermute | solution.py:1117
  60.4 3.9 %collective-permute-start.15 = (f32[8,2,8,128]{3,2,1,0:T(8,128)S(1)}, f32[8,2,8,128]{3,2,1,0:T(8,128)S(1)}, u32[]{:S(2)}, u32[]{:S(2)}) collective-permute-start(f32[8,2,8,128]{3,2,1,0:T(8,128)S(1)} %get-tuple-element.115), channel_id=1, source_target_pairs={{1,0},{2,1},{3,2},{4,3},{5,4},{6,5},{7,6},{0,7},{9,8},{10,9},{11,1... | collective-permute-start | bytes 196616 | tf_op jit(solution)/shard_map/ppermute | solution.py:1117

commit v6 on v5

--- a/solution.py
+++ b/solution.py
@@ -753,7 +753,7 @@
             )
         return carry
 
-    lax.fori_loop(0, 8, step, 0)
+    lax.fori_loop(0, 8, step, 0, unroll=2)
 
 
 def store_halves(halves, layer, half, value):

time: 65.7 us -> 65.6 us (level)
  no operation moved by 1% of the time
where the time goes in v6:
time: 65.6 us; the launch traced here: 64.8 us
  Pallas kernels  22.3 us (34%)
  waiting for transfers between devices  22.2 us (34%)
  starting transfers between devices  16.4 us (25%)
  local copies, waits for them, and re-layouts  2.22 us (3%)
  between operations  0.89 us (1%)
  other arithmetic  0.79 us (1%)
    pallas_call x17, Pallas kernels, call(): pl.pallas_call(body, out_shape=tuple(outs), in_specs=[whole(pltpu.SMEM if...  17.3 us
    ppermute x4, starting transfers between devices, exchange_along_first(): lax.ppermute(first, axes, forward)  12.2 us
    ppermute x4, waiting for transfers between devices, exchange_along_first(): lax.ppermute(second, axes, backward)  8.53 us
    ppermute x4, waiting for transfers between devices, exchange(): lax.ppermute(to_low, axis, downward)  6.99 us
    ppermute x4, waiting for transfers between devices, exchange_along_first(): lax.ppermute(first, axes, forward)  6.31 us
    ppermute x4, starting transfers between devices, exchange(): lax.ppermute(to_high, axis, upward)  3.25 us
    unnamed x16, local copies, waits for them, and re-layouts  2.22 us
    pallas_call x1, Pallas kernels, pack_first(): pl.pallas_call(pack_body, out_shape=(layers(8, 5), layers(8, 5)), in_spec...  1.98 us
  transfers between devices with their start and end apart: 16, of which 12 were waited for; matrix products, arithmetic and copies ran while one was open for 1% of the time, Pallas kernels for 24%

profile of v6, /device:TPU:25, one launch (start us, length us, event | category | flops | bytes accessed | tf_op | source)
XLA Modules:
  0.0 64.8 jit_solution(17602094751534531949)
XLA Ops:
  0.6 2.0 %pack_first.1 = (f32[8,5,8,128]{3,2,1,0:T(8,128)}, f32[8,5,8,128]{3,2,1,0:T(8,128)}) custom-call(s32[8,32]{1,0:T(8,128)} %outflow.1, f32[8,32,8,128]{3,2,1,0:T(8,128)} %start.5, f32[8,32,8,128]{3,2,1,0:T(8,128)} %source.3, f32[3,1,4,128]{3,2,1,0:T(4,128)} %coefficients.2), custom_call_target="tpu_custom_call" | custom-call | tf_op jit(solution)/shard_map/pack_first/pallas_call | solution.py:350
  2.6 1.8 %collective-permute-start = (f32[8,5,8,128]{3,2,1,0:T(8,128)}, f32[8,5,8,128]{3,2,1,0:T(8,128)S(1)}, u32[]{:S(2)}, u32[]{:S(2)}) collective-permute-start(f32[8,5,8,128]{3,2,1,0:T(8,128)} %get-tuple-element.69), channel_id=1, source_target_pairs={{0,1},{1,2},{2,3},{3,4},{4,5},{5,6},{6,7},{7,0},{8,9},{9,10},{10,1... | collective-permute-start | bytes 491528 | tf_op jit(solution)/shard_map/ppermute | solution.py:1117
  7.4 2.0 %collective-permute-done.1.from_high.refs_3_ = f32[8,5,8,128]{3,2,1,0:T(8,128)S(1)} collective-permute-done((f32[8,5,8,128]{3,2,1,0:T(8,128)}, f32[8,5,8,128]{3,2,1,0:T(8,128)S(1)}, u32[]{:S(2)}, u32[]{:S(2)}) %collective-permute-start.1) | collective-permute-done | bytes 163872 | tf_op jit(solution)/shard_map/ppermute | solution.py:1117
  9.6 4.0 %collective-permute-start.2 = (f32[2,31,8,128]{3,2,1,0:T(8,128)S(1)}, f32[2,31,8,128]{3,2,1,0:T(8,128)S(1)}, u32[]{:S(2)}, u32[]{:S(2)}) collective-permute-start(f32[2,31,8,128]{3,2,1,0:T(8,128)S(1)} %get-tuple-element.85), channel_id=1, source_target_pairs={{0,8},{8,16},{16,24},{24,32},{32,40},{40,48},{48,56},{56,64},{64,7... | collective-permute-start | bytes 761864 | tf_op jit(solution)/shard_map/ppermute | solution.py:1132
  15.8 2.2 %inner_forward.2 = (f32[10,2,128,256]{3,2,1,0:T(8,128)S(1)}, f32[4,2,128,256]{3,2,1,0:T(8,128)S(1)}) custom-call(f32[6,31,8,128]{3,2,1,0:T(8,128)S(1)} %first_inner.1.inner, bf16[128,240]{1,0:T(8,128)(2,1)S(1)} %copy-done.3, f32[10,2,128,256]{3,2,1,0:T(8,128)S(1)} %get-tuple-element.83.reciprocals), custom_call_target="tpu_custom_call" | custom-call | flops 300000000 | bytes 7176192 | tf_op jit(solution)/shard_map/inner_forward/pallas_call | solution.py:286
  18.9 1.9 %collective-permute-done.3.second = f32[2,31,8,128]{3,2,1,0:T(8,128)S(1)} collective-permute-done((f32[2,31,8,128]{3,2,1,0:T(8,128)S(1)}, f32[2,31,8,128]{3,2,1,0:T(8,128)S(1)}, u32[]{:S(2)}, u32[]{:S(2)}) %collective-permute-start.3) | collective-permute-done | bytes 253984 | tf_op jit(solution)/shard_map/ppermute | solution.py:1132
  20.8 1.8 %edge_solve.2 = (f32[2,31,8,128]{3,2,1,0:T(8,128)S(1)}, f32[2,31,8,128]{3,2,1,0:T(8,128)S(1)}, f32[2,31,8,128]{3,2,1,0:T(8,128)S(1)}, f32[2,31,8,128]{3,2,1,0:T(8,128)S(1)}, f32[4,2,128,256]{3,2,1,0:T(8,128)S(1)}) custom-call(f32[6,2,128,256]{3,2,1,0:T(8,128)S(1)} %get-tuple-element.68.blocks, bf16[128,240]{1,0:T(8,128)(2,1)S(1)} %copy-done.3, ...), custom_call_target="tpu_custom_call" | custom-call | flops 1000000000 | bytes 6152192 | tf_op jit(solution)/shard_map/edge_solve/pallas_call | solution.py:286
  22.6 2.5 %collective-permute-start.4 = (f32[2,31,8,128]{3,2,1,0:T(8,128)S(1)}, f32[2,31,8,128]{3,2,1,0:T(8,128)S(1)}, u32[]{:S(2)}, u32[]{:S(2)}) collective-permute-start(f32[2,31,8,128]{3,2,1,0:T(8,128)S(1)} %get-tuple-element.91), channel_id=1, source_target_pairs={{0,8},{8,16},{16,24},{24,32},{32,40},{40,48},{48,56},{56,64},{64,7... | collective-permute-start | bytes 761864 | tf_op jit(solution)/shard_map/ppermute | solution.py:1132
  25.1 2.7 %inner_backward.2.inner = f32[6,31,8,128]{3,2,1,0:T(8,128)S(1)} custom-call(f32[4,2,128,256]{3,2,1,0:T(8,128)S(1)} %get-tuple-element.88.spectral, f32[10,2,128,256]{3,2,1,0:T(8,128)S(1)} %get-tuple-element.89.partial, f32[10,2,128,256]{3,2,1,0:T(8,128)S(1)} %get-tuple-element.83.reciprocals, bf16[320,256]{1,0:T(8,128)(2,1)S(1)} %copy-done.2), custom_call_target="tpu_custom_call" | custom-call | flops 300000000 | bytes 7380992 | tf_op jit(solution)/shard_map/inner_backward/pallas_call | solution.py:286
  27.9 1.4 %collective-permute-start.8 = (f32[4,5,8,128]{3,2,1,0:T(8,128)S(1)}, f32[4,5,8,128]{3,2,1,0:T(8,128)S(1)}, u32[]{:S(2)}, u32[]{:S(2)}) collective-permute-start(f32[4,5,8,128]{3,2,1,0:T(8,128)S(1)} %get-tuple-element.97), channel_id=1, source_target_pairs={{0,1},{1,2},{2,3},{3,4},{4,5},{5,6},{6,7},{7,0},{8,9},{9,10},{10,1... | collective-permute-start | bytes 245768 | tf_op jit(solution)/shard_map/ppermute | solution.py:1117
  29.3 1.3 %collective-permute-done.4.first = f32[2,31,8,128]{3,2,1,0:T(8,128)S(1)} collective-permute-done((f32[2,31,8,128]{3,2,1,0:T(8,128)S(1)}, f32[2,31,8,128]{3,2,1,0:T(8,128)S(1)}, u32[]{:S(2)}, u32[]{:S(2)}) %collective-permute-start.4) | collective-permute-done | bytes 253984 | tf_op jit(solution)/shard_map/ppermute | solution.py:1132
  30.6 2.0 %collective-permute-done.5.second = f32[2,31,8,128]{3,2,1,0:T(8,128)S(1)} collective-permute-done((f32[2,31,8,128]{3,2,1,0:T(8,128)S(1)}, f32[2,31,8,128]{3,2,1,0:T(8,128)S(1)}, u32[]{:S(2)}, u32[]{:S(2)}) %collective-permute-start.5) | collective-permute-done | bytes 253984 | tf_op jit(solution)/shard_map/ppermute | solution.py:1132
  34.3 2.7 %collective-permute-done.7.high_edges = f32[4,5,8,128]{3,2,1,0:T(8,128)S(1)} collective-permute-done((f32[4,5,8,128]{3,2,1,0:T(8,128)S(1)}, f32[4,5,8,128]{3,2,1,0:T(8,128)S(1)}, u32[]{:S(2)}, u32[]{:S(2)}) %collective-permute-start.7) | collective-permute-done | bytes 81952 | tf_op jit(solution)/shard_map/ppermute | solution.py:1117
  37.4 3.7 %collective-permute-start.10 = (f32[2,31,8,128]{3,2,1,0:T(8,128)S(1)}, f32[2,31,8,128]{3,2,1,0:T(8,128)S(1)}, u32[]{:S(2)}, u32[]{:S(2)}) collective-permute-start(f32[2,31,8,128]{3,2,1,0:T(8,128)S(1)} %get-tuple-element.104), channel_id=1, source_target_pairs={{0,8},{8,16},{16,24},{24,32},{32,40},{40,48},{48,56},{56,64},{64,7... | collective-permute-start | bytes 761864 | tf_op jit(solution)/shard_map/ppermute | solution.py:1132
  41.6 2.2 %inner_forward.3 = (f32[10,2,128,256]{3,2,1,0:T(8,128)S(1)}, f32[4,2,128,256]{3,2,1,0:T(8,128)S(1)}) custom-call(f32[6,31,8,128]{3,2,1,0:T(8,128)S(1)} %second_inner.1.inner, bf16[128,240]{1,0:T(8,128)(2,1)S(1)} %copy-done.3, f32[10,2,128,256]{3,2,1,0:T(8,128)S(1)} %get-tuple-element.83.reciprocals), custom_call_target="tpu_custom_call" | custom-call | flops 300000000 | bytes 7176192 | tf_op jit(solution)/shard_map/inner_forward/pallas_call | solution.py:286
  43.8 2.2 %collective-permute-done.10.first = f32[2,31,8,128]{3,2,1,0:T(8,128)S(1)} collective-permute-done((f32[2,31,8,128]{3,2,1,0:T(8,128)S(1)}, f32[2,31,8,128]{3,2,1,0:T(8,128)S(1)}, u32[]{:S(2)}, u32[]{:S(2)}) %collective-permute-start.10) | collective-permute-done | bytes 253984 | tf_op jit(solution)/shard_map/ppermute | solution.py:1132
  46.0 2.4 %collective-permute-done.11.second = f32[2,31,8,128]{3,2,1,0:T(8,128)S(1)} collective-permute-done((f32[2,31,8,128]{3,2,1,0:T(8,128)S(1)}, f32[2,31,8,128]{3,2,1,0:T(8,128)S(1)}, u32[]{:S(2)}, u32[]{:S(2)}) %collective-permute-start.11) | collective-permute-done | bytes 253984 | tf_op jit(solution)/shard_map/ppermute | solution.py:1132
  48.4 1.8 %edge_solve.3 = (f32[2,31,8,128]{3,2,1,0:T(8,128)S(1)}, f32[2,31,8,128]{3,2,1,0:T(8,128)S(1)}, f32[2,31,8,128]{3,2,1,0:T(8,128)S(1)}, f32[2,31,8,128]{3,2,1,0:T(8,128)S(1)}, f32[4,2,128,256]{3,2,1,0:T(8,128)S(1)}) custom-call(f32[6,2,128,256]{3,2,1,0:T(8,128)S(1)} %get-tuple-element.68.blocks, bf16[128,240]{1,0:T(8,128)(2,1)S(1)} %copy-done.3, ...), custom_call_target="tpu_custom_call" | custom-call | flops 1000000000 | bytes 6152192 | tf_op jit(solution)/shard_map/edge_solve/pallas_call | solution.py:286
  50.2 2.0 %collective-permute-start.12 = (f32[2,31,8,128]{3,2,1,0:T(8,128)S(1)}, f32[2,31,8,128]{3,2,1,0:T(8,128)S(1)}, u32[]{:S(2)}, u32[]{:S(2)}) collective-permute-start(f32[2,31,8,128]{3,2,1,0:T(8,128)S(1)} %get-tuple-element.111), channel_id=1, source_target_pairs={{0,8},{8,16},{16,24},{24,32},{32,40},{40,48},{48,56},{56,64},{64,7... | collective-permute-start | bytes 761864 | tf_op jit(solution)/shard_map/ppermute | solution.py:1132
  52.2 1.3 %residual.1 = f32[8,32,8,128]{3,2,1,0:T(8,128)} custom-call(f32[2,31,8,128]{3,2,1,0:T(8,128)S(1)} %get-tuple-element.101.low, f32[6,31,8,128]{3,2,1,0:T(8,128)S(1)} %second_inner.1.inner, f32[2,31,8,128]{3,2,1,0:T(8,128)S(1)} %get-tuple-element.102.high, f32[2,31,8,128]{3,2,1,0:T(8,128)S(1)} %collective-permute-done.10.first, ...), custom_call_target="tpu_custom_call" | custom-call | flops 10000000 | bytes 4194304 | tf_op jit(solution)/shard_map/residual/pallas_call | solution.py:875
  53.5 2.7 %inner_backward.3.inner = f32[6,31,8,128]{3,2,1,0:T(8,128)S(1)} custom-call(f32[4,2,128,256]{3,2,1,0:T(8,128)S(1)} %get-tuple-element.107.spectral, f32[10,2,128,256]{3,2,1,0:T(8,128)S(1)} %get-tuple-element.108.partial, f32[10,2,128,256]{3,2,1,0:T(8,128)S(1)} %get-tuple-element.83.reciprocals, bf16[320,256]{1,0:T(8,128)(2,1)S(1)} %copy-done.2), custom_call_target="tpu_custom_call" | custom-call | flops 300000000 | bytes 7380992 | tf_op jit(solution)/shard_map/inner_backward/pallas_call | solution.py:286
  56.2 1.9 %collective-permute-done.12.first = f32[2,31,8,128]{3,2,1,0:T(8,128)S(1)} collective-permute-done((f32[2,31,8,128]{3,2,1,0:T(8,128)S(1)}, f32[2,31,8,128]{3,2,1,0:T(8,128)S(1)}, u32[]{:S(2)}, u32[]{:S(2)}) %collective-permute-start.12) | collective-permute-done | bytes 253984 | tf_op jit(solution)/shard_map/ppermute | solution.py:1132
  58.0 2.2 %collective-permute-done.13.second = f32[2,31,8,128]{3,2,1,0:T(8,128)S(1)} collective-permute-done((f32[2,31,8,128]{3,2,1,0:T(8,128)S(1)}, f32[2,31,8,128]{3,2,1,0:T(8,128)S(1)}, u32[]{:S(2)}, u32[]{:S(2)}) %collective-permute-start.13) | collective-permute-done | bytes 253984 | tf_op jit(solution)/shard_map/ppermute | solution.py:1132
  61.9 2.3 %collective-permute-done.15.high_news = f32[8,2,8,128]{3,2,1,0:T(8,128)S(1)} collective-permute-done((f32[8,2,8,128]{3,2,1,0:T(8,128)S(1)}, f32[8,2,8,128]{3,2,1,0:T(8,128)S(1)}, u32[]{:S(2)}, u32[]{:S(2)}) %collective-permute-start.15) | collective-permute-done | bytes 65568 | tf_op jit(solution)/shard_map/ppermute | solution.py:1117
  (48 shorter events, 11.0 us)
Async XLA Ops:
  0.6 4.5 %copy-start.1 = (f32[8,32,8,128]{3,2,1,0:T(8,128)S(1)}, f32[8,32,8,128]{3,2,1,0:T(8,128)}, u32[]{:S(2)}) copy-start(f32[8,32,8,128]{3,2,1,0:T(8,128)} %source.3) | copy-start | bytes 3145732
  0.6 4.5 %copy-start = (f32[8,32,8,128]{3,2,1,0:T(8,128)S(1)}, f32[8,32,8,128]{3,2,1,0:T(8,128)}, u32[]{:S(2)}) copy-start(f32[8,32,8,128]{3,2,1,0:T(8,128)} %start.5) | copy-start | bytes 3145732
  2.6 4.7 %collective-permute-start = (f32[8,5,8,128]{3,2,1,0:T(8,128)}, f32[8,5,8,128]{3,2,1,0:T(8,128)S(1)}, u32[]{:S(2)}, u32[]{:S(2)}) collective-permute-start(f32[8,5,8,128]{3,2,1,0:T(8,128)} %get-tuple-element.69), channel_id=1, source_target_pairs={{0,1},{1,2},{2,3},{3,4},{4,5},{5,6},{6,7},{7,0},{8,9},{9,10},{10,1... | collective-permute-start | bytes 491528 | tf_op jit(solution)/shard_map/ppermute | solution.py:1117
  4.4 5.0 %collective-permute-start.1 = (f32[8,5,8,128]{3,2,1,0:T(8,128)}, f32[8,5,8,128]{3,2,1,0:T(8,128)S(1)}, u32[]{:S(2)}, u32[]{:S(2)}) collective-permute-start(f32[8,5,8,128]{3,2,1,0:T(8,128)} %get-tuple-element.70), channel_id=1, source_target_pairs={{1,0},{2,1},{3,2},{4,3},{5,4},{6,5},{7,6},{0,7},{9,8},{10,9},{11,1... | collective-permute-start | bytes 491528 | tf_op jit(solution)/shard_map/ppermute | solution.py:1117
  5.1 0.9 %copy-start.4 = (bf16[144,192]{1,0:T(8,128)(2,1)S(1)}, bf16[144,192]{1,0:T(8,128)(2,1)}, u32[]{:S(2)}) copy-start(bf16[144,192]{1,0:T(8,128)(2,1)} %constant.16.clone.table) | copy-start | bytes 165892
  6.0 0.7 %copy-start.5 = (f32[3,1,4,128]{3,2,1,0:T(4,128)S(1)}, f32[3,1,4,128]{3,2,1,0:T(4,128)}, u32[]{:S(2)}) copy-start(f32[3,1,4,128]{3,2,1,0:T(4,128)} %coefficients.2) | copy-start | bytes 18436
  6.7 6.9 %copy-start.6 = (f32[128,128]{1,0:T(8,128)S(1)}, f32[128,128]{1,0:T(8,128)}, u32[]{:S(2)}) copy-start(f32[128,128]{1,0:T(8,128)} %constant.18.clone.third_values) | copy-start | bytes 196612
  6.7 6.9 %copy-start.7 = (f32[128,128]{1,0:T(8,128)S(1)}, f32[128,128]{1,0:T(8,128)}, u32[]{:S(2)}) copy-start(f32[128,128]{1,0:T(8,128)} %constant.17.clone.second_values) | copy-start | bytes 196612
  9.6 9.3 %collective-permute-start.2 = (f32[2,31,8,128]{3,2,1,0:T(8,128)S(1)}, f32[2,31,8,128]{3,2,1,0:T(8,128)S(1)}, u32[]{:S(2)}, u32[]{:S(2)}) collective-permute-start(f32[2,31,8,128]{3,2,1,0:T(8,128)S(1)} %get-tuple-element.85), channel_id=1, source_target_pairs={{0,8},{8,16},{16,24},{24,32},{32,40},{40,48},{48,56},{56,64},{64,7... | collective-permute-start | bytes 761864 | tf_op jit(solution)/shard_map/ppermute | solution.py:1132
  13.6 7.2 %collective-permute-start.3 = (f32[2,31,8,128]{3,2,1,0:T(8,128)S(1)}, f32[2,31,8,128]{3,2,1,0:T(8,128)S(1)}, u32[]{:S(2)}, u32[]{:S(2)}) collective-permute-start(f32[2,31,8,128]{3,2,1,0:T(8,128)S(1)} %get-tuple-element.86), channel_id=1, source_target_pairs={{8,0},{16,8},{24,16},{32,24},{40,32},{48,40},{56,48},{64,56},{72,6... | collective-permute-start | bytes 761864 | tf_op jit(solution)/shard_map/ppermute | solution.py:1132
  14.9 0.8 %copy-start.3 = (bf16[128,240]{1,0:T(8,128)(2,1)S(1)}, bf16[128,240]{1,0:T(8,128)(2,1)}, u32[]{:S(2)}) copy-start(bf16[128,240]{1,0:T(8,128)(2,1)} %constant.19.clone.forward) | copy-start | bytes 184324
  15.2 5.7 %copy-start.2 = (bf16[320,256]{1,0:T(8,128)(2,1)S(1)}, bf16[320,256]{1,0:T(8,128)(2,1)}, u32[]{:S(2)}) copy-start(bf16[320,256]{1,0:T(8,128)(2,1)} %constant.20.clone.backward) | copy-start | bytes 491524
  22.6 8.0 %collective-permute-start.4 = (f32[2,31,8,128]{3,2,1,0:T(8,128)S(1)}, f32[2,31,8,128]{3,2,1,0:T(8,128)S(1)}, u32[]{:S(2)}, u32[]{:S(2)}) collective-permute-start(f32[2,31,8,128]{3,2,1,0:T(8,128)S(1)} %get-tuple-element.91), channel_id=1, source_target_pairs={{0,8},{8,16},{16,24},{24,32},{32,40},{40,48},{48,56},{56,64},{64,7... | collective-permute-start | bytes 761864 | tf_op jit(solution)/shard_map/ppermute | solution.py:1132
  25.1 7.6 %collective-permute-start.5 = (f32[2,31,8,128]{3,2,1,0:T(8,128)S(1)}, f32[2,31,8,128]{3,2,1,0:T(8,128)S(1)}, u32[]{:S(2)}, u32[]{:S(2)}) collective-permute-start(f32[2,31,8,128]{3,2,1,0:T(8,128)S(1)} %get-tuple-element.92), channel_id=1, source_target_pairs={{8,0},{16,8},{24,16},{32,24},{40,32},{48,40},{56,48},{64,56},{72,6... | collective-permute-start | bytes 761864 | tf_op jit(solution)/shard_map/ppermute | solution.py:1132
  27.9 6.1 %collective-permute-start.8 = (f32[4,5,8,128]{3,2,1,0:T(8,128)S(1)}, f32[4,5,8,128]{3,2,1,0:T(8,128)S(1)}, u32[]{:S(2)}, u32[]{:S(2)}) collective-permute-start(f32[4,5,8,128]{3,2,1,0:T(8,128)S(1)} %get-tuple-element.97), channel_id=1, source_target_pairs={{0,1},{1,2},{2,3},{3,4},{4,5},{5,6},{6,7},{7,0},{8,9},{9,10},{10,1... | collective-permute-start | bytes 245768 | tf_op jit(solution)/shard_map/ppermute | solution.py:1117
  29.3 4.7 %collective-permute-start.9 = (f32[4,5,8,128]{3,2,1,0:T(8,128)S(1)}, f32[4,5,8,128]{3,2,1,0:T(8,128)S(1)}, u32[]{:S(2)}, u32[]{:S(2)}) collective-permute-start(f32[4,5,8,128]{3,2,1,0:T(8,128)S(1)} %get-tuple-element.98), channel_id=1, source_target_pairs={{1,0},{2,1},{3,2},{4,3},{5,4},{6,5},{7,6},{0,7},{9,8},{10,9},{11,1... | collective-permute-start | bytes 245768 | tf_op jit(solution)/shard_map/ppermute | solution.py:1117
  32.8 1.5 %collective-permute-start.6 = (f32[4,5,8,128]{3,2,1,0:T(8,128)S(1)}, f32[4,5,8,128]{3,2,1,0:T(8,128)S(1)}, u32[]{:S(2)}, u32[]{:S(2)}) collective-permute-start(f32[4,5,8,128]{3,2,1,0:T(8,128)S(1)} %get-tuple-element.95), channel_id=1, source_target_pairs={{0,1},{1,2},{2,3},{3,4},{4,5},{5,6},{6,7},{7,0},{8,9},{9,10},{10,1... | collective-permute-start | bytes 245768 | tf_op jit(solution)/shard_map/ppermute | solution.py:1117
  32.8 4.2 %collective-permute-start.7 = (f32[4,5,8,128]{3,2,1,0:T(8,128)S(1)}, f32[4,5,8,128]{3,2,1,0:T(8,128)S(1)}, u32[]{:S(2)}, u32[]{:S(2)}) collective-permute-start(f32[4,5,8,128]{3,2,1,0:T(8,128)S(1)} %get-tuple-element.96), channel_id=1, source_target_pairs={{1,0},{2,1},{3,2},{4,3},{5,4},{6,5},{7,6},{0,7},{9,8},{10,9},{11,1... | collective-permute-start | bytes 245768 | tf_op jit(solution)/shard_map/ppermute | solution.py:1117
  37.4 8.5 %collective-permute-start.10 = (f32[2,31,8,128]{3,2,1,0:T(8,128)S(1)}, f32[2,31,8,128]{3,2,1,0:T(8,128)S(1)}, u32[]{:S(2)}, u32[]{:S(2)}) collective-permute-start(f32[2,31,8,128]{3,2,1,0:T(8,128)S(1)} %get-tuple-element.104), channel_id=1, source_target_pairs={{0,8},{8,16},{16,24},{24,32},{32,40},{40,48},{48,56},{56,64},{64,7... | collective-permute-start | bytes 761864 | tf_op jit(solution)/shard_map/ppermute | solution.py:1132
  41.1 7.2 %collective-permute-start.11 = (f32[2,31,8,128]{3,2,1,0:T(8,128)S(1)}, f32[2,31,8,128]{3,2,1,0:T(8,128)S(1)}, u32[]{:S(2)}, u32[]{:S(2)}) collective-permute-start(f32[2,31,8,128]{3,2,1,0:T(8,128)S(1)} %get-tuple-element.105), channel_id=1, source_target_pairs={{8,0},{16,8},{24,16},{32,24},{40,32},{48,40},{56,48},{64,56},{72,6... | collective-permute-start | bytes 761864 | tf_op jit(solution)/shard_map/ppermute | solution.py:1132
  50.2 7.9 %collective-permute-start.12 = (f32[2,31,8,128]{3,2,1,0:T(8,128)S(1)}, f32[2,31,8,128]{3,2,1,0:T(8,128)S(1)}, u32[]{:S(2)}, u32[]{:S(2)}) collective-permute-start(f32[2,31,8,128]{3,2,1,0:T(8,128)S(1)} %get-tuple-element.111), channel_id=1, source_target_pairs={{0,8},{8,16},{16,24},{24,32},{32,40},{40,48},{48,56},{56,64},{64,7... | collective-permute-start | bytes 761864 | tf_op jit(solution)/shard_map/ppermute | solution.py:1132
  52.2 8.1 %collective-permute-start.13 = (f32[2,31,8,128]{3,2,1,0:T(8,128)S(1)}, f32[2,31,8,128]{3,2,1,0:T(8,128)S(1)}, u32[]{:S(2)}, u32[]{:S(2)}) collective-permute-start(f32[2,31,8,128]{3,2,1,0:T(8,128)S(1)} %get-tuple-element.112), channel_id=1, source_target_pairs={{8,0},{16,8},{24,16},{32,24},{40,32},{48,40},{56,48},{64,56},{72,6... | collective-permute-start | bytes 761864 | tf_op jit(solution)/shard_map/ppermute | solution.py:1132
  60.3 1.6 %collective-permute-start.14 = (f32[8,2,8,128]{3,2,1,0:T(8,128)S(1)}, f32[8,2,8,128]{3,2,1,0:T(8,128)S(1)}, u32[]{:S(2)}, u32[]{:S(2)}) collective-permute-start(f32[8,2,8,128]{3,2,1,0:T(8,128)S(1)} %get-tuple-element.114), channel_id=1, source_target_pairs={{0,1},{1,2},{2,3},{3,4},{4,5},{5,6},{6,7},{7,0},{8,9},{9,10},{10,1... | collective-permute-start | bytes 196616 | tf_op jit(solution)/shard_map/ppermute | solution.py:1117
  60.3 3.9 %collective-permute-start.15 = (f32[8,2,8,128]{3,2,1,0:T(8,128)S(1)}, f32[8,2,8,128]{3,2,1,0:T(8,128)S(1)}, u32[]{:S(2)}, u32[]{:S(2)}) collective-permute-start(f32[8,2,8,128]{3,2,1,0:T(8,128)S(1)} %get-tuple-element.115), channel_id=1, source_target_pairs={{1,0},{2,1},{3,2},{4,3},{5,4},{6,5},{7,6},{0,7},{9,8},{10,9},{11,1... | collective-permute-start | bytes 196616 | tf_op jit(solution)/shard_map/ppermute | solution.py:1117
